TPU v7x, 256 devices: a whole 4x4x8 slice. The times are simulated.
256 devices in a mesh: tm: 32 (over z, x_hi, core), gz: 8 (over x_lo, y).
Axes of the slice: x: 4 (x_hi: 2, x_lo: 2; x = x_hi * 2 + x_lo), y: 4, z: 8, core: 2. Of those that a mesh axis runs over, the one named last changes fastest.
Arguments:
- starts: float32 [32, 32, 32, 128], P('tm', 'gz'), may hold values from -6 to 6
- cell_rates: float32 [32, 32, 128], P('gz'), may hold values from 0.3 to 1
Outputs:
- slab_ends: float32 [32, 32, 32, 128], P('tm', 'gz')
- next_starts: float32 [32, 32, 32, 128], P('tm', 'gz')
All inputs are finite; a program needn't handle non-finite values.
Results may differ from a plain program's by a relative error of at most 0.0001.
Values sent between devices are 32-bit elements; how exact they have to be, the bound alone decides.
No kernel may reach another device: no remote copies, remote signals or barrier semaphores. Data moves between devices by JAX's collectives and lax.ppermute only.
A program may use at most 64 MiB of HBM per device.

v0:
```python
import jax
import jax.numpy as jnp
from jax import lax
from jax.sharding import PartitionSpec as P

FINE = 4


fine_along_z = (0.1, 0.12)
fine_along_x = (0.15, 0.12)
fine_along_y = (0.2, 0.12)
coarse_along_z = (0.2, 0.25)
coarse_along_x = (0.3, 0.25)
coarse_along_y = (0.4, 0.25)


def padded_2(cells, sides, width):
    for axis, dim in sides:
        count = lax.axis_size(axis)
        head = lax.slice_in_dim(cells, 0, width, axis=dim)
        tail = lax.slice_in_dim(cells, cells.shape[dim] - width, cells.shape[dim], axis=dim)
        cells = jnp.concatenate(
            [
                lax.ppermute(tail, axis, [(i, (i + 1) % count) for i in range(count)]),
                cells,
                lax.ppermute(head, axis, [((i + 1) % count, i) for i in range(count)]),
            ],
            axis=dim,
        )
    return cells


def sent_to_all(shard, axis):
    copies = jnp.broadcast_to(shard, (lax.axis_size(axis), *shard.shape))
    return lax.all_to_all(copies, axis, split_axis=0, concat_axis=0, tiled=True)


def in_order(tiles, dim):
    lengths = list(tiles.shape[1:])
    lengths[dim] *= tiles.shape[0]
    return jnp.moveaxis(tiles, 0, dim).reshape(lengths)


def collect(shard, axis, dim):
    tiles = sent_to_all(shard, axis)
    return in_order(tiles, dim)


def sent_together(arrays, axis, dim, along):
    ends, at = ([], 0)
    for a in arrays[:-1]:
        at += a.shape[along]
        ends.append(at)
    both = jnp.concatenate(arrays, axis=along)
    return tuple(jnp.split(collect(both, axis, dim), ends, axis=along))


def shifted(shard, axis, by):
    size = lax.axis_size(axis)
    return lax.ppermute(shard, axis, [(i, (i + by) % size) for i in range(size)])


def line_filter(behind, middle, beyond, courant, diffuse):
    return (
        (diffuse + 0.5 * courant) * behind
        + (1.0 - 2.0 * diffuse) * middle
        + (diffuse - 0.5 * courant) * beyond
    )


def plane_filter(values, along_x, along_y):
    mixed = line_filter(
        jnp.roll(values, 1, 2), values, jnp.roll(values, -1, 2), along_y[0], along_y[1]
    )
    return line_filter(jnp.roll(mixed, 1, 1), mixed, jnp.roll(mixed, -1, 1), along_x[0], along_x[1])


def depth_filter(padded, along_z):
    return line_filter(padded[:-2], padded[1:-1], padded[2:], along_z[0], along_z[1])


def restrict(values):
    extent_z, extent_x, extent_y = values.shape
    blocks = values.reshape(extent_z // 2, 2, extent_x // 2, 2, extent_y // 2, 2)
    return jnp.mean(blocks, axis=(1, 3, 5))


def prolong(values):
    extent_z, extent_x, extent_y = values.shape
    spread = jnp.broadcast_to(
        values[:, None, :, None, :, None], (extent_z, 2, extent_x, 2, extent_y, 2)
    )
    return spread.reshape(extent_z * 2, extent_x * 2, extent_y * 2)


def coarse_step(coarse, coarse_rates):
    padded = padded_2(coarse, (("gz", 0),), 1)
    mixed = depth_filter(plane_filter(padded, coarse_along_x, coarse_along_y), coarse_along_z)
    return coarse + coarse_rates * (mixed - coarse)


def per_device(starts, cell_rates):
    start = starts[0]
    coarse_rates = restrict(cell_rates)
    stacked = jnp.stack([start, cell_rates])
    widened = padded_2(stacked, (("gz", 1),), FINE)
    current = widened[0]
    weights = widened[1]
    for sweep_index in range(FINE):
        mixed = depth_filter(plane_filter(current, fine_along_x, fine_along_y), fine_along_z)
        inner = current[1:-1]
        weights = weights[1:-1]
        current = inner + weights * (mixed - inner)
    correction = current - prolong(coarse_step(restrict(start), coarse_rates))
    my_index = lax.axis_index("tm")
    links = lax.axis_size("tm") - 1
    all_starts, all_terms = sent_together(
        (restrict(start)[None], restrict(correction)[None]), "tm", 0, 1
    )

    def advance(turn_index, coarse):
        term = lax.dynamic_index_in_dim(all_terms, turn_index, 0, keepdims=False)
        finish = coarse_step(coarse, coarse_rates) + term
        return jnp.where(turn_index < my_index, finish, coarse)

    coarse = lax.fori_loop(0, links, advance, all_starts[0])
    slab_end = prolong(coarse_step(coarse, coarse_rates)) + correction
    next_start = shifted(slab_end, "tm", 1)
    return (slab_end[None], next_start[None])


def solution(mesh):
    return jax.shard_map(
        per_device,
        mesh=mesh,
        in_specs=(P("tm", "gz", None, None), P("gz", None, None)),
        out_specs=(P("tm", "gz", None, None), P("tm", "gz", None, None)),
        check_vma=False,
    )
```

profile of v0, /device:TPU:1, one launch (start us, length us, event | category | flops | bytes accessed | tf_op | source)
XLA Modules:
  0.0 290.8 jit_solution(4179183880385338651)
XLA Ops:
  0.6 6.3 %reshape_squeeze.4 = f32[2,2,16,2,64,2]{5,4,3,2,1,0:T(8,128)} reshape(f32[1,4,32,128]{3,2,1,0:T(8,128)} %param.4) | data formatting | bytes 131072 | tf_op jit(solution)/shard_map/reshape;squeeze | solution.py:84
  7.0 2.5 reduce_sum.27
  9.5 4.6 %collective-permute-start.5 = (f32[1,16,64]{2,1,0:T(8,128)S(1)}, f32[1,16,64]{2,1,0:T(8,128)S(1)}, u32[]{:S(2)}, u32[]{:S(2)}) collective-permute-start(f32[1,16,64]{2,1,0:T(8,128)S(1)} %get-tuple-element.171), channel_id=1, source_target_pairs={{1,0},{2,1},{3,2},{4,3},{5,4},{6,5},{7,6},{0,7},{9,8},{10,9},{11,1... | collective-permute-start | bytes 12296 | tf_op jit(solution)/shard_map/ppermute | solution.py:26
  14.1 3.6 %collective-permute-start.3 = (f32[2,4,32,128]{3,2,1,0:T(8,128)S(1)}, f32[2,4,32,128]{3,2,1,0:T(8,128)S(1)}, u32[]{:S(2)}, u32[]{:S(2)}) collective-permute-start(f32[2,4,32,128]{3,2,1,0:T(8,128)S(1)} %pad_maximum_fusion.1), channel_id=1, source_target_pairs={{1,0},{2,1},{3,2},{4,3},{5,4},{6,5},{7,6},{0,7},{9,8},{10,9},{11,1... | collective-permute-start | bytes 393224 | tf_op jit(solution)/shard_map/ppermute | solution.py:26
  17.8 5.5 %reshape.46 = f32[2,2,16,2,64,2]{5,4,3,2,1,0:T(8,128)} reshape(f32[4,32,128]{2,1,0:T(8,128)S(1)} %copy-done) | data formatting | bytes 131072 | tf_op jit(solution)/shard_map/reshape | solution.py:84
  23.3 2.5 reduce_sum.32
  26.2 2.6 broadcast_in_dim.10
  28.8 4.0 %reshape.47 = f32[4,32,128]{2,1,0:T(8,128)S(1)} reshape(f32[2,2,16,2,64,2]{5,4,3,2,1,0:T(8,128)} %broadcast_in_dim.10) | data formatting | bytes 131072 | tf_op jit(solution)/shard_map/reshape | solution.py:93
  35.0 5.5 %reshape.48 = f32[2,2,16,2,64,2]{5,4,3,2,1,0:T(8,128)} reshape(f32[4,32,128]{2,1,0:T(8,128)S(1)} %fusion.46) | data formatting | bytes 131072 | tf_op jit(solution)/shard_map/reshape | solution.py:84
  40.5 2.5 reduce_sum.33
  43.2 1.4 reshape.51
  44.6 12.3 %all-to-all-start = ((f32[32,1,4096]{2,1,0:T(1,128)}), f32[32,1,4096]{2,1,0:T(1,128)S(1)}, u32[]{:S(2)}, u32[]{:S(2)}) async-start(f32[32,1,4096]{2,1,0:T(1,128)} %reshape.51), calls=%async_computation | async-start | bytes 1048576 | tf_op jit(solution)/shard_map/all_to_all | solution.py:35
  57.0 17.0 %all-to-all-done = f32[32,1,4096]{2,1,0:T(1,128)S(1)} async-done(((f32[32,1,4096]{2,1,0:T(1,128)}), f32[32,1,4096]{2,1,0:T(1,128)S(1)}, u32[]{:S(2)}, u32[]{:S(2)}) %all-to-all-start) | async-done | bytes 524320 | tf_op jit(solution)/shard_map/all_to_all | solution.py:35
  74.5 1.9 reduce
  76.9 159.6 %while.13 = (s32[]{:T(128)}, f32[2,16,64]{2,1,0:T(8,128)S(1)}, s32[]{:T(128)}, f32[2,16,64]{2,1,0:T(8,128)S(1)}, f32[32,2,16,64]{3,2,1,0:T(8,128)S(1)}, /*index=5*/s32[]{:T(128)}) while((s32[]{:T(128)}, f32[2,16,64]{2,1,0:T(8,128)S(1)}, s32[]{:T(128)}, f32[2,16,64]{2,1,0:T(8,128)S(1)}, f32[32,2,16,64]{3,2,1,0:T(8,128)S(1)}, ...), condition=%wide.region_4.5_spmd, body=%wide.region_3.4_spmd.sunk | while | flops 77827 | bytes 430251 | solution.py:126
  77.0 3.6 %collective-permute-start.1 = (f32[1,16,64]{2,1,0:T(8,128)S(1)}, f32[1,16,64]{2,1,0:T(8,128)S(1)}, u32[]{:S(2)}, u32[]{:S(2)}) collective-permute-start(f32[1,16,64]{2,1,0:T(8,128)S(1)} %get-tuple-element.214), channel_id=1, source_target_pairs={{1,0},{2,1},{3,2},{4,3},{5,4},{6,5},{7,6},{0,7},{9,8},{10,9},{11,1... | collective-permute-start | bytes 12296 | tf_op jit(solution)/shard_map/while/body/eval_jaxpr/ppermute | solution.py:26
  80.5 1.0 collective-permute-done
  82.5 3.2 %collective-permute-start.1 = (f32[1,16,64]{2,1,0:T(8,128)S(1)}, f32[1,16,64]{2,1,0:T(8,128)S(1)}, u32[]{:S(2)}, u32[]{:S(2)}) collective-permute-start(f32[1,16,64]{2,1,0:T(8,128)S(1)} %get-tuple-element.214), channel_id=1, source_target_pairs={{1,0},{2,1},{3,2},{4,3},{5,4},{6,5},{7,6},{0,7},{9,8},{10,9},{11,1... | collective-permute-start | bytes 12296 | tf_op jit(solution)/shard_map/while/body/eval_jaxpr/ppermute | solution.py:26
  87.7 3.2 %collective-permute-start.1 = (f32[1,16,64]{2,1,0:T(8,128)S(1)}, f32[1,16,64]{2,1,0:T(8,128)S(1)}, u32[]{:S(2)}, u32[]{:S(2)}) collective-permute-start(f32[1,16,64]{2,1,0:T(8,128)S(1)} %get-tuple-element.214), channel_id=1, source_target_pairs={{1,0},{2,1},{3,2},{4,3},{5,4},{6,5},{7,6},{0,7},{9,8},{10,9},{11,1... | collective-permute-start | bytes 12296 | tf_op jit(solution)/shard_map/while/body/eval_jaxpr/ppermute | solution.py:26
  92.8 3.2 %collective-permute-start.1 = (f32[1,16,64]{2,1,0:T(8,128)S(1)}, f32[1,16,64]{2,1,0:T(8,128)S(1)}, u32[]{:S(2)}, u32[]{:S(2)}) collective-permute-start(f32[1,16,64]{2,1,0:T(8,128)S(1)} %get-tuple-element.214), channel_id=1, source_target_pairs={{1,0},{2,1},{3,2},{4,3},{5,4},{6,5},{7,6},{0,7},{9,8},{10,9},{11,1... | collective-permute-start | bytes 12296 | tf_op jit(solution)/shard_map/while/body/eval_jaxpr/ppermute | solution.py:26
  98.0 3.2 %collective-permute-start.1 = (f32[1,16,64]{2,1,0:T(8,128)S(1)}, f32[1,16,64]{2,1,0:T(8,128)S(1)}, u32[]{:S(2)}, u32[]{:S(2)}) collective-permute-start(f32[1,16,64]{2,1,0:T(8,128)S(1)} %get-tuple-element.214), channel_id=1, source_target_pairs={{1,0},{2,1},{3,2},{4,3},{5,4},{6,5},{7,6},{0,7},{9,8},{10,9},{11,1... | collective-permute-start | bytes 12296 | tf_op jit(solution)/shard_map/while/body/eval_jaxpr/ppermute | solution.py:26
  101.1 1.3 collective-permute-done
  103.5 3.0 %collective-permute-start.1 = (f32[1,16,64]{2,1,0:T(8,128)S(1)}, f32[1,16,64]{2,1,0:T(8,128)S(1)}, u32[]{:S(2)}, u32[]{:S(2)}) collective-permute-start(f32[1,16,64]{2,1,0:T(8,128)S(1)} %get-tuple-element.214), channel_id=1, source_target_pairs={{1,0},{2,1},{3,2},{4,3},{5,4},{6,5},{7,6},{0,7},{9,8},{10,9},{11,1... | collective-permute-start | bytes 12296 | tf_op jit(solution)/shard_map/while/body/eval_jaxpr/ppermute | solution.py:26
  106.5 1.0 collective-permute-done
  108.6 3.0 %collective-permute-start.1 = (f32[1,16,64]{2,1,0:T(8,128)S(1)}, f32[1,16,64]{2,1,0:T(8,128)S(1)}, u32[]{:S(2)}, u32[]{:S(2)}) collective-permute-start(f32[1,16,64]{2,1,0:T(8,128)S(1)} %get-tuple-element.214), channel_id=1, source_target_pairs={{1,0},{2,1},{3,2},{4,3},{5,4},{6,5},{7,6},{0,7},{9,8},{10,9},{11,1... | collective-permute-start | bytes 12296 | tf_op jit(solution)/shard_map/while/body/eval_jaxpr/ppermute | solution.py:26
  113.9 2.9 collective-permute-start.1
  118.9 3.0 %collective-permute-start.1 = (f32[1,16,64]{2,1,0:T(8,128)S(1)}, f32[1,16,64]{2,1,0:T(8,128)S(1)}, u32[]{:S(2)}, u32[]{:S(2)}) collective-permute-start(f32[1,16,64]{2,1,0:T(8,128)S(1)} %get-tuple-element.214), channel_id=1, source_target_pairs={{1,0},{2,1},{3,2},{4,3},{5,4},{6,5},{7,6},{0,7},{9,8},{10,9},{11,1... | collective-permute-start | bytes 12296 | tf_op jit(solution)/shard_map/while/body/eval_jaxpr/ppermute | solution.py:26
  124.0 3.0 %collective-permute-start.1 = (f32[1,16,64]{2,1,0:T(8,128)S(1)}, f32[1,16,64]{2,1,0:T(8,128)S(1)}, u32[]{:S(2)}, u32[]{:S(2)}) collective-permute-start(f32[1,16,64]{2,1,0:T(8,128)S(1)} %get-tuple-element.214), channel_id=1, source_target_pairs={{1,0},{2,1},{3,2},{4,3},{5,4},{6,5},{7,6},{0,7},{9,8},{10,9},{11,1... | collective-permute-start | bytes 12296 | tf_op jit(solution)/shard_map/while/body/eval_jaxpr/ppermute | solution.py:26
  129.2 3.0 %collective-permute-start.1 = (f32[1,16,64]{2,1,0:T(8,128)S(1)}, f32[1,16,64]{2,1,0:T(8,128)S(1)}, u32[]{:S(2)}, u32[]{:S(2)}) collective-permute-start(f32[1,16,64]{2,1,0:T(8,128)S(1)} %get-tuple-element.214), channel_id=1, source_target_pairs={{1,0},{2,1},{3,2},{4,3},{5,4},{6,5},{7,6},{0,7},{9,8},{10,9},{11,1... | collective-permute-start | bytes 12296 | tf_op jit(solution)/shard_map/while/body/eval_jaxpr/ppermute | solution.py:26
  134.3 3.0 %collective-permute-start.1 = (f32[1,16,64]{2,1,0:T(8,128)S(1)}, f32[1,16,64]{2,1,0:T(8,128)S(1)}, u32[]{:S(2)}, u32[]{:S(2)}) collective-permute-start(f32[1,16,64]{2,1,0:T(8,128)S(1)} %get-tuple-element.214), channel_id=1, source_target_pairs={{1,0},{2,1},{3,2},{4,3},{5,4},{6,5},{7,6},{0,7},{9,8},{10,9},{11,1... | collective-permute-start | bytes 12296 | tf_op jit(solution)/shard_map/while/body/eval_jaxpr/ppermute | solution.py:26
  139.5 3.0 %collective-permute-start.1 = (f32[1,16,64]{2,1,0:T(8,128)S(1)}, f32[1,16,64]{2,1,0:T(8,128)S(1)}, u32[]{:S(2)}, u32[]{:S(2)}) collective-permute-start(f32[1,16,64]{2,1,0:T(8,128)S(1)} %get-tuple-element.214), channel_id=1, source_target_pairs={{1,0},{2,1},{3,2},{4,3},{5,4},{6,5},{7,6},{0,7},{9,8},{10,9},{11,1... | collective-permute-start | bytes 12296 | tf_op jit(solution)/shard_map/while/body/eval_jaxpr/ppermute | solution.py:26
  144.8 2.8 collective-permute-start.1
  149.9 2.8 collective-permute-start.1
  155.1 2.8 collective-permute-start.1
  157.9 1.1 collective-permute-done
  160.2 2.9 collective-permute-start.1
  163.1 1.0 collective-permute-done
  165.4 2.9 collective-permute-start.1
  170.5 2.8 collective-permute-start.1
  175.7 2.9 collective-permute-start.1
  180.8 2.9 collective-permute-start.1
  185.9 2.9 collective-permute-start.1
  191.1 2.9 collective-permute-start.1
  196.2 2.9 collective-permute-start.1
  200.4 1.1 collective-permute-start
  201.5 2.7 collective-permute-start.1
  205.6 1.1 collective-permute-start
  206.6 2.7 collective-permute-start.1
  210.7 1.1 collective-permute-start
  211.8 2.7 collective-permute-start.1
  214.5 1.2 collective-permute-done
  216.9 2.8 collective-permute-start.1
  219.7 1.0 collective-permute-done
  222.1 2.8 collective-permute-start.1
  226.2 1.0 collective-permute-start
  227.2 2.8 collective-permute-start.1
  231.4 1.0 collective-permute-start
  232.4 2.8 collective-permute-start.1
  236.5 1.0 collective-permute-start.6
  237.5 2.8 collective-permute-start.7
  241.6 2.6 broadcast_in_dim.12
  244.2 4.0 %reshape.50 = f32[4,32,128]{2,1,0:T(8,128)S(1)} reshape(f32[2,2,16,2,64,2]{5,4,3,2,1,0:T(8,128)} %broadcast_in_dim.12) | data formatting | bytes 131072 | tf_op jit(solution)/shard_map/reshape | solution.py:93
  248.2 40.6 %collective-permute-start.8 = (f32[4,32,128]{2,1,0:T(8,128)S(1)}, f32[4,32,128]{2,1,0:T(8,128)S(1)}, u32[]{:S(2)}, u32[]{:S(2)}) collective-permute-start(f32[4,32,128]{2,1,0:T(8,128)S(1)} %add.249), channel_id=1, source_target_pairs={{0,8},{8,16},{16,24},{24,32},{32,40},{40,48},{48,56},{56,64},{64,7... | collective-permute-start | bytes 196616 | tf_op jit(solution)/shard_map/ppermute | solution.py:60
  288.8 1.3 collective-permute-done.8
  (497 shorter events, 58.9 us)
Async XLA Ops:
  9.5 16.3 %collective-permute-start.5 = (f32[1,16,64]{2,1,0:T(8,128)S(1)}, f32[1,16,64]{2,1,0:T(8,128)S(1)}, u32[]{:S(2)}, u32[]{:S(2)}) collective-permute-start(f32[1,16,64]{2,1,0:T(8,128)S(1)} %get-tuple-element.171), channel_id=1, source_target_pairs={{1,0},{2,1},{3,2},{4,3},{5,4},{6,5},{7,6},{0,7},{9,8},{10,9},{11,1... | collective-permute-start | bytes 12296 | tf_op jit(solution)/shard_map/ppermute | solution.py:26
  14.1 11.8 %collective-permute-start.4 = (f32[1,16,64]{2,1,0:T(8,128)S(1)}, f32[1,16,64]{2,1,0:T(8,128)S(1)}, u32[]{:S(2)}, u32[]{:S(2)}) collective-permute-start(f32[1,16,64]{2,1,0:T(8,128)S(1)} %get-tuple-element.170), channel_id=1, source_target_pairs={{0,1},{1,2},{2,3},{3,4},{4,5},{5,6},{6,7},{7,0},{8,9},{9,10},{10,1... | collective-permute-start | bytes 12296 | tf_op jit(solution)/shard_map/ppermute | solution.py:24
  14.1 18.6 %collective-permute-start.3 = (f32[2,4,32,128]{3,2,1,0:T(8,128)S(1)}, f32[2,4,32,128]{3,2,1,0:T(8,128)S(1)}, u32[]{:S(2)}, u32[]{:S(2)}) collective-permute-start(f32[2,4,32,128]{3,2,1,0:T(8,128)S(1)} %pad_maximum_fusion.1), channel_id=1, source_target_pairs={{1,0},{2,1},{3,2},{4,3},{5,4},{6,5},{7,6},{0,7},{9,8},{10,9},{11,1... | collective-permute-start | bytes 393224 | tf_op jit(solution)/shard_map/ppermute | solution.py:26
  17.8 15.0 %collective-permute-start.2 = (f32[2,4,32,128]{3,2,1,0:T(8,128)S(1)}, f32[2,4,32,128]{3,2,1,0:T(8,128)S(1)}, u32[]{:S(2)}, u32[]{:S(2)}) collective-permute-start(f32[2,4,32,128]{3,2,1,0:T(8,128)S(1)} %pad_maximum_fusion.1), channel_id=1, source_target_pairs={{0,1},{1,2},{2,3},{3,4},{4,5},{5,6},{6,7},{7,0},{8,9},{9,10},{10,1... | collective-permute-start | bytes 393224 | tf_op jit(solution)/shard_map/ppermute | solution.py:24
  44.6 29.3 %all-to-all-start = ((f32[32,1,4096]{2,1,0:T(1,128)}), f32[32,1,4096]{2,1,0:T(1,128)S(1)}, u32[]{:S(2)}, u32[]{:S(2)}) async-start(f32[32,1,4096]{2,1,0:T(1,128)} %reshape.51), calls=%async_computation | async-start | bytes 1048576 | tf_op jit(solution)/shard_map/all_to_all | solution.py:35
  76.9 4.7 %collective-permute-start = (f32[1,16,64]{2,1,0:T(8,128)S(1)}, f32[1,16,64]{2,1,0:T(8,128)S(1)}, u32[]{:S(2)}, u32[]{:S(2)}) collective-permute-start(f32[1,16,64]{2,1,0:T(8,128)S(1)} %get-tuple-element.213), channel_id=1, source_target_pairs={{0,1},{1,2},{2,3},{3,4},{4,5},{5,6},{6,7},{7,0},{8,9},{9,10},{10,1... | collective-permute-start | bytes 12296 | tf_op jit(solution)/shard_map/while/body/eval_jaxpr/ppermute | solution.py:24
  77.0 4.6 %collective-permute-start.1 = (f32[1,16,64]{2,1,0:T(8,128)S(1)}, f32[1,16,64]{2,1,0:T(8,128)S(1)}, u32[]{:S(2)}, u32[]{:S(2)}) collective-permute-start(f32[1,16,64]{2,1,0:T(8,128)S(1)} %get-tuple-element.214), channel_id=1, source_target_pairs={{1,0},{2,1},{3,2},{4,3},{5,4},{6,5},{7,6},{0,7},{9,8},{10,9},{11,1... | collective-permute-start | bytes 12296 | tf_op jit(solution)/shard_map/while/body/eval_jaxpr/ppermute | solution.py:26
  81.9 4.7 %collective-permute-start = (f32[1,16,64]{2,1,0:T(8,128)S(1)}, f32[1,16,64]{2,1,0:T(8,128)S(1)}, u32[]{:S(2)}, u32[]{:S(2)}) collective-permute-start(f32[1,16,64]{2,1,0:T(8,128)S(1)} %get-tuple-element.213), channel_id=1, source_target_pairs={{0,1},{1,2},{2,3},{3,4},{4,5},{5,6},{6,7},{7,0},{8,9},{9,10},{10,1... | collective-permute-start | bytes 12296 | tf_op jit(solution)/shard_map/while/body/eval_jaxpr/ppermute | solution.py:24
  82.5 4.1 %collective-permute-start.1 = (f32[1,16,64]{2,1,0:T(8,128)S(1)}, f32[1,16,64]{2,1,0:T(8,128)S(1)}, u32[]{:S(2)}, u32[]{:S(2)}) collective-permute-start(f32[1,16,64]{2,1,0:T(8,128)S(1)} %get-tuple-element.214), channel_id=1, source_target_pairs={{1,0},{2,1},{3,2},{4,3},{5,4},{6,5},{7,6},{0,7},{9,8},{10,9},{11,1... | collective-permute-start | bytes 12296 | tf_op jit(solution)/shard_map/while/body/eval_jaxpr/ppermute | solution.py:26
  87.0 4.8 %collective-permute-start = (f32[1,16,64]{2,1,0:T(8,128)S(1)}, f32[1,16,64]{2,1,0:T(8,128)S(1)}, u32[]{:S(2)}, u32[]{:S(2)}) collective-permute-start(f32[1,16,64]{2,1,0:T(8,128)S(1)} %get-tuple-element.213), channel_id=1, source_target_pairs={{0,1},{1,2},{2,3},{3,4},{4,5},{5,6},{6,7},{7,0},{8,9},{9,10},{10,1... | collective-permute-start | bytes 12296 | tf_op jit(solution)/shard_map/while/body/eval_jaxpr/ppermute | solution.py:24
  87.7 4.1 %collective-permute-start.1 = (f32[1,16,64]{2,1,0:T(8,128)S(1)}, f32[1,16,64]{2,1,0:T(8,128)S(1)}, u32[]{:S(2)}, u32[]{:S(2)}) collective-permute-start(f32[1,16,64]{2,1,0:T(8,128)S(1)} %get-tuple-element.214), channel_id=1, source_target_pairs={{1,0},{2,1},{3,2},{4,3},{5,4},{6,5},{7,6},{0,7},{9,8},{10,9},{11,1... | collective-permute-start | bytes 12296 | tf_op jit(solution)/shard_map/while/body/eval_jaxpr/ppermute | solution.py:26
  92.2 4.8 %collective-permute-start = (f32[1,16,64]{2,1,0:T(8,128)S(1)}, f32[1,16,64]{2,1,0:T(8,128)S(1)}, u32[]{:S(2)}, u32[]{:S(2)}) collective-permute-start(f32[1,16,64]{2,1,0:T(8,128)S(1)} %get-tuple-element.213), channel_id=1, source_target_pairs={{0,1},{1,2},{2,3},{3,4},{4,5},{5,6},{6,7},{7,0},{8,9},{9,10},{10,1... | collective-permute-start | bytes 12296 | tf_op jit(solution)/shard_map/while/body/eval_jaxpr/ppermute | solution.py:24
  92.8 4.1 %collective-permute-start.1 = (f32[1,16,64]{2,1,0:T(8,128)S(1)}, f32[1,16,64]{2,1,0:T(8,128)S(1)}, u32[]{:S(2)}, u32[]{:S(2)}) collective-permute-start(f32[1,16,64]{2,1,0:T(8,128)S(1)} %get-tuple-element.214), channel_id=1, source_target_pairs={{1,0},{2,1},{3,2},{4,3},{5,4},{6,5},{7,6},{0,7},{9,8},{10,9},{11,1... | collective-permute-start | bytes 12296 | tf_op jit(solution)/shard_map/while/body/eval_jaxpr/ppermute | solution.py:26
  97.3 5.1 %collective-permute-start = (f32[1,16,64]{2,1,0:T(8,128)S(1)}, f32[1,16,64]{2,1,0:T(8,128)S(1)}, u32[]{:S(2)}, u32[]{:S(2)}) collective-permute-start(f32[1,16,64]{2,1,0:T(8,128)S(1)} %get-tuple-element.213), channel_id=1, source_target_pairs={{0,1},{1,2},{2,3},{3,4},{4,5},{5,6},{6,7},{7,0},{8,9},{9,10},{10,1... | collective-permute-start | bytes 12296 | tf_op jit(solution)/shard_map/while/body/eval_jaxpr/ppermute | solution.py:24
  98.0 4.5 %collective-permute-start.1 = (f32[1,16,64]{2,1,0:T(8,128)S(1)}, f32[1,16,64]{2,1,0:T(8,128)S(1)}, u32[]{:S(2)}, u32[]{:S(2)}) collective-permute-start(f32[1,16,64]{2,1,0:T(8,128)S(1)} %get-tuple-element.214), channel_id=1, source_target_pairs={{1,0},{2,1},{3,2},{4,3},{5,4},{6,5},{7,6},{0,7},{9,8},{10,9},{11,1... | collective-permute-start | bytes 12296 | tf_op jit(solution)/shard_map/while/body/eval_jaxpr/ppermute | solution.py:26
  102.8 4.7 %collective-permute-start = (f32[1,16,64]{2,1,0:T(8,128)S(1)}, f32[1,16,64]{2,1,0:T(8,128)S(1)}, u32[]{:S(2)}, u32[]{:S(2)}) collective-permute-start(f32[1,16,64]{2,1,0:T(8,128)S(1)} %get-tuple-element.213), channel_id=1, source_target_pairs={{0,1},{1,2},{2,3},{3,4},{4,5},{5,6},{6,7},{7,0},{8,9},{9,10},{10,1... | collective-permute-start | bytes 12296 | tf_op jit(solution)/shard_map/while/body/eval_jaxpr/ppermute | solution.py:24
  103.5 4.0 %collective-permute-start.1 = (f32[1,16,64]{2,1,0:T(8,128)S(1)}, f32[1,16,64]{2,1,0:T(8,128)S(1)}, u32[]{:S(2)}, u32[]{:S(2)}) collective-permute-start(f32[1,16,64]{2,1,0:T(8,128)S(1)} %get-tuple-element.214), channel_id=1, source_target_pairs={{1,0},{2,1},{3,2},{4,3},{5,4},{6,5},{7,6},{0,7},{9,8},{10,9},{11,1... | collective-permute-start | bytes 12296 | tf_op jit(solution)/shard_map/while/body/eval_jaxpr/ppermute | solution.py:26
  107.9 4.7 %collective-permute-start = (f32[1,16,64]{2,1,0:T(8,128)S(1)}, f32[1,16,64]{2,1,0:T(8,128)S(1)}, u32[]{:S(2)}, u32[]{:S(2)}) collective-permute-start(f32[1,16,64]{2,1,0:T(8,128)S(1)} %get-tuple-element.213), channel_id=1, source_target_pairs={{0,1},{1,2},{2,3},{3,4},{4,5},{5,6},{6,7},{7,0},{8,9},{9,10},{10,1... | collective-permute-start | bytes 12296 | tf_op jit(solution)/shard_map/while/body/eval_jaxpr/ppermute | solution.py:24
  108.6 4.0 %collective-permute-start.1 = (f32[1,16,64]{2,1,0:T(8,128)S(1)}, f32[1,16,64]{2,1,0:T(8,128)S(1)}, u32[]{:S(2)}, u32[]{:S(2)}) collective-permute-start(f32[1,16,64]{2,1,0:T(8,128)S(1)} %get-tuple-element.214), channel_id=1, source_target_pairs={{1,0},{2,1},{3,2},{4,3},{5,4},{6,5},{7,6},{0,7},{9,8},{10,9},{11,1... | collective-permute-start | bytes 12296 | tf_op jit(solution)/shard_map/while/body/eval_jaxpr/ppermute | solution.py:26
  112.9 4.8 %collective-permute-start = (f32[1,16,64]{2,1,0:T(8,128)S(1)}, f32[1,16,64]{2,1,0:T(8,128)S(1)}, u32[]{:S(2)}, u32[]{:S(2)}) collective-permute-start(f32[1,16,64]{2,1,0:T(8,128)S(1)} %get-tuple-element.213), channel_id=1, source_target_pairs={{0,1},{1,2},{2,3},{3,4},{4,5},{5,6},{6,7},{7,0},{8,9},{9,10},{10,1... | collective-permute-start | bytes 12296 | tf_op jit(solution)/shard_map/while/body/eval_jaxpr/ppermute | solution.py:24
  113.9 3.8 %collective-permute-start.1 = (f32[1,16,64]{2,1,0:T(8,128)S(1)}, f32[1,16,64]{2,1,0:T(8,128)S(1)}, u32[]{:S(2)}, u32[]{:S(2)}) collective-permute-start(f32[1,16,64]{2,1,0:T(8,128)S(1)} %get-tuple-element.214), channel_id=1, source_target_pairs={{1,0},{2,1},{3,2},{4,3},{5,4},{6,5},{7,6},{0,7},{9,8},{10,9},{11,1... | collective-permute-start | bytes 12296 | tf_op jit(solution)/shard_map/while/body/eval_jaxpr/ppermute | solution.py:26
  118.1 4.8 %collective-permute-start = (f32[1,16,64]{2,1,0:T(8,128)S(1)}, f32[1,16,64]{2,1,0:T(8,128)S(1)}, u32[]{:S(2)}, u32[]{:S(2)}) collective-permute-start(f32[1,16,64]{2,1,0:T(8,128)S(1)} %get-tuple-element.213), channel_id=1, source_target_pairs={{0,1},{1,2},{2,3},{3,4},{4,5},{5,6},{6,7},{7,0},{8,9},{9,10},{10,1... | collective-permute-start | bytes 12296 | tf_op jit(solution)/shard_map/while/body/eval_jaxpr/ppermute | solution.py:24
  118.9 4.0 %collective-permute-start.1 = (f32[1,16,64]{2,1,0:T(8,128)S(1)}, f32[1,16,64]{2,1,0:T(8,128)S(1)}, u32[]{:S(2)}, u32[]{:S(2)}) collective-permute-start(f32[1,16,64]{2,1,0:T(8,128)S(1)} %get-tuple-element.214), channel_id=1, source_target_pairs={{1,0},{2,1},{3,2},{4,3},{5,4},{6,5},{7,6},{0,7},{9,8},{10,9},{11,1... | collective-permute-start | bytes 12296 | tf_op jit(solution)/shard_map/while/body/eval_jaxpr/ppermute | solution.py:26
  123.2 4.8 %collective-permute-start = (f32[1,16,64]{2,1,0:T(8,128)S(1)}, f32[1,16,64]{2,1,0:T(8,128)S(1)}, u32[]{:S(2)}, u32[]{:S(2)}) collective-permute-start(f32[1,16,64]{2,1,0:T(8,128)S(1)} %get-tuple-element.213), channel_id=1, source_target_pairs={{0,1},{1,2},{2,3},{3,4},{4,5},{5,6},{6,7},{7,0},{8,9},{9,10},{10,1... | collective-permute-start | bytes 12296 | tf_op jit(solution)/shard_map/while/body/eval_jaxpr/ppermute | solution.py:24
  124.0 4.0 %collective-permute-start.1 = (f32[1,16,64]{2,1,0:T(8,128)S(1)}, f32[1,16,64]{2,1,0:T(8,128)S(1)}, u32[]{:S(2)}, u32[]{:S(2)}) collective-permute-start(f32[1,16,64]{2,1,0:T(8,128)S(1)} %get-tuple-element.214), channel_id=1, source_target_pairs={{1,0},{2,1},{3,2},{4,3},{5,4},{6,5},{7,6},{0,7},{9,8},{10,9},{11,1... | collective-permute-start | bytes 12296 | tf_op jit(solution)/shard_map/while/body/eval_jaxpr/ppermute | solution.py:26
  128.4 4.8 %collective-permute-start = (f32[1,16,64]{2,1,0:T(8,128)S(1)}, f32[1,16,64]{2,1,0:T(8,128)S(1)}, u32[]{:S(2)}, u32[]{:S(2)}) collective-permute-start(f32[1,16,64]{2,1,0:T(8,128)S(1)} %get-tuple-element.213), channel_id=1, source_target_pairs={{0,1},{1,2},{2,3},{3,4},{4,5},{5,6},{6,7},{7,0},{8,9},{9,10},{10,1... | collective-permute-start | bytes 12296 | tf_op jit(solution)/shard_map/while/body/eval_jaxpr/ppermute | solution.py:24
  129.2 4.0 %collective-permute-start.1 = (f32[1,16,64]{2,1,0:T(8,128)S(1)}, f32[1,16,64]{2,1,0:T(8,128)S(1)}, u32[]{:S(2)}, u32[]{:S(2)}) collective-permute-start(f32[1,16,64]{2,1,0:T(8,128)S(1)} %get-tuple-element.214), channel_id=1, source_target_pairs={{1,0},{2,1},{3,2},{4,3},{5,4},{6,5},{7,6},{0,7},{9,8},{10,9},{11,1... | collective-permute-start | bytes 12296 | tf_op jit(solution)/shard_map/while/body/eval_jaxpr/ppermute | solution.py:26
  133.5 4.8 %collective-permute-start = (f32[1,16,64]{2,1,0:T(8,128)S(1)}, f32[1,16,64]{2,1,0:T(8,128)S(1)}, u32[]{:S(2)}, u32[]{:S(2)}) collective-permute-start(f32[1,16,64]{2,1,0:T(8,128)S(1)} %get-tuple-element.213), channel_id=1, source_target_pairs={{0,1},{1,2},{2,3},{3,4},{4,5},{5,6},{6,7},{7,0},{8,9},{9,10},{10,1... | collective-permute-start | bytes 12296 | tf_op jit(solution)/shard_map/while/body/eval_jaxpr/ppermute | solution.py:24
  134.3 4.0 %collective-permute-start.1 = (f32[1,16,64]{2,1,0:T(8,128)S(1)}, f32[1,16,64]{2,1,0:T(8,128)S(1)}, u32[]{:S(2)}, u32[]{:S(2)}) collective-permute-start(f32[1,16,64]{2,1,0:T(8,128)S(1)} %get-tuple-element.214), channel_id=1, source_target_pairs={{1,0},{2,1},{3,2},{4,3},{5,4},{6,5},{7,6},{0,7},{9,8},{10,9},{11,1... | collective-permute-start | bytes 12296 | tf_op jit(solution)/shard_map/while/body/eval_jaxpr/ppermute | solution.py:26
  138.7 4.8 %collective-permute-start = (f32[1,16,64]{2,1,0:T(8,128)S(1)}, f32[1,16,64]{2,1,0:T(8,128)S(1)}, u32[]{:S(2)}, u32[]{:S(2)}) collective-permute-start(f32[1,16,64]{2,1,0:T(8,128)S(1)} %get-tuple-element.213), channel_id=1, source_target_pairs={{0,1},{1,2},{2,3},{3,4},{4,5},{5,6},{6,7},{7,0},{8,9},{9,10},{10,1... | collective-permute-start | bytes 12296 | tf_op jit(solution)/shard_map/while/body/eval_jaxpr/ppermute | solution.py:24
  139.5 4.0 %collective-permute-start.1 = (f32[1,16,64]{2,1,0:T(8,128)S(1)}, f32[1,16,64]{2,1,0:T(8,128)S(1)}, u32[]{:S(2)}, u32[]{:S(2)}) collective-permute-start(f32[1,16,64]{2,1,0:T(8,128)S(1)} %get-tuple-element.214), channel_id=1, source_target_pairs={{1,0},{2,1},{3,2},{4,3},{5,4},{6,5},{7,6},{0,7},{9,8},{10,9},{11,1... | collective-permute-start | bytes 12296 | tf_op jit(solution)/shard_map/while/body/eval_jaxpr/ppermute | solution.py:26
  143.8 4.8 %collective-permute-start = (f32[1,16,64]{2,1,0:T(8,128)S(1)}, f32[1,16,64]{2,1,0:T(8,128)S(1)}, u32[]{:S(2)}, u32[]{:S(2)}) collective-permute-start(f32[1,16,64]{2,1,0:T(8,128)S(1)} %get-tuple-element.213), channel_id=1, source_target_pairs={{0,1},{1,2},{2,3},{3,4},{4,5},{5,6},{6,7},{7,0},{8,9},{9,10},{10,1... | collective-permute-start | bytes 12296 | tf_op jit(solution)/shard_map/while/body/eval_jaxpr/ppermute | solution.py:24
  144.8 3.8 %collective-permute-start.1 = (f32[1,16,64]{2,1,0:T(8,128)S(1)}, f32[1,16,64]{2,1,0:T(8,128)S(1)}, u32[]{:S(2)}, u32[]{:S(2)}) collective-permute-start(f32[1,16,64]{2,1,0:T(8,128)S(1)} %get-tuple-element.214), channel_id=1, source_target_pairs={{1,0},{2,1},{3,2},{4,3},{5,4},{6,5},{7,6},{0,7},{9,8},{10,9},{11,1... | collective-permute-start | bytes 12296 | tf_op jit(solution)/shard_map/while/body/eval_jaxpr/ppermute | solution.py:26
  148.9 4.8 %collective-permute-start = (f32[1,16,64]{2,1,0:T(8,128)S(1)}, f32[1,16,64]{2,1,0:T(8,128)S(1)}, u32[]{:S(2)}, u32[]{:S(2)}) collective-permute-start(f32[1,16,64]{2,1,0:T(8,128)S(1)} %get-tuple-element.213), channel_id=1, source_target_pairs={{0,1},{1,2},{2,3},{3,4},{4,5},{5,6},{6,7},{7,0},{8,9},{9,10},{10,1... | collective-permute-start | bytes 12296 | tf_op jit(solution)/shard_map/while/body/eval_jaxpr/ppermute | solution.py:24
  149.9 3.8 %collective-permute-start.1 = (f32[1,16,64]{2,1,0:T(8,128)S(1)}, f32[1,16,64]{2,1,0:T(8,128)S(1)}, u32[]{:S(2)}, u32[]{:S(2)}) collective-permute-start(f32[1,16,64]{2,1,0:T(8,128)S(1)} %get-tuple-element.214), channel_id=1, source_target_pairs={{1,0},{2,1},{3,2},{4,3},{5,4},{6,5},{7,6},{0,7},{9,8},{10,9},{11,1... | collective-permute-start | bytes 12296 | tf_op jit(solution)/shard_map/while/body/eval_jaxpr/ppermute | solution.py:26
  154.1 4.9 %collective-permute-start = (f32[1,16,64]{2,1,0:T(8,128)S(1)}, f32[1,16,64]{2,1,0:T(8,128)S(1)}, u32[]{:S(2)}, u32[]{:S(2)}) collective-permute-start(f32[1,16,64]{2,1,0:T(8,128)S(1)} %get-tuple-element.213), channel_id=1, source_target_pairs={{0,1},{1,2},{2,3},{3,4},{4,5},{5,6},{6,7},{7,0},{8,9},{9,10},{10,1... | collective-permute-start | bytes 12296 | tf_op jit(solution)/shard_map/while/body/eval_jaxpr/ppermute | solution.py:24
  155.1 4.0 %collective-permute-start.1 = (f32[1,16,64]{2,1,0:T(8,128)S(1)}, f32[1,16,64]{2,1,0:T(8,128)S(1)}, u32[]{:S(2)}, u32[]{:S(2)}) collective-permute-start(f32[1,16,64]{2,1,0:T(8,128)S(1)} %get-tuple-element.214), channel_id=1, source_target_pairs={{1,0},{2,1},{3,2},{4,3},{5,4},{6,5},{7,6},{0,7},{9,8},{10,9},{11,1... | collective-permute-start | bytes 12296 | tf_op jit(solution)/shard_map/while/body/eval_jaxpr/ppermute | solution.py:26
  159.4 4.7 %collective-permute-start = (f32[1,16,64]{2,1,0:T(8,128)S(1)}, f32[1,16,64]{2,1,0:T(8,128)S(1)}, u32[]{:S(2)}, u32[]{:S(2)}) collective-permute-start(f32[1,16,64]{2,1,0:T(8,128)S(1)} %get-tuple-element.213), channel_id=1, source_target_pairs={{0,1},{1,2},{2,3},{3,4},{4,5},{5,6},{6,7},{7,0},{8,9},{9,10},{10,1... | collective-permute-start | bytes 12296 | tf_op jit(solution)/shard_map/while/body/eval_jaxpr/ppermute | solution.py:24
  160.2 3.9 %collective-permute-start.1 = (f32[1,16,64]{2,1,0:T(8,128)S(1)}, f32[1,16,64]{2,1,0:T(8,128)S(1)}, u32[]{:S(2)}, u32[]{:S(2)}) collective-permute-start(f32[1,16,64]{2,1,0:T(8,128)S(1)} %get-tuple-element.214), channel_id=1, source_target_pairs={{1,0},{2,1},{3,2},{4,3},{5,4},{6,5},{7,6},{0,7},{9,8},{10,9},{11,1... | collective-permute-start | bytes 12296 | tf_op jit(solution)/shard_map/while/body/eval_jaxpr/ppermute | solution.py:26
  164.5 4.7 %collective-permute-start = (f32[1,16,64]{2,1,0:T(8,128)S(1)}, f32[1,16,64]{2,1,0:T(8,128)S(1)}, u32[]{:S(2)}, u32[]{:S(2)}) collective-permute-start(f32[1,16,64]{2,1,0:T(8,128)S(1)} %get-tuple-element.213), channel_id=1, source_target_pairs={{0,1},{1,2},{2,3},{3,4},{4,5},{5,6},{6,7},{7,0},{8,9},{9,10},{10,1... | collective-permute-start | bytes 12296 | tf_op jit(solution)/shard_map/while/body/eval_jaxpr/ppermute | solution.py:24
  165.4 3.8 %collective-permute-start.1 = (f32[1,16,64]{2,1,0:T(8,128)S(1)}, f32[1,16,64]{2,1,0:T(8,128)S(1)}, u32[]{:S(2)}, u32[]{:S(2)}) collective-permute-start(f32[1,16,64]{2,1,0:T(8,128)S(1)} %get-tuple-element.214), channel_id=1, source_target_pairs={{1,0},{2,1},{3,2},{4,3},{5,4},{6,5},{7,6},{0,7},{9,8},{10,9},{11,1... | collective-permute-start | bytes 12296 | tf_op jit(solution)/shard_map/while/body/eval_jaxpr/ppermute | solution.py:26
  169.6 4.8 %collective-permute-start = (f32[1,16,64]{2,1,0:T(8,128)S(1)}, f32[1,16,64]{2,1,0:T(8,128)S(1)}, u32[]{:S(2)}, u32[]{:S(2)}) collective-permute-start(f32[1,16,64]{2,1,0:T(8,128)S(1)} %get-tuple-element.213), channel_id=1, source_target_pairs={{0,1},{1,2},{2,3},{3,4},{4,5},{5,6},{6,7},{7,0},{8,9},{9,10},{10,1... | collective-permute-start | bytes 12296 | tf_op jit(solution)/shard_map/while/body/eval_jaxpr/ppermute | solution.py:24
  170.5 3.8 %collective-permute-start.1 = (f32[1,16,64]{2,1,0:T(8,128)S(1)}, f32[1,16,64]{2,1,0:T(8,128)S(1)}, u32[]{:S(2)}, u32[]{:S(2)}) collective-permute-start(f32[1,16,64]{2,1,0:T(8,128)S(1)} %get-tuple-element.214), channel_id=1, source_target_pairs={{1,0},{2,1},{3,2},{4,3},{5,4},{6,5},{7,6},{0,7},{9,8},{10,9},{11,1... | collective-permute-start | bytes 12296 | tf_op jit(solution)/shard_map/while/body/eval_jaxpr/ppermute | solution.py:26
  174.7 4.8 %collective-permute-start = (f32[1,16,64]{2,1,0:T(8,128)S(1)}, f32[1,16,64]{2,1,0:T(8,128)S(1)}, u32[]{:S(2)}, u32[]{:S(2)}) collective-permute-start(f32[1,16,64]{2,1,0:T(8,128)S(1)} %get-tuple-element.213), channel_id=1, source_target_pairs={{0,1},{1,2},{2,3},{3,4},{4,5},{5,6},{6,7},{7,0},{8,9},{9,10},{10,1... | collective-permute-start | bytes 12296 | tf_op jit(solution)/shard_map/while/body/eval_jaxpr/ppermute | solution.py:24
  175.7 3.8 %collective-permute-start.1 = (f32[1,16,64]{2,1,0:T(8,128)S(1)}, f32[1,16,64]{2,1,0:T(8,128)S(1)}, u32[]{:S(2)}, u32[]{:S(2)}) collective-permute-start(f32[1,16,64]{2,1,0:T(8,128)S(1)} %get-tuple-element.214), channel_id=1, source_target_pairs={{1,0},{2,1},{3,2},{4,3},{5,4},{6,5},{7,6},{0,7},{9,8},{10,9},{11,1... | collective-permute-start | bytes 12296 | tf_op jit(solution)/shard_map/while/body/eval_jaxpr/ppermute | solution.py:26
  179.8 4.8 %collective-permute-start = (f32[1,16,64]{2,1,0:T(8,128)S(1)}, f32[1,16,64]{2,1,0:T(8,128)S(1)}, u32[]{:S(2)}, u32[]{:S(2)}) collective-permute-start(f32[1,16,64]{2,1,0:T(8,128)S(1)} %get-tuple-element.213), channel_id=1, source_target_pairs={{0,1},{1,2},{2,3},{3,4},{4,5},{5,6},{6,7},{7,0},{8,9},{9,10},{10,1... | collective-permute-start | bytes 12296 | tf_op jit(solution)/shard_map/while/body/eval_jaxpr/ppermute | solution.py:24
  180.8 3.8 %collective-permute-start.1 = (f32[1,16,64]{2,1,0:T(8,128)S(1)}, f32[1,16,64]{2,1,0:T(8,128)S(1)}, u32[]{:S(2)}, u32[]{:S(2)}) collective-permute-start(f32[1,16,64]{2,1,0:T(8,128)S(1)} %get-tuple-element.214), channel_id=1, source_target_pairs={{1,0},{2,1},{3,2},{4,3},{5,4},{6,5},{7,6},{0,7},{9,8},{10,9},{11,1... | collective-permute-start | bytes 12296 | tf_op jit(solution)/shard_map/while/body/eval_jaxpr/ppermute | solution.py:26
  185.0 4.8 %collective-permute-start = (f32[1,16,64]{2,1,0:T(8,128)S(1)}, f32[1,16,64]{2,1,0:T(8,128)S(1)}, u32[]{:S(2)}, u32[]{:S(2)}) collective-permute-start(f32[1,16,64]{2,1,0:T(8,128)S(1)} %get-tuple-element.213), channel_id=1, source_target_pairs={{0,1},{1,2},{2,3},{3,4},{4,5},{5,6},{6,7},{7,0},{8,9},{9,10},{10,1... | collective-permute-start | bytes 12296 | tf_op jit(solution)/shard_map/while/body/eval_jaxpr/ppermute | solution.py:24
  185.9 3.8 %collective-permute-start.1 = (f32[1,16,64]{2,1,0:T(8,128)S(1)}, f32[1,16,64]{2,1,0:T(8,128)S(1)}, u32[]{:S(2)}, u32[]{:S(2)}) collective-permute-start(f32[1,16,64]{2,1,0:T(8,128)S(1)} %get-tuple-element.214), channel_id=1, source_target_pairs={{1,0},{2,1},{3,2},{4,3},{5,4},{6,5},{7,6},{0,7},{9,8},{10,9},{11,1... | collective-permute-start | bytes 12296 | tf_op jit(solution)/shard_map/while/body/eval_jaxpr/ppermute | solution.py:26
  190.1 4.8 %collective-permute-start = (f32[1,16,64]{2,1,0:T(8,128)S(1)}, f32[1,16,64]{2,1,0:T(8,128)S(1)}, u32[]{:S(2)}, u32[]{:S(2)}) collective-permute-start(f32[1,16,64]{2,1,0:T(8,128)S(1)} %get-tuple-element.213), channel_id=1, source_target_pairs={{0,1},{1,2},{2,3},{3,4},{4,5},{5,6},{6,7},{7,0},{8,9},{9,10},{10,1... | collective-permute-start | bytes 12296 | tf_op jit(solution)/shard_map/while/body/eval_jaxpr/ppermute | solution.py:24
  191.1 3.8 %collective-permute-start.1 = (f32[1,16,64]{2,1,0:T(8,128)S(1)}, f32[1,16,64]{2,1,0:T(8,128)S(1)}, u32[]{:S(2)}, u32[]{:S(2)}) collective-permute-start(f32[1,16,64]{2,1,0:T(8,128)S(1)} %get-tuple-element.214), channel_id=1, source_target_pairs={{1,0},{2,1},{3,2},{4,3},{5,4},{6,5},{7,6},{0,7},{9,8},{10,9},{11,1... | collective-permute-start | bytes 12296 | tf_op jit(solution)/shard_map/while/body/eval_jaxpr/ppermute | solution.py:26
  195.3 4.8 %collective-permute-start = (f32[1,16,64]{2,1,0:T(8,128)S(1)}, f32[1,16,64]{2,1,0:T(8,128)S(1)}, u32[]{:S(2)}, u32[]{:S(2)}) collective-permute-start(f32[1,16,64]{2,1,0:T(8,128)S(1)} %get-tuple-element.213), channel_id=1, source_target_pairs={{0,1},{1,2},{2,3},{3,4},{4,5},{5,6},{6,7},{7,0},{8,9},{9,10},{10,1... | collective-permute-start | bytes 12296 | tf_op jit(solution)/shard_map/while/body/eval_jaxpr/ppermute | solution.py:24
  196.2 3.8 %collective-permute-start.1 = (f32[1,16,64]{2,1,0:T(8,128)S(1)}, f32[1,16,64]{2,1,0:T(8,128)S(1)}, u32[]{:S(2)}, u32[]{:S(2)}) collective-permute-start(f32[1,16,64]{2,1,0:T(8,128)S(1)} %get-tuple-element.214), channel_id=1, source_target_pairs={{1,0},{2,1},{3,2},{4,3},{5,4},{6,5},{7,6},{0,7},{9,8},{10,9},{11,1... | collective-permute-start | bytes 12296 | tf_op jit(solution)/shard_map/while/body/eval_jaxpr/ppermute | solution.py:26
  200.4 4.8 %collective-permute-start = (f32[1,16,64]{2,1,0:T(8,128)S(1)}, f32[1,16,64]{2,1,0:T(8,128)S(1)}, u32[]{:S(2)}, u32[]{:S(2)}) collective-permute-start(f32[1,16,64]{2,1,0:T(8,128)S(1)} %get-tuple-element.213), channel_id=1, source_target_pairs={{0,1},{1,2},{2,3},{3,4},{4,5},{5,6},{6,7},{7,0},{8,9},{9,10},{10,1... | collective-permute-start | bytes 12296 | tf_op jit(solution)/shard_map/while/body/eval_jaxpr/ppermute | solution.py:24
  205.6 4.8 %collective-permute-start = (f32[1,16,64]{2,1,0:T(8,128)S(1)}, f32[1,16,64]{2,1,0:T(8,128)S(1)}, u32[]{:S(2)}, u32[]{:S(2)}) collective-permute-start(f32[1,16,64]{2,1,0:T(8,128)S(1)} %get-tuple-element.213), channel_id=1, source_target_pairs={{0,1},{1,2},{2,3},{3,4},{4,5},{5,6},{6,7},{7,0},{8,9},{9,10},{10,1... | collective-permute-start | bytes 12296 | tf_op jit(solution)/shard_map/while/body/eval_jaxpr/ppermute | solution.py:24
  210.7 5.0 %collective-permute-start = (f32[1,16,64]{2,1,0:T(8,128)S(1)}, f32[1,16,64]{2,1,0:T(8,128)S(1)}, u32[]{:S(2)}, u32[]{:S(2)}) collective-permute-start(f32[1,16,64]{2,1,0:T(8,128)S(1)} %get-tuple-element.213), channel_id=1, source_target_pairs={{0,1},{1,2},{2,3},{3,4},{4,5},{5,6},{6,7},{7,0},{8,9},{9,10},{10,1... | collective-permute-start | bytes 12296 | tf_op jit(solution)/shard_map/while/body/eval_jaxpr/ppermute | solution.py:24
  211.8 3.9 %collective-permute-start.1 = (f32[1,16,64]{2,1,0:T(8,128)S(1)}, f32[1,16,64]{2,1,0:T(8,128)S(1)}, u32[]{:S(2)}, u32[]{:S(2)}) collective-permute-start(f32[1,16,64]{2,1,0:T(8,128)S(1)} %get-tuple-element.214), channel_id=1, source_target_pairs={{1,0},{2,1},{3,2},{4,3},{5,4},{6,5},{7,6},{0,7},{9,8},{10,9},{11,1... | collective-permute-start | bytes 12296 | tf_op jit(solution)/shard_map/while/body/eval_jaxpr/ppermute | solution.py:26
  216.1 4.7 %collective-permute-start = (f32[1,16,64]{2,1,0:T(8,128)S(1)}, f32[1,16,64]{2,1,0:T(8,128)S(1)}, u32[]{:S(2)}, u32[]{:S(2)}) collective-permute-start(f32[1,16,64]{2,1,0:T(8,128)S(1)} %get-tuple-element.213), channel_id=1, source_target_pairs={{0,1},{1,2},{2,3},{3,4},{4,5},{5,6},{6,7},{7,0},{8,9},{9,10},{10,1... | collective-permute-start | bytes 12296 | tf_op jit(solution)/shard_map/while/body/eval_jaxpr/ppermute | solution.py:24
  216.9 3.9 %collective-permute-start.1 = (f32[1,16,64]{2,1,0:T(8,128)S(1)}, f32[1,16,64]{2,1,0:T(8,128)S(1)}, u32[]{:S(2)}, u32[]{:S(2)}) collective-permute-start(f32[1,16,64]{2,1,0:T(8,128)S(1)} %get-tuple-element.214), channel_id=1, source_target_pairs={{1,0},{2,1},{3,2},{4,3},{5,4},{6,5},{7,6},{0,7},{9,8},{10,9},{11,1... | collective-permute-start | bytes 12296 | tf_op jit(solution)/shard_map/while/body/eval_jaxpr/ppermute | solution.py:26
  221.1 4.7 %collective-permute-start = (f32[1,16,64]{2,1,0:T(8,128)S(1)}, f32[1,16,64]{2,1,0:T(8,128)S(1)}, u32[]{:S(2)}, u32[]{:S(2)}) collective-permute-start(f32[1,16,64]{2,1,0:T(8,128)S(1)} %get-tuple-element.213), channel_id=1, source_target_pairs={{0,1},{1,2},{2,3},{3,4},{4,5},{5,6},{6,7},{7,0},{8,9},{9,10},{10,1... | collective-permute-start | bytes 12296 | tf_op jit(solution)/shard_map/while/body/eval_jaxpr/ppermute | solution.py:24
  226.2 4.8 %collective-permute-start = (f32[1,16,64]{2,1,0:T(8,128)S(1)}, f32[1,16,64]{2,1,0:T(8,128)S(1)}, u32[]{:S(2)}, u32[]{:S(2)}) collective-permute-start(f32[1,16,64]{2,1,0:T(8,128)S(1)} %get-tuple-element.213), channel_id=1, source_target_pairs={{0,1},{1,2},{2,3},{3,4},{4,5},{5,6},{6,7},{7,0},{8,9},{9,10},{10,1... | collective-permute-start | bytes 12296 | tf_op jit(solution)/shard_map/while/body/eval_jaxpr/ppermute | solution.py:24
  231.4 4.8 %collective-permute-start = (f32[1,16,64]{2,1,0:T(8,128)S(1)}, f32[1,16,64]{2,1,0:T(8,128)S(1)}, u32[]{:S(2)}, u32[]{:S(2)}) collective-permute-start(f32[1,16,64]{2,1,0:T(8,128)S(1)} %get-tuple-element.213), channel_id=1, source_target_pairs={{0,1},{1,2},{2,3},{3,4},{4,5},{5,6},{6,7},{7,0},{8,9},{9,10},{10,1... | collective-permute-start | bytes 12296 | tf_op jit(solution)/shard_map/while/body/eval_jaxpr/ppermute | solution.py:24
  236.5 4.8 %collective-permute-start.6 = (f32[1,16,64]{2,1,0:T(8,128)S(1)}, f32[1,16,64]{2,1,0:T(8,128)S(1)}, u32[]{:S(2)}, u32[]{:S(2)}) collective-permute-start(f32[1,16,64]{2,1,0:T(8,128)S(1)} %get-tuple-element.166), channel_id=1, source_target_pairs={{0,1},{1,2},{2,3},{3,4},{4,5},{5,6},{6,7},{7,0},{8,9},{9,10},{10,1... | collective-permute-start | bytes 12296 | tf_op jit(solution)/shard_map/ppermute | solution.py:24
  248.2 41.9 %collective-permute-start.8 = (f32[4,32,128]{2,1,0:T(8,128)S(1)}, f32[4,32,128]{2,1,0:T(8,128)S(1)}, u32[]{:S(2)}, u32[]{:S(2)}) collective-permute-start(f32[4,32,128]{2,1,0:T(8,128)S(1)} %add.249), channel_id=1, source_target_pairs={{0,8},{8,16},{16,24},{24,32},{32,40},{40,48},{48,56},{56,64},{64,7... | collective-permute-start | bytes 196616 | tf_op jit(solution)/shard_map/ppermute | solution.py:60
  (9 other events, 92.0 us)
where the time goes:
time: 294 us; the launch traced here: 291 us
  starting transfers between devices  182 us (62%)
  waiting for transfers between devices  50 us (17%)
  local copies, waits for them, and re-layouts  40.2 us (14%)
  other arithmetic  15.1 us (5%)
    ppermute x34, starting transfers between devices, padded_2(): lax.ppermute(head, axis, [((i + 1) % count, i) for i in range(count)])  102 us
    ppermute x1, starting transfers between devices, shifted(): lax.ppermute(shard, axis, [(i, (i + by) % size) for i in range(size)])  40.6 us
    ppermute x34, waiting for transfers between devices, padded_2(): lax.ppermute(tail, axis, [(i, (i + 1) % count) for i in range(count)])  31.5 us
    ppermute x34, starting transfers between devices, padded_2(): lax.ppermute(tail, axis, [(i, (i + 1) % count) for i in range(count)])  27.3 us
    all_to_all x1, waiting for transfers between devices, sent_to_all(): return lax.all_to_all(copies, axis, split_axis=0, concat_axis=0, tiled=True)  17 us
    all_to_all x1, starting transfers between devices, sent_to_all(): return lax.all_to_all(copies, axis, split_axis=0, concat_axis=0, tiled=True)  12.3 us
    reshape x2, local copies, waits for them, and re-layouts, restrict(): values.reshape(extent_z // 2, 2, extent_x // 2, 2, extent_y // 2, 2)  11.1 us
    reshape x2, local copies, waits for them, and re-layouts, prolong(): return spread.reshape(extent_z * 2, extent_x * 2, extent_y * 2)  8 us
  transfers between devices with their start and end apart: 70, of which 34 were waited for; matrix products, arithmetic and copies ran while one was open for 5% of the time, Pallas kernels for 0%

commit v1 on v0

v1 whole, which is shorter than its diff:
```python
import jax
import jax.numpy as jnp
from jax import lax
from jax.experimental import pallas as pl
from jax.experimental.pallas import tpu as pltpu
from jax.sharding import Mesh, PartitionSpec as P

FINE = 4
STEPS = 32
GROUP = 4

fine_along_z = (0.1, 0.12)
fine_along_x = (0.15, 0.12)
fine_along_y = (0.2, 0.12)
coarse_along_z = (0.2, 0.25)
coarse_along_x = (0.3, 0.25)
coarse_along_y = (0.4, 0.25)

AXES = ("z", "h", "c", "l", "y")
SLAB = ("z", "h", "c")
GRID = ("l", "y")
PLANE = ("h", "c", "l", "y")


def weights_of(kind):
    courant, diffuse = kind
    return diffuse + 0.5 * courant, 1.0 - 2.0 * diffuse, diffuse - 0.5 * courant


def line_filter(behind, middle, beyond, kind):
    a, b, c = weights_of(kind)
    return a * behind + b * middle + c * beyond


def even_lanes():
    return lax.broadcasted_iota(jnp.int32, (8, 128), 1) % 2 == 0


def packed_plane_filter(v, even):
    v = line_filter(pltpu.roll(v, 2, 1), v, pltpu.roll(v, 126, 1), coarse_along_y)
    right, left = pltpu.roll(v, 1, 1), pltpu.roll(v, 127, 1)
    behind = jnp.where(even, pltpu.roll(left, 1, 0), right)
    beyond = jnp.where(even, left, pltpu.roll(right, 7, 0))
    return line_filter(behind, v, beyond, coarse_along_x)


def packed_layer(ref, first, even):
    def rows(at):
        near = ref[pl.ds(first + at, 8, stride=4), :] + ref[pl.ds(first + at + 1, 8, stride=4), :]
        far = ref[pl.ds(first + 32 + at, 8, stride=4), :] + ref[pl.ds(first + 33 + at, 8, stride=4), :]
        return near + far

    low, high = rows(0), rows(2)
    return 0.125 * jnp.where(even, low + pltpu.roll(low, 127, 1), high + pltpu.roll(high, 1, 1))


def fine_kernel(start, rates, low, high, smooth_out, send_out, wide, ends):
    even = even_lanes()
    is_first = (lax.axis_index("z") == 0) & (lax.axis_index("h") == 0) & (lax.axis_index("c") == 0)
    wide[0:128] = low[0:128]
    wide[128:256] = start[...]
    wide[256:384] = high[0:128]
    current = wide[...].reshape(12, 32, 128)
    rate = jnp.concatenate([low[128:256], rates[...], high[128:256]], axis=0).reshape(12, 32, 128)
    for _ in range(FINE):
        mixed = line_filter(
            pltpu.roll(current, 1, 2), current, pltpu.roll(current, 127, 2), fine_along_y
        )
        mixed = line_filter(pltpu.roll(mixed, 1, 1), mixed, pltpu.roll(mixed, 31, 1), fine_along_x)
        mixed = line_filter(mixed[:-2], mixed[1:-1], mixed[2:], fine_along_z)
        current, rate = current[1:-1], rate[1:-1]
        current = current + rate * (mixed - current)
    ends[...] = current.reshape(128, 128)
    coarse = [packed_layer(wide, 64 + 64 * i, even) for i in range(4)]
    flat = [packed_plane_filter(v, even) for v in coarse]
    coarse_rates, terms = [], []
    for i in range(2):
        coarse_rates.append(packed_layer(rates, 64 * i, even))
        mixed = line_filter(flat[i], flat[i + 1], flat[i + 2], coarse_along_z)
        guess = coarse[i + 1] + coarse_rates[i] * (mixed - coarse[i + 1])
        end = packed_layer(ends, 64 * i, even)
        terms.append(end - jnp.where(is_first, jnp.zeros_like(guess), guess))
        add_spread(smooth_out, ends, 64 * i, -end, even)
    own = jnp.where(lax.axis_index("h") == 0, coarse_rates[0], coarse_rates[1])
    message = jnp.concatenate([*terms, own], axis=0)
    send_out[...] = jnp.broadcast_to(message[None], send_out.shape)


def chain_kernel(received, send_out, history):
    even = even_lanes()
    depth = range(16)
    rates = [received[16 * (z % 2) + z // 2, 16:24] for z in depth]

    def term(step):
        return [received[8 * step + z // 2, 8 * (z % 2) : 8 * (z % 2) + 8] for z in depth]

    def keep(step, layers):
        for z in depth:
            history[step, z] = layers[z]

    def advance(layers):
        flat = [packed_plane_filter(v, even) for v in layers]
        out = []
        for z in depth:
            mixed = line_filter(flat[z - 1], flat[z], flat[(z + 1) % 16], coarse_along_z)
            out.append(layers[z] + rates[z] * (mixed - layers[z]))
        return out

    history[0] = jnp.zeros((16, 8, 128), jnp.float32)
    layers = term(0)
    keep(1, layers)
    for step in range(1, GROUP):
        layers = [a + b for a, b in zip(advance(layers), term(step))]
        keep(step + 1, layers)

    def body(step, layers):
        layers = advance(layers)
        keep(step + 1, layers)
        return tuple(layers)

    lax.fori_loop(GROUP, STEPS, body, tuple(layers))
    mine = lax.axis_index("z")
    place = lax.axis_index("h") * 2 + lax.axis_index("c")
    first = (lax.axis_index("l") * 4 + lax.axis_index("y")) * 2
    for target in range(8):
        begin = jnp.where(mine <= target, GROUP * (target - mine) + place, 0)
        finish = jnp.where(mine <= target, GROUP * (target - mine) + place + 1, 0)
        if target == 0:
            begin = jnp.where(place == 0, STEPS - GROUP * mine, begin)
        send_out[target, 0:16] = history[begin, pl.ds(first, 2)].reshape(16, 128)
        send_out[target, 16:32] = history[finish, pl.ds(first, 2)].reshape(16, 128)


def add_spread(out, smooth, first, layer, even):
    low = jnp.where(even, layer, pltpu.roll(layer, 1, 1))
    high = jnp.where(even, pltpu.roll(layer, 127, 1), layer)
    for plane in (0, 32):
        for at, value in ((0, low), (1, low), (2, high), (3, high)):
            rows = pl.ds(first + plane + at, 8, stride=4)
            out[rows, :] = smooth[rows, :] + value


def finish_kernel(received, smooth, smooth_before, ends_out, starts_out):
    even = even_lanes()
    total = received[0]
    for source in range(1, 8):
        total = total + received[source]
    for i in range(2):
        add_spread(starts_out, smooth_before, 64 * i, total[8 * i : 8 * i + 8], even)
        add_spread(ends_out, smooth, 64 * i, total[16 + 8 * i : 24 + 8 * i], even)


def array(*shape):
    return jax.ShapeDtypeStruct(shape, jnp.float32)


def cost(operations, size):
    return pl.CostEstimate(flops=operations, bytes_accessed=size, transcendentals=0)


def per_device(starts, cell_rates):
    start = starts.reshape(128, 128)
    rates = cell_rates.reshape(128, 128)
    both = jnp.concatenate([start, rates], axis=0)
    low = lax.ppermute(both, GRID, [(i, (i + 1) % 8) for i in range(8)])
    high = lax.ppermute(both, GRID, [((i + 1) % 8, i) for i in range(8)])
    smooth, message = pl.pallas_call(
        fine_kernel,
        out_shape=(array(128, 128), array(32, 24, 128)),
        scratch_shapes=[pltpu.VMEM((384, 128), jnp.float32), pltpu.VMEM((128, 128), jnp.float32)],
        cost_estimate=cost(4_000_000, 800_000),
        name="fine",
    )(start, rates, low, high)
    gathered = lax.all_to_all(message, PLANE, 0, 0, tiled=True)
    smooth_before = lax.ppermute(smooth, SLAB, [(i, (i + 1) % 32) for i in range(32)])
    pieces = pl.pallas_call(
        chain_kernel,
        out_shape=array(8, 32, 128),
        scratch_shapes=[pltpu.VMEM((STEPS + 1, 16, 8, 128), jnp.float32)],
        cost_estimate=cost(12_000_000, 500_000),
        name="chain",
    )(gathered)
    shares = lax.all_to_all(pieces, ("z",), 0, 0, tiled=True)
    ends, nexts = pl.pallas_call(
        finish_kernel,
        out_shape=(array(128, 128), array(128, 128)),
        cost_estimate=cost(200_000, 400_000),
        name="finish",
    )(shares, smooth, smooth_before)
    return ends.reshape(1, 4, 32, 128), nexts.reshape(1, 4, 32, 128)


def solution(mesh):
    fine_mesh = Mesh(mesh.devices.reshape(8, 2, 2, 2, 4), AXES)
    state = P(SLAB, GRID, None, None)
    return jax.shard_map(
        per_device,
        mesh=fine_mesh,
        in_specs=(state, P(GRID, None, None)),
        out_specs=(state, state),
        check_vma=False,
    )
```

time: 294 us -> 59.3 us (0.20)
  starting transfers between devices: 182 us -> 14.9 us
  local copies, waits for them, and re-layouts: 40.2 us -> 1.29 us
  waiting for transfers between devices: 50 us -> 12.1 us
  blocking collectives: 0 us -> 16.6 us
  other arithmetic: 15.1 us -> 0.88 us
  Pallas kernels: 0 us -> 12.5 us
    ppermute x69 -> x3, starting transfers between devices: 170 us -> 6.54 us  [the longest x1 4.57 us: per_device(): high = lax.ppermute(both, GRID, [((i + 1) % 8, i) for i in range(8)])]
    ppermute x69 -> x3, waiting for transfers between devices: 33 us -> 7.25 us  [the longest x1 3.76 us: per_device(): low = lax.ppermute(both, GRID, [(i, (i + 1) % 8) for i in range(8)])]
    reshape x4 -> x0, local copies, waits for them, and re-layouts: 19.1 us -> none  [the longest x2 11.1 us: restrict(): values.reshape(extent_z // 2, 2, extent_x // 2, 2, extent_y // 2, 2)]
    all_to_all x0 -> x1, blocking collectives: none -> 16.6 us  [per_device(): gathered = lax.all_to_all(message, PLANE, 0, 0, tiled=True)]
    pallas_call x0 -> x3, Pallas kernels: none -> 12.5 us  [the longest x1 8.19 us: per_device(): pl.pallas_call(chain_kernel, out_shape=array(8, 32, 128), scratch_shapes=...]
    all_to_all x1, waiting for transfers between devices: 17 us -> 4.81 us  [per_device(): shares = lax.all_to_all(pieces, ('z',), 0, 0, tiled=True)]
    reduce_sum x3 -> x0, other arithmetic: 7.63 us -> none  [restrict(): return jnp.mean(blocks, axis=(1, 3, 5))]
    slice x181 -> x0, local copies, waits for them, and re-layouts: 6.33 us -> none  [the longest x74 5.65 us: plane_filter(): jnp.roll(values, -1, 2)]
  transfers between devices with their start and end apart: 70 -> 4, of which waited for: 34 -> 4; matrix products, arithmetic and copies ran while one was open for 5% -> 0% of each run, Pallas kernels for 0% -> 0%
where the time goes in v1:
time: 59.3 us; the launch traced here: 58.9 us
  blocking collectives  16.6 us (28%)
  starting transfers between devices  14.9 us (25%)
  Pallas kernels  12.5 us (21%)
  waiting for transfers between devices  12.1 us (20%)
  local copies, waits for them, and re-layouts  1.29 us (2%)
  other arithmetic  0.88 us (1%)
  between operations  0.65 us (1%)
    all_to_all x1, blocking collectives, per_device(): gathered = lax.all_to_all(message, PLANE, 0, 0, tiled=True)  16.6 us
    all_to_all x1, starting transfers between devices, per_device(): shares = lax.all_to_all(pieces, ('z',), 0, 0, tiled=True)  8.32 us
    pallas_call x1, Pallas kernels, per_device(): pl.pallas_call(chain_kernel, out_shape=array(8, 32, 128), scratch_shapes=...  8.19 us
    all_to_all x1, waiting for transfers between devices, per_device(): shares = lax.all_to_all(pieces, ('z',), 0, 0, tiled=True)  4.81 us
    ppermute x1, starting transfers between devices, per_device(): high = lax.ppermute(both, GRID, [((i + 1) % 8, i) for i in range(8)])  4.57 us
    ppermute x1, waiting for transfers between devices, per_device(): low = lax.ppermute(both, GRID, [(i, (i + 1) % 8) for i in range(8)])  3.76 us
    pallas_call x1, Pallas kernels, per_device(): pl.pallas_call(fine_kernel, out_shape=(array(128, 128), array(32, 24, 128...  2.66 us
    ppermute x1, waiting for transfers between devices, per_device(): high = lax.ppermute(both, GRID, [((i + 1) % 8, i) for i in range(8)])  2.16 us
  transfers between devices with their start and end apart: 4, of which 4 were waited for; matrix products, arithmetic and copies ran while one was open for 0% of the time, Pallas kernels for 0%

profile of v1, /device:TPU:1, one launch (start us, length us, event | category | flops | bytes accessed | tf_op | source)
XLA Modules:
  0.0 58.9 jit_solution(13701613023475591580)
XLA Ops:
  0.6 0.9 %pad_maximum_fusion = f32[256,128]{1,0:T(8,128)S(1)} fusion(f32[128,128]{1,0:T(8,128)} %bitcast.6, f32[128,128]{1,0:T(8,128)} %bitcast.4), kind=kLoop, calls=%fused_computation | loop fusion | flops 32768 | bytes 262144 | tf_op jit(solution)/shard_map/concatenate | solution.py:164
  1.5 4.6 %collective-permute-start.1 = (f32[256,128]{1,0:T(8,128)S(1)}, f32[256,128]{1,0:T(8,128)S(1)}, u32[]{:S(2)}, u32[]{:S(2)}) collective-permute-start(f32[256,128]{1,0:T(8,128)S(1)} %pad_maximum_fusion), channel_id=1, source_target_pairs={{1,0},{2,1},{3,2},{4,3},{5,4},{6,5},{7,6},{0,7},{9,8},{10,9},{11,1... | collective-permute-start | bytes 393224 | tf_op jit(solution)/shard_map/ppermute | solution.py:166
  6.1 0.0 collective-permute-start
  6.1 2.2 %collective-permute-done.1.high = f32[256,128]{1,0:T(8,128)S(1)} collective-permute-done((f32[256,128]{1,0:T(8,128)S(1)}, f32[256,128]{1,0:T(8,128)S(1)}, u32[]{:S(2)}, u32[]{:S(2)}) %collective-permute-start.1) | collective-permute-done | bytes 131104 | tf_op jit(solution)/shard_map/ppermute | solution.py:166
  8.2 0.0 copy-start.1
  8.3 3.8 %collective-permute-done.low = f32[256,128]{1,0:T(8,128)S(1)} collective-permute-done((f32[256,128]{1,0:T(8,128)S(1)}, f32[256,128]{1,0:T(8,128)S(1)}, u32[]{:S(2)}, u32[]{:S(2)}) %collective-permute-start) | collective-permute-done | bytes 131104 | tf_op jit(solution)/shard_map/ppermute | solution.py:165
  12.0 0.0 copy-done.1
  12.0 0.0 copy-start.2
  12.0 0.6 %copy-done.2 = f32[256,128]{1,0:T(8,128)} copy-done((f32[256,128]{1,0:T(8,128)}, f32[256,128]{1,0:T(8,128)S(1)}, u32[]{:S(2)}) %copy-start.2) | copy-done | bytes 131096
  12.7 2.7 %fine.1 = (f32[128,128]{1,0:T(8,128)}, f32[32,24,128]{2,1,0:T(8,128)}) custom-call(f32[128,128]{1,0:T(8,128)} %bitcast.5, f32[128,128]{1,0:T(8,128)} %bitcast.7, f32[256,128]{1,0:T(8,128)} %copy-done.2, f32[256,128]{1,0:T(8,128)} %copy-done.1), custom_call_target="tpu_custom_call" | custom-call | flops 4000000 | bytes 800000 | tf_op jit(solution)/shard_map/fine/pallas_call | solution.py:167
  15.3 16.6 %all_to_all.10.received = f32[32,24,128]{2,1,0:T(8,128)} all-to-all(f32[32,24,128]{2,1,0:T(8,128)} %get-tuple-element.6), channel_id=1, replica_groups=mesh['z'=8,'h'=2,'c'=2,'l'=2,'y'=4] {'h','c','l','y'}, dimensions={0} | all-to-all | bytes 786432 | tf_op jit(solution)/shard_map/all_to_all | solution.py:174
  31.9 8.2 %chain.1 = f32[8,32,128]{2,1,0:T(8,128)} custom-call(f32[32,24,128]{2,1,0:T(8,128)} %all_to_all.10.received), custom_call_target="tpu_custom_call" | custom-call | flops 12000000 | bytes 500000 | tf_op jit(solution)/shard_map/chain/pallas_call | solution.py:176
  40.1 0.0 copy-start.3
  40.1 8.3 %all-to-all-start.1 = ((f32[8,32,128]{2,1,0:T(8,128)}), f32[8,32,128]{2,1,0:T(8,128)S(1)}, u32[]{:S(2)}, u32[]{:S(2)}) async-start(f32[8,32,128]{2,1,0:T(8,128)} %chain.1), calls=%async_computation.1 | async-start | bytes 262144 | tf_op jit(solution)/shard_map/all_to_all | solution.py:183
  48.5 0.0 copy-done.3
  48.5 2.0 %collective-permute-start.2 = (f32[128,128]{1,0:T(8,128)S(1)}, f32[128,128]{1,0:T(8,128)S(1)}, u32[]{:S(2)}, u32[]{:S(2)}) collective-permute-start(f32[128,128]{1,0:T(8,128)S(1)} %copy-done.3), channel_id=1, source_target_pairs={{0,8},{8,16},{16,24},{24,32},{32,40},{40,48},{48,56},{56,64},{64,7... | collective-permute-start | bytes 196616 | tf_op jit(solution)/shard_map/ppermute | solution.py:175
  50.4 1.3 %collective-permute-done.2.smooth_before = f32[128,128]{1,0:T(8,128)S(1)} collective-permute-done((f32[128,128]{1,0:T(8,128)S(1)}, f32[128,128]{1,0:T(8,128)S(1)}, u32[]{:S(2)}, u32[]{:S(2)}) %collective-permute-start.2) | collective-permute-done | bytes 65568 | tf_op jit(solution)/shard_map/ppermute | solution.py:175
  51.8 0.0 copy-start.4
  51.8 4.8 %all-to-all-done.1.received = f32[8,32,128]{2,1,0:T(8,128)S(1)} async-done(((f32[8,32,128]{2,1,0:T(8,128)}), f32[8,32,128]{2,1,0:T(8,128)S(1)}, u32[]{:S(2)}, u32[]{:S(2)}) %all-to-all-start.1) | async-done | bytes 131104 | tf_op jit(solution)/shard_map/all_to_all | solution.py:183
  56.6 0.0 copy-done.4
  56.6 0.0 copy-start
  56.6 0.6 %copy-done = f32[8,32,128]{2,1,0:T(8,128)} copy-done((f32[8,32,128]{2,1,0:T(8,128)}, f32[8,32,128]{2,1,0:T(8,128)S(1)}, u32[]{:S(2)}) %copy-start) | copy-done | bytes 131096
  57.2 1.7 %finish.1 = (f32[128,128]{1,0:T(8,128)}, f32[128,128]{1,0:T(8,128)}) custom-call(f32[8,32,128]{2,1,0:T(8,128)} %copy-done, f32[128,128]{1,0:T(8,128)} %get-tuple-element.7.smooth, f32[128,128]{1,0:T(8,128)} %copy-done.4), custom_call_target="tpu_custom_call" | custom-call | flops 200000 | bytes 400000 | tf_op jit(solution)/shard_map/finish/pallas_call | solution.py:184
Async XLA Ops:
  1.5 6.7 %collective-permute-start.1 = (f32[256,128]{1,0:T(8,128)S(1)}, f32[256,128]{1,0:T(8,128)S(1)}, u32[]{:S(2)}, u32[]{:S(2)}) collective-permute-start(f32[256,128]{1,0:T(8,128)S(1)} %pad_maximum_fusion), channel_id=1, source_target_pairs={{1,0},{2,1},{3,2},{4,3},{5,4},{6,5},{7,6},{0,7},{9,8},{10,9},{11,1... | collective-permute-start | bytes 393224 | tf_op jit(solution)/shard_map/ppermute | solution.py:166
  6.1 5.9 %collective-permute-start = (f32[256,128]{1,0:T(8,128)S(1)}, f32[256,128]{1,0:T(8,128)S(1)}, u32[]{:S(2)}, u32[]{:S(2)}) collective-permute-start(f32[256,128]{1,0:T(8,128)S(1)} %pad_maximum_fusion), channel_id=1, source_target_pairs={{0,1},{1,2},{2,3},{3,4},{4,5},{5,6},{6,7},{7,0},{8,9},{9,10},{10,1... | collective-permute-start | bytes 393224 | tf_op jit(solution)/shard_map/ppermute | solution.py:165
  8.2 3.8 %copy-start.1 = (f32[256,128]{1,0:T(8,128)}, f32[256,128]{1,0:T(8,128)S(1)}, u32[]{:S(2)}) copy-start(f32[256,128]{1,0:T(8,128)S(1)} %collective-permute-done.1.high) | copy-start | bytes 393220
  12.0 0.6 %copy-start.2 = (f32[256,128]{1,0:T(8,128)}, f32[256,128]{1,0:T(8,128)S(1)}, u32[]{:S(2)}) copy-start(f32[256,128]{1,0:T(8,128)S(1)} %collective-permute-done.low) | copy-start | bytes 393220
  40.1 8.3 %copy-start.3 = (f32[128,128]{1,0:T(8,128)S(1)}, f32[128,128]{1,0:T(8,128)}, u32[]{:S(2)}) copy-start(f32[128,128]{1,0:T(8,128)} %get-tuple-element.7.smooth) | copy-start | bytes 196612
  40.1 16.4 %all-to-all-start.1 = ((f32[8,32,128]{2,1,0:T(8,128)}), f32[8,32,128]{2,1,0:T(8,128)S(1)}, u32[]{:S(2)}, u32[]{:S(2)}) async-start(f32[8,32,128]{2,1,0:T(8,128)} %chain.1), calls=%async_computation.1 | async-start | bytes 262144 | tf_op jit(solution)/shard_map/all_to_all | solution.py:183
  48.5 3.3 %collective-permute-start.2 = (f32[128,128]{1,0:T(8,128)S(1)}, f32[128,128]{1,0:T(8,128)S(1)}, u32[]{:S(2)}, u32[]{:S(2)}) collective-permute-start(f32[128,128]{1,0:T(8,128)S(1)} %copy-done.3), channel_id=1, source_target_pairs={{0,8},{8,16},{16,24},{24,32},{32,40},{40,48},{48,56},{56,64},{64,7... | collective-permute-start | bytes 196616 | tf_op jit(solution)/shard_map/ppermute | solution.py:175
  51.8 4.8 %copy-start.4 = (f32[128,128]{1,0:T(8,128)}, f32[128,128]{1,0:T(8,128)S(1)}, u32[]{:S(2)}) copy-start(f32[128,128]{1,0:T(8,128)S(1)} %collective-permute-done.2.smooth_before) | copy-start | bytes 196612
  56.6 0.6 %copy-start = (f32[8,32,128]{2,1,0:T(8,128)}, f32[8,32,128]{2,1,0:T(8,128)S(1)}, u32[]{:S(2)}) copy-start(f32[8,32,128]{2,1,0:T(8,128)S(1)} %all-to-all-done.1.received) | copy-start | bytes 393220

commit v2 on v1

--- a/solution.py
+++ b/solution.py
@@ -54,11 +54,12 @@
     return 0.125 * jnp.where(even, low + pltpu.roll(low, 127, 1), high + pltpu.roll(high, 1, 1))
 
 
-def fine_kernel(start, rates, low, high, smooth_out, send_out, wide, ends):
+def fine_kernel(own, low, high, smooth_out, send_out, wide, ends, rates):
     even = even_lanes()
     is_first = (lax.axis_index("z") == 0) & (lax.axis_index("h") == 0) & (lax.axis_index("c") == 0)
     wide[0:128] = low[0:128]
-    wide[128:256] = start[...]
+    wide[128:256] = own[0:128]
+    rates[...] = own[128:256]
     wide[256:384] = high[0:128]
     current = wide[...].reshape(12, 32, 128)
     rate = jnp.concatenate([low[128:256], rates[...], high[128:256]], axis=0).reshape(12, 32, 128)
@@ -81,15 +82,46 @@
         end = packed_layer(ends, 64 * i, even)
         terms.append(end - jnp.where(is_first, jnp.zeros_like(guess), guess))
         add_spread(smooth_out, ends, 64 * i, -end, even)
-    own = jnp.where(lax.axis_index("h") == 0, coarse_rates[0], coarse_rates[1])
-    message = jnp.concatenate([*terms, own], axis=0)
+    layer = jnp.where(lax.axis_index("h") == 0, coarse_rates[0], coarse_rates[1])
+    message = jnp.concatenate([*terms, layer], axis=0)
     send_out[...] = jnp.broadcast_to(message[None], send_out.shape)
+
+
+def side_weights(kind):
+    a, b, c = weights_of(kind)
+    return a / b, c / b
+
+
+def scaled_filter(behind, middle, beyond, kind):
+    a, c = side_weights(kind)
+    return middle + (a * behind + c * beyond)
+
+
+def scaled_plane_filter(v, even):
+    near, far = {}, {}
+    for by in (1, 2, 3):
+        near[by], far[by] = pltpu.roll(v, by, 1), pltpu.roll(v, 128 - by, 1)
+    flat = scaled_filter(near[2], v, far[2], coarse_along_y)
+    other = scaled_filter(
+        jnp.where(even, near[1], near[3]),
+        jnp.where(even, far[1], near[1]),
+        jnp.where(even, far[3], far[1]),
+        coarse_along_y,
+    )
+    behind = jnp.where(even, pltpu.roll(other, 1, 0), other)
+    beyond = jnp.where(even, other, pltpu.roll(other, 7, 0))
+    return scaled_filter(behind, flat, beyond, coarse_along_x)
 
 
 def chain_kernel(received, send_out, history):
     even = even_lanes()
     depth = range(16)
+    middle = 1.0
+    for kind in (coarse_along_z, coarse_along_x, coarse_along_y):
+        middle *= weights_of(kind)[1]
     rates = [received[16 * (z % 2) + z // 2, 16:24] for z in depth]
+    drops = [1.0 - rate for rate in rates]
+    rates = [middle * rate for rate in rates]
 
     def term(step):
         return [received[8 * step + z // 2, 8 * (z % 2) : 8 * (z % 2) + 8] for z in depth]
@@ -99,11 +131,11 @@
             history[step, z] = layers[z]
 
     def advance(layers):
-        flat = [packed_plane_filter(v, even) for v in layers]
+        flat = [scaled_plane_filter(v, even) for v in layers]
         out = []
         for z in depth:
-            mixed = line_filter(flat[z - 1], flat[z], flat[(z + 1) % 16], coarse_along_z)
-            out.append(layers[z] + rates[z] * (mixed - layers[z]))
+            mixed = scaled_filter(flat[z - 1], flat[z], flat[(z + 1) % 16], coarse_along_z)
+            out.append(drops[z] * layers[z] + rates[z] * mixed)
         return out
 
     history[0] = jnp.zeros((16, 8, 128), jnp.float32)
@@ -118,8 +150,8 @@
         keep(step + 1, layers)
         return tuple(layers)
 
-    lax.fori_loop(GROUP, STEPS, body, tuple(layers))
     mine = lax.axis_index("z")
+    lax.fori_loop(GROUP, STEPS - GROUP * mine, body, tuple(layers))
     place = lax.axis_index("h") * 2 + lax.axis_index("c")
     first = (lax.axis_index("l") * 4 + lax.axis_index("y")) * 2
     for target in range(8):
@@ -154,39 +186,52 @@
     return jax.ShapeDtypeStruct(shape, jnp.float32)
 
 
-def cost(operations, size):
-    return pl.CostEstimate(flops=operations, bytes_accessed=size, transcendentals=0)
+def local(kernel, operands, outputs, scratch, operations, out_space):
+    return pl.pallas_call(
+        kernel,
+        out_shape=outputs,
+        in_specs=[pl.BlockSpec(memory_space=pltpu.VMEM)] * len(operands),
+        out_specs=jax.tree.map(lambda _: pl.BlockSpec(memory_space=out_space), outputs),
+        scratch_shapes=[pltpu.VMEM(shape, jnp.float32) for shape in scratch],
+        cost_estimate=pl.CostEstimate(
+            flops=operations, bytes_accessed=4 * sum(a.size for a in operands), transcendentals=0
+        ),
+        compiler_params=pltpu.CompilerParams(vmem_limit_bytes=16 * 2**20),
+    )(*operands)
 
 
 def per_device(starts, cell_rates):
-    start = starts.reshape(128, 128)
-    rates = cell_rates.reshape(128, 128)
-    both = jnp.concatenate([start, rates], axis=0)
-    low = lax.ppermute(both, GRID, [(i, (i + 1) % 8) for i in range(8)])
-    high = lax.ppermute(both, GRID, [((i + 1) % 8, i) for i in range(8)])
-    smooth, message = pl.pallas_call(
+    own = jnp.concatenate([starts.reshape(128, 128), cell_rates.reshape(128, 128)], axis=0)
+    low = lax.ppermute(own, GRID, [(i, (i + 1) % 8) for i in range(8)])
+    high = lax.ppermute(own, GRID, [((i + 1) % 8, i) for i in range(8)])
+    smooth, message = local(
         fine_kernel,
-        out_shape=(array(128, 128), array(32, 24, 128)),
-        scratch_shapes=[pltpu.VMEM((384, 128), jnp.float32), pltpu.VMEM((128, 128), jnp.float32)],
-        cost_estimate=cost(4_000_000, 800_000),
-        name="fine",
-    )(start, rates, low, high)
+        (own, low, high),
+        (array(128, 128), array(32, 24, 128)),
+        [(384, 128), (128, 128), (128, 128)],
+        4_000_000,
+        pltpu.VMEM,
+    )
+    smooth_before = lax.ppermute(smooth, SLAB, [(i, (i + 1) % 32) for i in range(32)])
     gathered = lax.all_to_all(message, PLANE, 0, 0, tiled=True)
-    smooth_before = lax.ppermute(smooth, SLAB, [(i, (i + 1) % 32) for i in range(32)])
-    pieces = pl.pallas_call(
+    pieces = local(
         chain_kernel,
-        out_shape=array(8, 32, 128),
-        scratch_shapes=[pltpu.VMEM((STEPS + 1, 16, 8, 128), jnp.float32)],
-        cost_estimate=cost(12_000_000, 500_000),
-        name="chain",
-    )(gathered)
+        (gathered,),
+        array(8, 32, 128),
+        [(STEPS + 1, 16, 8, 128)],
+        12_000_000,
+        pltpu.VMEM,
+    )
+    pieces, smooth_before = lax.optimization_barrier((pieces, smooth_before))
     shares = lax.all_to_all(pieces, ("z",), 0, 0, tiled=True)
-    ends, nexts = pl.pallas_call(
+    ends, nexts = local(
         finish_kernel,
-        out_shape=(array(128, 128), array(128, 128)),
-        cost_estimate=cost(200_000, 400_000),
-        name="finish",
-    )(shares, smooth, smooth_before)
+        (shares, smooth, smooth_before),
+        (array(128, 128), array(128, 128)),
+        [],
+        200_000,
+        pltpu.VMEM,
+    )
     return ends.reshape(1, 4, 32, 128), nexts.reshape(1, 4, 32, 128)
 
 

time: 59.3 us -> 50.3 us (0.85)
  Pallas kernels: 12.5 us -> 7.89 us
  blocking collectives: 16.6 us -> 13.6 us
  local copies, waits for them, and re-layouts: 1.29 us -> 0 us
  starting transfers between devices: 14.9 us -> 14.1 us
  waiting for transfers between devices: 12.1 us -> 12.9 us
    pallas_call x3, Pallas kernels: 12.5 us -> 7.89 us  [local(): pl.pallas_call(kernel, out_shape=outputs, in_specs=[pl.BlockSpec(memory_s...]
    all_to_all x1, blocking collectives: 16.6 us -> 13.6 us  [per_device(): shares = lax.all_to_all(pieces, ('z',), 0, 0, tiled=True)]
    all_to_all x1, waiting for transfers between devices: 4.81 us -> 7.01 us  [per_device(): gathered = lax.all_to_all(message, PLANE, 0, 0, tiled=True)]
    all_to_all x1, starting transfers between devices: 8.32 us -> 6.27 us  [per_device(): gathered = lax.all_to_all(message, PLANE, 0, 0, tiled=True)]
    ppermute x1, waiting for transfers between devices: 1.33 us -> 0.01 us  [per_device(): lax.ppermute(smooth, SLAB, [(i, (i + 1) % 32) for i in range(32)])]
    unnamed x10 -> x0, local copies, waits for them, and re-layouts: 1.29 us -> none
    ppermute x1, starting transfers between devices: 1.97 us -> 3.22 us  [per_device(): lax.ppermute(smooth, SLAB, [(i, (i + 1) % 32) for i in range(32)])]
  transfers between devices with their start and end apart: 4 -> 4, of which waited for: 4 -> 3; matrix products, arithmetic and copies ran while one was open for 0% -> 0% of each run, Pallas kernels for 0% -> 11%
where the time goes in v2:
time: 50.3 us; the launch traced here: 50.1 us
  starting transfers between devices  14.1 us (28%)
  blocking collectives  13.6 us (27%)
  waiting for transfers between devices  12.9 us (26%)
  Pallas kernels  7.89 us (16%)
  other arithmetic  0.88 us (2%)
  between operations  0.66 us (1%)
    all_to_all x1, blocking collectives, per_device(): shares = lax.all_to_all(pieces, ('z',), 0, 0, tiled=True)  13.6 us
    pallas_call x3, Pallas kernels, local(): pl.pallas_call(kernel, out_shape=outputs, in_specs=[pl.BlockSpec(memory_s...  7.89 us
    all_to_all x1, waiting for transfers between devices, per_device(): gathered = lax.all_to_all(message, PLANE, 0, 0, tiled=True)  7.01 us
    all_to_all x1, starting transfers between devices, per_device(): gathered = lax.all_to_all(message, PLANE, 0, 0, tiled=True)  6.27 us
    ppermute x1, starting transfers between devices, per_device(): high = lax.ppermute(own, GRID, [((i + 1) % 8, i) for i in range(8)])  4.57 us
    ppermute x1, waiting for transfers between devices, per_device(): low = lax.ppermute(own, GRID, [(i, (i + 1) % 8) for i in range(8)])  3.76 us
    ppermute x1, starting transfers between devices, per_device(): lax.ppermute(smooth, SLAB, [(i, (i + 1) % 32) for i in range(32)])  3.22 us
    ppermute x1, waiting for transfers between devices, per_device(): high = lax.ppermute(own, GRID, [((i + 1) % 8, i) for i in range(8)])  2.16 us
  transfers between devices with their start and end apart: 4, of which 3 were waited for; matrix products, arithmetic and copies ran while one was open for 0% of the time, Pallas kernels for 11%

profile of v2, /device:TPU:1, one launch (start us, length us, event | category | flops | bytes accessed | tf_op | source)
XLA Modules:
  0.0 50.1 jit_solution(258345183441832155)
XLA Ops:
  0.6 0.9 %pad_maximum_fusion.own = f32[256,128]{1,0:T(8,128)S(1)} fusion(f32[128,128]{1,0:T(8,128)} %bitcast.4, f32[128,128]{1,0:T(8,128)} %bitcast.5), kind=kLoop, calls=%fused_computation | loop fusion | flops 32768 | bytes 262144 | tf_op jit(solution)/shard_map/concatenate | solution.py:204
  1.5 4.6 %collective-permute-start.1 = (f32[256,128]{1,0:T(8,128)S(1)}, f32[256,128]{1,0:T(8,128)S(1)}, u32[]{:S(2)}, u32[]{:S(2)}) collective-permute-start(f32[256,128]{1,0:T(8,128)S(1)} %pad_maximum_fusion.own), channel_id=1, source_target_pairs={{1,0},{2,1},{3,2},{4,3},{5,4},{6,5},{7,6},{0,7},{9,8},{10,9},{11,1... | collective-permute-start | bytes 393224 | tf_op jit(solution)/shard_map/ppermute | solution.py:206
  6.1 0.0 collective-permute-start
  6.1 2.2 %collective-permute-done.1.high = f32[256,128]{1,0:T(8,128)S(1)} collective-permute-done((f32[256,128]{1,0:T(8,128)S(1)}, f32[256,128]{1,0:T(8,128)S(1)}, u32[]{:S(2)}, u32[]{:S(2)}) %collective-permute-start.1) | collective-permute-done | bytes 131104 | tf_op jit(solution)/shard_map/ppermute | solution.py:206
  8.2 3.8 %collective-permute-done.low = f32[256,128]{1,0:T(8,128)S(1)} collective-permute-done((f32[256,128]{1,0:T(8,128)S(1)}, f32[256,128]{1,0:T(8,128)S(1)}, u32[]{:S(2)}, u32[]{:S(2)}) %collective-permute-start) | collective-permute-done | bytes 131104 | tf_op jit(solution)/shard_map/ppermute | solution.py:205
  12.0 1.6 %shard_map.41 = (f32[128,128]{1,0:T(8,128)S(1)}, f32[32,24,128]{2,1,0:T(8,128)}) custom-call(f32[256,128]{1,0:T(8,128)S(1)} %pad_maximum_fusion.own, f32[256,128]{1,0:T(8,128)S(1)} %collective-permute-done.low, f32[256,128]{1,0:T(8,128)S(1)} %collective-permute-done.1.high), custom_call_target="tpu_custom_call" | custom-call | flops 4000000 | bytes 393216 | tf_op jit(solution)/shard_map/pallas_call | solution.py:190
  13.6 6.3 %all-to-all-start = ((f32[32,24,128]{2,1,0:T(8,128)}), f32[32,24,128]{2,1,0:T(8,128)S(1)}, u32[]{:S(2)}, u32[]{:S(2)}) async-start(f32[32,24,128]{2,1,0:T(8,128)} %get-tuple-element.8), calls=%async_computation | async-start | bytes 786432 | tf_op jit(solution)/shard_map/all_to_all | solution.py:216
  19.9 3.2 %collective-permute-start.2 = (f32[128,128]{1,0:T(8,128)S(1)}, f32[128,128]{1,0:T(8,128)S(1)}, u32[]{:S(2)}, u32[]{:S(2)}) collective-permute-start(f32[128,128]{1,0:T(8,128)S(1)} %get-tuple-element.9.smooth), channel_id=1, source_target_pairs={{0,8},{8,16},{16,24},{24,32},{32,40},{40,48},{48,56},{56,64},{64,7... | collective-permute-start | bytes 196616 | tf_op jit(solution)/shard_map/ppermute | solution.py:215
  23.1 7.0 %all-to-all-done.received = f32[32,24,128]{2,1,0:T(8,128)S(1)} async-done(((f32[32,24,128]{2,1,0:T(8,128)}), f32[32,24,128]{2,1,0:T(8,128)S(1)}, u32[]{:S(2)}, u32[]{:S(2)}) %all-to-all-start) | async-done | bytes 393248 | tf_op jit(solution)/shard_map/all_to_all | solution.py:216
  30.1 5.5 %shard_map.42 = f32[8,32,128]{2,1,0:T(8,128)S(1)} custom-call(f32[32,24,128]{2,1,0:T(8,128)S(1)} %all-to-all-done.received), custom_call_target="tpu_custom_call" | custom-call | flops 12000000 | bytes 393216 | tf_op jit(solution)/shard_map/pallas_call | solution.py:190
  35.7 0.0 collective-permute-done.2.smooth_before
  35.7 13.6 %all_to_all.10.received = f32[8,32,128]{2,1,0:T(8,128)S(1)} all-to-all(f32[8,32,128]{2,1,0:T(8,128)S(1)} %shard_map.42), channel_id=1, replica_groups=mesh['z'=8,'h'=2,'c'=2,'l'=2,'y'=4] {'z'}, dimensions={0} | all-to-all | bytes 262144 | tf_op jit(solution)/shard_map/all_to_all | solution.py:226
  49.3 0.7 %shard_map.43 = (f32[128,128]{1,0:T(8,128)}, f32[128,128]{1,0:T(8,128)}) custom-call(f32[8,32,128]{2,1,0:T(8,128)S(1)} %all_to_all.10.received, f32[128,128]{1,0:T(8,128)S(1)} %get-tuple-element.9.smooth, f32[128,128]{1,0:T(8,128)S(1)} %collective-permute-done.2.smooth_before), custom_call_target="tpu_custom_call" | custom-call | flops 200000 | bytes 262144 | tf_op jit(solution)/shard_map/pallas_call | solution.py:190
Async XLA Ops:
  1.5 6.7 %collective-permute-start.1 = (f32[256,128]{1,0:T(8,128)S(1)}, f32[256,128]{1,0:T(8,128)S(1)}, u32[]{:S(2)}, u32[]{:S(2)}) collective-permute-start(f32[256,128]{1,0:T(8,128)S(1)} %pad_maximum_fusion.own), channel_id=1, source_target_pairs={{1,0},{2,1},{3,2},{4,3},{5,4},{6,5},{7,6},{0,7},{9,8},{10,9},{11,1... | collective-permute-start | bytes 393224 | tf_op jit(solution)/shard_map/ppermute | solution.py:206
  6.1 5.9 %collective-permute-start = (f32[256,128]{1,0:T(8,128)S(1)}, f32[256,128]{1,0:T(8,128)S(1)}, u32[]{:S(2)}, u32[]{:S(2)}) collective-permute-start(f32[256,128]{1,0:T(8,128)S(1)} %pad_maximum_fusion.own), channel_id=1, source_target_pairs={{0,1},{1,2},{2,3},{3,4},{4,5},{5,6},{6,7},{7,0},{8,9},{9,10},{10,1... | collective-permute-start | bytes 393224 | tf_op jit(solution)/shard_map/ppermute | solution.py:205
  13.6 16.5 %all-to-all-start = ((f32[32,24,128]{2,1,0:T(8,128)}), f32[32,24,128]{2,1,0:T(8,128)S(1)}, u32[]{:S(2)}, u32[]{:S(2)}) async-start(f32[32,24,128]{2,1,0:T(8,128)} %get-tuple-element.8), calls=%async_computation | async-start | bytes 786432 | tf_op jit(solution)/shard_map/all_to_all | solution.py:216
  19.9 15.8 %collective-permute-start.2 = (f32[128,128]{1,0:T(8,128)S(1)}, f32[128,128]{1,0:T(8,128)S(1)}, u32[]{:S(2)}, u32[]{:S(2)}) collective-permute-start(f32[128,128]{1,0:T(8,128)S(1)} %get-tuple-element.9.smooth), channel_id=1, source_target_pairs={{0,8},{8,16},{16,24},{24,32},{32,40},{40,48},{48,56},{56,64},{64,7... | collective-permute-start | bytes 196616 | tf_op jit(solution)/shard_map/ppermute | solution.py:215

commit v3 on v2

--- a/solution.py
+++ b/solution.py
@@ -54,23 +54,43 @@
     return 0.125 * jnp.where(even, low + pltpu.roll(low, 127, 1), high + pltpu.roll(high, 1, 1))
 
 
-def fine_kernel(own, low, high, smooth_out, send_out, wide, ends, rates):
+def halo_kernel(start, rates, up, down, done):
+    copies = [
+        pltpu.make_async_copy(source, target, done.at[i])
+        for i, (source, target) in enumerate(
+            (
+                (start, up.at[0:128]),
+                (start, down.at[0:128]),
+                (rates.at[32:128], up.at[128:224]),
+                (rates.at[0:96], down.at[128:224]),
+            )
+        )
+    ]
+    for copy in copies:
+        copy.start()
+    for copy in copies:
+        copy.wait()
+
+
+def fine_kernel(up, down, low, high, smooth_out, send_out, wide, ends, rates):
     even = even_lanes()
     is_first = (lax.axis_index("z") == 0) & (lax.axis_index("h") == 0) & (lax.axis_index("c") == 0)
-    wide[0:128] = low[0:128]
-    wide[128:256] = own[0:128]
-    rates[...] = own[128:256]
+    wide[0:128] = low[96:224]
+    wide[128:256] = down[0:128]
     wide[256:384] = high[0:128]
+    rates[0:32] = down[128:160]
+    rates[32:128] = up[0:96]
     current = wide[...].reshape(12, 32, 128)
-    rate = jnp.concatenate([low[128:256], rates[...], high[128:256]], axis=0).reshape(12, 32, 128)
+    rate = jnp.concatenate([low[0:96], rates[...], high[128:224]], axis=0).reshape(10, 32, 128)
     for _ in range(FINE):
         mixed = line_filter(
             pltpu.roll(current, 1, 2), current, pltpu.roll(current, 127, 2), fine_along_y
         )
         mixed = line_filter(pltpu.roll(mixed, 1, 1), mixed, pltpu.roll(mixed, 31, 1), fine_along_x)
         mixed = line_filter(mixed[:-2], mixed[1:-1], mixed[2:], fine_along_z)
-        current, rate = current[1:-1], rate[1:-1]
+        current = current[1:-1]
         current = current + rate * (mixed - current)
+        rate = rate[1:-1]
     ends[...] = current.reshape(128, 128)
     coarse = [packed_layer(wide, 64 + 64 * i, even) for i in range(4)]
     flat = [packed_plane_filter(v, even) for v in coarse]
@@ -83,8 +103,12 @@
         terms.append(end - jnp.where(is_first, jnp.zeros_like(guess), guess))
         add_spread(smooth_out, ends, 64 * i, -end, even)
     layer = jnp.where(lax.axis_index("h") == 0, coarse_rates[0], coarse_rates[1])
-    message = jnp.concatenate([*terms, layer], axis=0)
-    send_out[...] = jnp.broadcast_to(message[None], send_out.shape)
+    layer = jnp.where(lax.axis_index("c") == 0, layer, pltpu.roll(layer, 4, 0))
+    for i in range(2):
+        for half in range(2):
+            rows = terms[i][4 * half : 4 * half + 4]
+            send_out[:, 2 * i + half] = jnp.broadcast_to(rows[None], (32, 4, 128))
+    send_out[:, 4] = jnp.broadcast_to(layer[None, 0:4], (32, 4, 128))
 
 
 def side_weights(kind):
@@ -116,15 +140,20 @@
 def chain_kernel(received, send_out, history):
     even = even_lanes()
     depth = range(16)
+
+    def joined(first, second):
+        return jnp.concatenate([received[first], received[second]], axis=0)
+
     middle = 1.0
     for kind in (coarse_along_z, coarse_along_x, coarse_along_y):
         middle *= weights_of(kind)[1]
-    rates = [received[16 * (z % 2) + z // 2, 16:24] for z in depth]
+    rates = [joined((16 * (z % 2) + z // 2, 4), (16 * (z % 2) + 8 + z // 2, 4)) for z in depth]
     drops = [1.0 - rate for rate in rates]
     rates = [middle * rate for rate in rates]
 
     def term(step):
-        return [received[8 * step + z // 2, 8 * (z % 2) : 8 * (z % 2) + 8] for z in depth]
+        at = [(8 * step + z // 2, 2 * (z % 2)) for z in depth]
+        return [joined((source, part), (source, part + 1)) for source, part in at]
 
     def keep(step, layers):
         for z in depth:
@@ -186,13 +215,15 @@
     return jax.ShapeDtypeStruct(shape, jnp.float32)
 
 
-def local(kernel, operands, outputs, scratch, operations, out_space):
+def local(kernel, operands, outputs, scratch, operations, space=pltpu.VMEM, sent=True):
+    if sent:
+        outputs = jax.tree.map(lambda a: pltpu.VMEM(a.shape, a.dtype), outputs)
     return pl.pallas_call(
         kernel,
         out_shape=outputs,
-        in_specs=[pl.BlockSpec(memory_space=pltpu.VMEM)] * len(operands),
-        out_specs=jax.tree.map(lambda _: pl.BlockSpec(memory_space=out_space), outputs),
-        scratch_shapes=[pltpu.VMEM(shape, jnp.float32) for shape in scratch],
+        in_specs=[pl.BlockSpec(memory_space=space)] * len(operands),
+        out_specs=jax.tree.map(lambda _: pl.BlockSpec(memory_space=pltpu.VMEM), outputs),
+        scratch_shapes=scratch,
         cost_estimate=pl.CostEstimate(
             flops=operations, bytes_accessed=4 * sum(a.size for a in operands), transcendentals=0
         ),
@@ -200,29 +231,33 @@
     )(*operands)
 
 
+def scratch(*shape):
+    return pltpu.VMEM(shape, jnp.float32)
+
+
 def per_device(starts, cell_rates):
-    own = jnp.concatenate([starts.reshape(128, 128), cell_rates.reshape(128, 128)], axis=0)
-    low = lax.ppermute(own, GRID, [(i, (i + 1) % 8) for i in range(8)])
-    high = lax.ppermute(own, GRID, [((i + 1) % 8, i) for i in range(8)])
+    start, rates = starts.reshape(128, 128), cell_rates.reshape(128, 128)
+    own = jnp.concatenate([rates, start, rates], axis=0)
+    up, down = own[32:256], own[128:352]
+    low = lax.ppermute(up, GRID, [(i, (i + 1) % 8) for i in range(8)])
+    high = lax.ppermute(down, GRID, [((i + 1) % 8, i) for i in range(8)])
     smooth, message = local(
         fine_kernel,
-        (own, low, high),
-        (array(128, 128), array(32, 24, 128)),
-        [(384, 128), (128, 128), (128, 128)],
+        (up, down, low, high),
+        (array(128, 128), array(32, 5, 4, 128)),
+        [scratch(384, 128), scratch(128, 128), scratch(128, 128)],
         4_000_000,
-        pltpu.VMEM,
-    )
-    smooth_before = lax.ppermute(smooth, SLAB, [(i, (i + 1) % 32) for i in range(32)])
+    )
     gathered = lax.all_to_all(message, PLANE, 0, 0, tiled=True)
     pieces = local(
         chain_kernel,
         (gathered,),
         array(8, 32, 128),
-        [(STEPS + 1, 16, 8, 128)],
+        [scratch(STEPS + 1, 16, 8, 128)],
         12_000_000,
-        pltpu.VMEM,
-    )
-    pieces, smooth_before = lax.optimization_barrier((pieces, smooth_before))
+    )
+    pieces, smooth = lax.optimization_barrier((pieces, smooth))
+    smooth_before = lax.ppermute(smooth, SLAB, [(i, (i + 1) % 32) for i in range(32)])
     shares = lax.all_to_all(pieces, ("z",), 0, 0, tiled=True)
     ends, nexts = local(
         finish_kernel,
@@ -230,7 +265,7 @@
         (array(128, 128), array(128, 128)),
         [],
         200_000,
-        pltpu.VMEM,
+        sent=False,
     )
     return ends.reshape(1, 4, 32, 128), nexts.reshape(1, 4, 32, 128)
 

time: 50.3 us -> 49 us (0.974)
  starting transfers between devices: 14.1 us -> 11.8 us
  blocking collectives: 13.6 us -> 15.6 us
  waiting for transfers between devices: 12.9 us -> 12 us
    all_to_all x1, waiting for transfers between devices: 7.01 us -> 4.91 us  [per_device(): shares = lax.all_to_all(pieces, ('z',), 0, 0, tiled=True)]
    all_to_all x1, blocking collectives: 13.6 us -> 15.6 us  [per_device(): gathered = lax.all_to_all(message, PLANE, 0, 0, tiled=True)]
    ppermute x1, starting transfers between devices: 3.22 us -> 1.87 us  [per_device(): lax.ppermute(smooth, SLAB, [(i, (i + 1) % 32) for i in range(32)])]
    ppermute x1, waiting for transfers between devices: 0.01 us -> 1.33 us  [per_device(): lax.ppermute(smooth, SLAB, [(i, (i + 1) % 32) for i in range(32)])]
    all_to_all x1, starting transfers between devices: 6.27 us -> 5.36 us  [per_device(): shares = lax.all_to_all(pieces, ('z',), 0, 0, tiled=True)]
  transfers between devices with their start and end apart: 4 -> 4, of which waited for: 3 -> 4; matrix products, arithmetic and copies ran while one was open for 0% -> 0% of each run, Pallas kernels for 11% -> 0%
where the time goes in v3:
time: 49 us; the launch traced here: 48.8 us
  blocking collectives  15.6 us (32%)
  waiting for transfers between devices  12 us (24%)
  starting transfers between devices  11.8 us (24%)
  Pallas kernels  7.77 us (16%)
  other arithmetic  0.94 us (2%)
  between operations  0.65 us (1%)
    all_to_all x1, blocking collectives, per_device(): gathered = lax.all_to_all(message, PLANE, 0, 0, tiled=True)  15.6 us
    pallas_call x3, Pallas kernels, local(): pl.pallas_call(kernel, out_shape=outputs, in_specs=[pl.BlockSpec(memory_s...  7.77 us
    all_to_all x1, starting transfers between devices, per_device(): shares = lax.all_to_all(pieces, ('z',), 0, 0, tiled=True)  5.36 us
    all_to_all x1, waiting for transfers between devices, per_device(): shares = lax.all_to_all(pieces, ('z',), 0, 0, tiled=True)  4.91 us
    ppermute x1, starting transfers between devices, per_device(): high = lax.ppermute(down, GRID, [((i + 1) % 8, i) for i in range(8)])  4.57 us
    ppermute x1, waiting for transfers between devices, per_device(): low = lax.ppermute(up, GRID, [(i, (i + 1) % 8) for i in range(8)])  3.96 us
    ppermute x1, starting transfers between devices, per_device(): lax.ppermute(smooth, SLAB, [(i, (i + 1) % 32) for i in range(32)])  1.87 us
    ppermute x1, waiting for transfers between devices, per_device(): high = lax.ppermute(down, GRID, [((i + 1) % 8, i) for i in range(8)])  1.79 us
  transfers between devices with their start and end apart: 4, of which 4 were waited for; matrix products, arithmetic and copies ran while one was open for 0% of the time, Pallas kernels for 0%

profile of v3, /device:TPU:1, one launch (start us, length us, event | category | flops | bytes accessed | tf_op | source)
XLA Modules:
  0.0 48.8 jit_solution(1568672646334778197)
XLA Ops:
  0.6 0.9 %pad_maximum_fusion = (f32[224,128]{1,0:T(8,128)S(1)}, f32[224,128]{1,0:T(8,128)S(1)}) fusion(f32[128,128]{1,0:T(8,128)} %bitcast.4, f32[128,128]{1,0:T(8,128)} %bitcast.5), kind=kLoop, calls=%fused_computation | loop fusion | flops 57344 | bytes 360448 | tf_op jit(solution)/shard_map/concatenate | solution.py:240
  1.6 4.6 %collective-permute-start.1 = (f32[224,128]{1,0:T(8,128)S(1)}, f32[224,128]{1,0:T(8,128)S(1)}, u32[]{:S(2)}, u32[]{:S(2)}) collective-permute-start(f32[224,128]{1,0:T(8,128)S(1)} %get-tuple-element.14.down), channel_id=1, source_target_pairs={{1,0},{2,1},{3,2},{4,3},{5,4},{6,5},{7,6},{0,7},{9,8},{10,9},{11,1... | collective-permute-start | bytes 344072 | tf_op jit(solution)/shard_map/ppermute | solution.py:243
  6.1 0.0 collective-permute-start
  6.1 1.8 %collective-permute-done.1.high = f32[224,128]{1,0:T(8,128)S(1)} collective-permute-done((f32[224,128]{1,0:T(8,128)S(1)}, f32[224,128]{1,0:T(8,128)S(1)}, u32[]{:S(2)}, u32[]{:S(2)}) %collective-permute-start.1) | collective-permute-done | bytes 114720 | tf_op jit(solution)/shard_map/ppermute | solution.py:243
  7.9 4.0 %collective-permute-done.low = f32[224,128]{1,0:T(8,128)S(1)} collective-permute-done((f32[224,128]{1,0:T(8,128)S(1)}, f32[224,128]{1,0:T(8,128)S(1)}, u32[]{:S(2)}, u32[]{:S(2)}) %collective-permute-start) | collective-permute-done | bytes 114720 | tf_op jit(solution)/shard_map/ppermute | solution.py:242
  11.9 0.8 %shard_map.41 = (f32[128,128]{1,0:T(8,128)S(1)}, f32[32,5,4,128]{3,2,1,0:T(4,128)S(1)}) custom-call(f32[224,128]{1,0:T(8,128)S(1)} %get-tuple-element.15.up, f32[224,128]{1,0:T(8,128)S(1)} %get-tuple-element.14.down, f32[224,128]{1,0:T(8,128)S(1)} %collective-permute-done.low, f32[224,128]{1,0:T(8,128)S(1)} %collective-permute-done.1.high), custom_call_target="tpu_custom_call" | custom-call | flops 4000000 | bytes 458752 | tf_op jit(solution)/shard_map/pallas_call | solution.py:221
  12.8 15.6 %all_to_all.10.received = f32[32,5,4,128]{3,2,1,0:T(4,128)S(1)} all-to-all(f32[32,5,4,128]{3,2,1,0:T(4,128)S(1)} %get-tuple-element.8), channel_id=1, replica_groups=mesh['z'=8,'h'=2,'c'=2,'l'=2,'y'=4] {'h','c','l','y'}, dimensions={0} | all-to-all | bytes 655360 | tf_op jit(solution)/shard_map/all_to_all | solution.py:251
  28.4 6.2 %shard_map.42 = f32[8,32,128]{2,1,0:T(8,128)} custom-call(f32[32,5,4,128]{3,2,1,0:T(4,128)S(1)} %all_to_all.10.received), custom_call_target="tpu_custom_call" | custom-call | flops 12000000 | bytes 327680 | tf_op jit(solution)/shard_map/pallas_call | solution.py:221
  34.6 5.4 %all-to-all-start.1 = ((f32[8,32,128]{2,1,0:T(8,128)}), f32[8,32,128]{2,1,0:T(8,128)S(1)}, u32[]{:S(2)}, u32[]{:S(2)}) async-start(f32[8,32,128]{2,1,0:T(8,128)} %shard_map.42), calls=%async_computation.1 | async-start | bytes 262144 | tf_op jit(solution)/shard_map/all_to_all | solution.py:261
  39.9 1.9 %collective-permute-start.2 = (f32[128,128]{1,0:T(8,128)S(1)}, f32[128,128]{1,0:T(8,128)S(1)}, u32[]{:S(2)}, u32[]{:S(2)}) collective-permute-start(f32[128,128]{1,0:T(8,128)S(1)} %get-tuple-element.11.smooth), channel_id=1, source_target_pairs={{0,8},{8,16},{16,24},{24,32},{32,40},{40,48},{48,56},{56,64},{64,7... | collective-permute-start | bytes 196616 | tf_op jit(solution)/shard_map/ppermute | solution.py:260
  41.8 1.3 %collective-permute-done.2.smooth_before = f32[128,128]{1,0:T(8,128)S(1)} collective-permute-done((f32[128,128]{1,0:T(8,128)S(1)}, f32[128,128]{1,0:T(8,128)S(1)}, u32[]{:S(2)}, u32[]{:S(2)}) %collective-permute-start.2) | collective-permute-done | bytes 65568 | tf_op jit(solution)/shard_map/ppermute | solution.py:260
  43.1 4.9 %all-to-all-done.1.received = f32[8,32,128]{2,1,0:T(8,128)S(1)} async-done(((f32[8,32,128]{2,1,0:T(8,128)}), f32[8,32,128]{2,1,0:T(8,128)S(1)}, u32[]{:S(2)}, u32[]{:S(2)}) %all-to-all-start.1) | async-done | bytes 131104 | tf_op jit(solution)/shard_map/all_to_all | solution.py:261
  48.0 0.7 %shard_map.43 = (f32[128,128]{1,0:T(8,128)}, f32[128,128]{1,0:T(8,128)}) custom-call(f32[8,32,128]{2,1,0:T(8,128)S(1)} %all-to-all-done.1.received, f32[128,128]{1,0:T(8,128)S(1)} %get-tuple-element.11.smooth, f32[128,128]{1,0:T(8,128)S(1)} %collective-permute-done.2.smooth_before), custom_call_target="tpu_custom_call" | custom-call | flops 200000 | bytes 262144 | tf_op jit(solution)/shard_map/pallas_call | solution.py:221
Async XLA Ops:
  1.6 6.4 %collective-permute-start.1 = (f32[224,128]{1,0:T(8,128)S(1)}, f32[224,128]{1,0:T(8,128)S(1)}, u32[]{:S(2)}, u32[]{:S(2)}) collective-permute-start(f32[224,128]{1,0:T(8,128)S(1)} %get-tuple-element.14.down), channel_id=1, source_target_pairs={{1,0},{2,1},{3,2},{4,3},{5,4},{6,5},{7,6},{0,7},{9,8},{10,9},{11,1... | collective-permute-start | bytes 344072 | tf_op jit(solution)/shard_map/ppermute | solution.py:243
  6.1 5.8 %collective-permute-start = (f32[224,128]{1,0:T(8,128)S(1)}, f32[224,128]{1,0:T(8,128)S(1)}, u32[]{:S(2)}, u32[]{:S(2)}) collective-permute-start(f32[224,128]{1,0:T(8,128)S(1)} %get-tuple-element.15.up), channel_id=1, source_target_pairs={{0,1},{1,2},{2,3},{3,4},{4,5},{5,6},{6,7},{7,0},{8,9},{9,10},{10,1... | collective-permute-start | bytes 344072 | tf_op jit(solution)/shard_map/ppermute | solution.py:242
  34.6 13.5 %all-to-all-start.1 = ((f32[8,32,128]{2,1,0:T(8,128)}), f32[8,32,128]{2,1,0:T(8,128)S(1)}, u32[]{:S(2)}, u32[]{:S(2)}) async-start(f32[8,32,128]{2,1,0:T(8,128)} %shard_map.42), calls=%async_computation.1 | async-start | bytes 262144 | tf_op jit(solution)/shard_map/all_to_all | solution.py:261
  39.9 3.2 %collective-permute-start.2 = (f32[128,128]{1,0:T(8,128)S(1)}, f32[128,128]{1,0:T(8,128)S(1)}, u32[]{:S(2)}, u32[]{:S(2)}) collective-permute-start(f32[128,128]{1,0:T(8,128)S(1)} %get-tuple-element.11.smooth), channel_id=1, source_target_pairs={{0,8},{8,16},{16,24},{24,32},{32,40},{40,48},{48,56},{56,64},{64,7... | collective-permute-start | bytes 196616 | tf_op jit(solution)/shard_map/ppermute | solution.py:260

commit v4 on v3

--- a/solution.py
+++ b/solution.py
@@ -19,7 +19,7 @@
 AXES = ("z", "h", "c", "l", "y")
 SLAB = ("z", "h", "c")
 GRID = ("l", "y")
-PLANE = ("h", "c", "l", "y")
+CORES = ("h", "l", "y")
 
 
 def weights_of(kind):
@@ -54,34 +54,20 @@
     return 0.125 * jnp.where(even, low + pltpu.roll(low, 127, 1), high + pltpu.roll(high, 1, 1))
 
 
-def halo_kernel(start, rates, up, down, done):
-    copies = [
-        pltpu.make_async_copy(source, target, done.at[i])
-        for i, (source, target) in enumerate(
-            (
-                (start, up.at[0:128]),
-                (start, down.at[0:128]),
-                (rates.at[32:128], up.at[128:224]),
-                (rates.at[0:96], down.at[128:224]),
-            )
-        )
-    ]
-    for copy in copies:
-        copy.start()
-    for copy in copies:
-        copy.wait()
-
-
-def fine_kernel(up, down, low, high, smooth_out, send_out, wide, ends, rates):
+def fine_kernel(one, two, from_one, from_two, smooth_out, send_out, wide, ends, all_rates, rates):
     even = even_lanes()
     is_first = (lax.axis_index("z") == 0) & (lax.axis_index("h") == 0) & (lax.axis_index("c") == 0)
-    wide[0:128] = low[96:224]
-    wide[128:256] = down[0:128]
-    wide[256:384] = high[0:128]
-    rates[0:32] = down[128:160]
-    rates[32:128] = up[0:96]
+    is_even = lax.axis_index("y") % 2 == 0
+    wide[pl.ds(pl.multiple_of(jnp.where(is_even, 256, 0), 32), 128)] = from_one[96:224]
+    wide[128:256] = one[96:224]
+    wide[pl.ds(pl.multiple_of(jnp.where(is_even, 0, 256), 32), 128)] = from_two[0:128]
+    rates[0:32] = jnp.where(is_even, two[128:160], one[0:32])
+    rates[32:128] = jnp.where(is_even, one[0:96], two[128:224])
+    all_rates[pl.ds(pl.multiple_of(jnp.where(is_even, 224, 0), 32), 96)] = from_one[0:96]
+    all_rates[96:224] = rates[...]
+    all_rates[pl.ds(pl.multiple_of(jnp.where(is_even, 0, 224), 32), 96)] = from_two[128:224]
     current = wide[...].reshape(12, 32, 128)
-    rate = jnp.concatenate([low[0:96], rates[...], high[128:224]], axis=0).reshape(10, 32, 128)
+    rate = all_rates[...].reshape(10, 32, 128)
     for _ in range(FINE):
         mixed = line_filter(
             pltpu.roll(current, 1, 2), current, pltpu.roll(current, 127, 2), fine_along_y
@@ -107,8 +93,8 @@
     for i in range(2):
         for half in range(2):
             rows = terms[i][4 * half : 4 * half + 4]
-            send_out[:, 2 * i + half] = jnp.broadcast_to(rows[None], (32, 4, 128))
-    send_out[:, 4] = jnp.broadcast_to(layer[None, 0:4], (32, 4, 128))
+            send_out[:, 2 * i + half] = jnp.broadcast_to(rows[None], (16, 4, 128))
+    send_out[:, 4] = jnp.broadcast_to(layer[None, 0:4], (16, 4, 128))
 
 
 def side_weights(kind):
@@ -137,23 +123,30 @@
     return scaled_filter(behind, flat, beyond, coarse_along_x)
 
 
-def chain_kernel(received, send_out, history):
+def chain_kernel(received, from_core, send_out, history):
     even = even_lanes()
+    is_first_core = lax.axis_index("c") == 0
     depth = range(16)
 
-    def joined(first, second):
-        return jnp.concatenate([received[first], received[second]], axis=0)
+    def piece(source, part):
+        far, core, place = source
+        first, second = (received, from_core) if core == 0 else (from_core, received)
+        at = (8 * far + place, part)
+        return jnp.where(is_first_core, first[at], second[at])
+
+    def joined(first, second, part, next_part):
+        return jnp.concatenate([piece(first, part), piece(second, next_part)], axis=0)
 
     middle = 1.0
     for kind in (coarse_along_z, coarse_along_x, coarse_along_y):
         middle *= weights_of(kind)[1]
-    rates = [joined((16 * (z % 2) + z // 2, 4), (16 * (z % 2) + 8 + z // 2, 4)) for z in depth]
+    rates = [joined((z % 2, 0, z // 2), (z % 2, 1, z // 2), 4, 4) for z in depth]
     drops = [1.0 - rate for rate in rates]
     rates = [middle * rate for rate in rates]
 
     def term(step):
-        at = [(8 * step + z // 2, 2 * (z % 2)) for z in depth]
-        return [joined((source, part), (source, part + 1)) for source, part in at]
+        at = [((step // 2, step % 2, z // 2), 2 * (z % 2)) for z in depth]
+        return [joined(source, source, part, part + 1) for source, part in at]
 
     def keep(step, layers):
         for z in depth:
@@ -215,15 +208,15 @@
     return jax.ShapeDtypeStruct(shape, jnp.float32)
 
 
-def local(kernel, operands, outputs, scratch, operations, space=pltpu.VMEM, sent=True):
+def local(kernel, operands, outputs, buffers, operations, sent=True):
     if sent:
         outputs = jax.tree.map(lambda a: pltpu.VMEM(a.shape, a.dtype), outputs)
     return pl.pallas_call(
         kernel,
         out_shape=outputs,
-        in_specs=[pl.BlockSpec(memory_space=space)] * len(operands),
+        in_specs=[pl.BlockSpec(memory_space=pltpu.VMEM)] * len(operands),
         out_specs=jax.tree.map(lambda _: pl.BlockSpec(memory_space=pltpu.VMEM), outputs),
-        scratch_shapes=scratch,
+        scratch_shapes=buffers,
         cost_estimate=pl.CostEstimate(
             flops=operations, bytes_accessed=4 * sum(a.size for a in operands), transcendentals=0
         ),
@@ -237,21 +230,33 @@
 
 def per_device(starts, cell_rates):
     start, rates = starts.reshape(128, 128), cell_rates.reshape(128, 128)
-    own = jnp.concatenate([rates, start, rates], axis=0)
-    up, down = own[32:256], own[128:352]
-    low = lax.ppermute(up, GRID, [(i, (i + 1) % 8) for i in range(8)])
-    high = lax.ppermute(down, GRID, [((i + 1) % 8, i) for i in range(8)])
+    is_even = lax.axis_index("y") % 2 == 0
+    for_below, for_above = rates[:96], rates[32:]
+    own = jnp.concatenate(
+        [
+            jnp.where(is_even, for_above, for_below),
+            start,
+            jnp.where(is_even, for_below, for_above),
+        ],
+        axis=0,
+    )
+    one, two = own[:224], own[96:]
+    pairs = [(i, i ^ 1) for i in range(8)]
+    others = [(i, (i - 1 + 2 * (i % 2)) % 8) for i in range(8)]
+    from_one = lax.ppermute(one, GRID, pairs)
+    from_two = lax.ppermute(two, GRID, others)
     smooth, message = local(
         fine_kernel,
-        (up, down, low, high),
-        (array(128, 128), array(32, 5, 4, 128)),
-        [scratch(384, 128), scratch(128, 128), scratch(128, 128)],
+        (one, two, from_one, from_two),
+        (array(128, 128), array(16, 5, 4, 128)),
+        [scratch(384, 128), scratch(128, 128), scratch(320, 128), scratch(128, 128)],
         4_000_000,
     )
-    gathered = lax.all_to_all(message, PLANE, 0, 0, tiled=True)
+    gathered = lax.all_to_all(message, CORES, 0, 0, tiled=True)
+    from_core = lax.ppermute(gathered, ("c",), [(0, 1), (1, 0)])
     pieces = local(
         chain_kernel,
-        (gathered,),
+        (gathered, from_core),
         array(8, 32, 128),
         [scratch(STEPS + 1, 16, 8, 128)],
         12_000_000,

time: 49 us -> 47.4 us (0.967)
  blocking collectives: 15.6 us -> 12.1 us
  starting transfers between devices: 11.8 us -> 14.4 us
  waiting for transfers between devices: 12 us -> 11.3 us
    all_to_all x1, blocking collectives: 15.6 us -> 12.1 us  [per_device(): gathered = lax.all_to_all(message, CORES, 0, 0, tiled=True)]
    ppermute x2 -> x3, starting transfers between devices: 4.57 us -> 7.45 us  [the longest x1 4.58 us: per_device(): from_two = lax.ppermute(two, GRID, others)]
    ppermute x2 -> x3, waiting for transfers between devices: 5.75 us -> 4.67 us  [the longest x1 2.18 us: per_device(): from_two = lax.ppermute(two, GRID, others)]
    concatenate x1, other arithmetic: 0.94 us -> 0.02 us  [per_device(): jnp.concatenate([jnp.where(is_even, for_above, for_below), start, jnp.whe...]
    select_n x0 -> x1, other arithmetic: none -> 0.88 us  [per_device(): jnp.where(is_even, for_below, for_above)]
  transfers between devices with their start and end apart: 4 -> 5, of which waited for: 4 -> 5; matrix products, arithmetic and copies ran while one was open for 0% -> 0% of each run, Pallas kernels for 0% -> 0%
where the time goes in v4:
time: 47.4 us; the launch traced here: 47.1 us
  starting transfers between devices  14.4 us (30%)
  blocking collectives  12.1 us (26%)
  waiting for transfers between devices  11.3 us (24%)
  Pallas kernels  7.77 us (16%)
  other arithmetic  0.9 us (2%)
  between operations  0.68 us (1%)
    all_to_all x1, blocking collectives, per_device(): gathered = lax.all_to_all(message, CORES, 0, 0, tiled=True)  12.1 us
    pallas_call x3, Pallas kernels, local(): pl.pallas_call(kernel, out_shape=outputs, in_specs=[pl.BlockSpec(memory_s...  7.77 us
    all_to_all x1, starting transfers between devices, per_device(): shares = lax.all_to_all(pieces, ('z',), 0, 0, tiled=True)  5.36 us
    all_to_all x1, waiting for transfers between devices, per_device(): shares = lax.all_to_all(pieces, ('z',), 0, 0, tiled=True)  5.31 us
    ppermute x1, starting transfers between devices, per_device(): from_two = lax.ppermute(two, GRID, others)  4.58 us
    ppermute x1, starting transfers between devices, per_device(): from_core = lax.ppermute(gathered, ('c',), [(0, 1), (1, 0)])  2.87 us
    ppermute x1, waiting for transfers between devices, per_device(): from_two = lax.ppermute(two, GRID, others)  2.18 us
    ppermute x1, starting transfers between devices, per_device(): lax.ppermute(smooth, SLAB, [(i, (i + 1) % 32) for i in range(32)])  1.54 us
  transfers between devices with their start and end apart: 5, of which 5 were waited for; matrix products, arithmetic and copies ran while one was open for 0% of the time, Pallas kernels for 0%

profile of v4, /device:TPU:1, one launch (start us, length us, event | category | flops | bytes accessed | tf_op | source)
XLA Modules:
  0.0 47.1 jit_solution(13019918759536208584)
XLA Ops:
  0.6 0.0 copy-start
  0.7 0.9 %slice_select_fusion = (f32[3,32,128]{2,1,0:T(8,128)S(1)}, f32[3,32,128]{2,1,0:T(8,128)S(1)}) fusion(f32[4,32,128]{2,1,0:T(8,128)} %param.3, pred[]{:T(512)S(6)} %eq.5), kind=kLoop, calls=%fused_computation.2 | loop fusion | flops 24576 | bytes 196609 | tf_op jit(solution)/shard_map/jit(_where)/select_n | solution.py:239
  1.5 0.0 copy-done
  1.6 4.6 %collective-permute-start.1 = (f32[224,128]{1,0:T(8,128)S(1)}, f32[224,128]{1,0:T(8,128)S(1)}, u32[]{:S(2)}, u32[]{:S(2)}) collective-permute-start(f32[224,128]{1,0:T(8,128)S(1)} %get-tuple-element.14.two), channel_id=1, source_target_pairs={{0,7},{1,2},{2,1},{3,4},{4,3},{5,6},{6,5},{7,0},{8,15},{9,10},{10,... | collective-permute-start | bytes 344072 | tf_op jit(solution)/shard_map/ppermute | solution.py:247
  6.2 0.0 collective-permute-start
  6.2 2.2 %collective-permute-done.1.from_two = f32[224,128]{1,0:T(8,128)S(1)} collective-permute-done((f32[224,128]{1,0:T(8,128)S(1)}, f32[224,128]{1,0:T(8,128)S(1)}, u32[]{:S(2)}, u32[]{:S(2)}) %collective-permute-start.1) | collective-permute-done | bytes 114720 | tf_op jit(solution)/shard_map/ppermute | solution.py:247
  8.3 1.5 %collective-permute-done.from_one = f32[224,128]{1,0:T(8,128)S(1)} collective-permute-done((f32[224,128]{1,0:T(8,128)S(1)}, f32[224,128]{1,0:T(8,128)S(1)}, u32[]{:S(2)}, u32[]{:S(2)}) %collective-permute-start) | collective-permute-done | bytes 114720 | tf_op jit(solution)/shard_map/ppermute | solution.py:246
  9.8 0.9 %shard_map.41 = (f32[128,128]{1,0:T(8,128)S(1)}, f32[16,5,4,128]{3,2,1,0:T(4,128)S(1)}) custom-call(f32[224,128]{1,0:T(8,128)S(1)} %get-tuple-element.15.one, f32[224,128]{1,0:T(8,128)S(1)} %get-tuple-element.14.two, f32[224,128]{1,0:T(8,128)S(1)} %collective-permute-done.from_one, f32[224,128]{1,0:T(8,128)S(1)} %collective-permute-done.1.from_two), custom_call_target="tpu_custom_call" | custom-call | flops 4000000 | bytes 458752 | tf_op jit(solution)/shard_map/pallas_call | solution.py:214
  10.7 12.1 %all_to_all.10.received = f32[16,5,4,128]{3,2,1,0:T(4,128)S(1)} all-to-all(f32[16,5,4,128]{3,2,1,0:T(4,128)S(1)} %get-tuple-element.8), channel_id=1, replica_groups=mesh['z'=8,'h'=2,'c'=2,'l'=2,'y'=4] {'h','l','y'}, dimensions={0} | all-to-all | bytes 327680 | tf_op jit(solution)/shard_map/all_to_all | solution.py:255
  22.8 2.9 %collective-permute-start.2 = (f32[16,5,4,128]{3,2,1,0:T(4,128)S(1)}, f32[16,5,4,128]{3,2,1,0:T(4,128)S(1)}, u32[]{:S(2)}, u32[]{:S(2)}) collective-permute-start(f32[16,5,4,128]{3,2,1,0:T(4,128)S(1)} %all_to_all.10.received), channel_id=1, source_target_pairs={{0,8},{8,0},{1,9},{9,1},{2,10},{10,2},{3,11},{11,3},{4,12},{12,4},... | collective-permute-start | bytes 491528 | tf_op jit(solution)/shard_map/ppermute | solution.py:256
  25.6 1.0 %collective-permute-done.2.from_core = f32[16,5,4,128]{3,2,1,0:T(4,128)S(1)} collective-permute-done((f32[16,5,4,128]{3,2,1,0:T(4,128)S(1)}, f32[16,5,4,128]{3,2,1,0:T(4,128)S(1)}, u32[]{:S(2)}, u32[]{:S(2)}) %collective-permute-start.2) | collective-permute-done | bytes 163872 | tf_op jit(solution)/shard_map/ppermute | solution.py:256
  26.7 6.2 %shard_map.42 = f32[8,32,128]{2,1,0:T(8,128)} custom-call(f32[16,5,4,128]{3,2,1,0:T(4,128)S(1)} %all_to_all.10.received, f32[16,5,4,128]{3,2,1,0:T(4,128)S(1)} %collective-permute-done.2.from_core), custom_call_target="tpu_custom_call" | custom-call | flops 12000000 | bytes 327680 | tf_op jit(solution)/shard_map/pallas_call | solution.py:214
  32.8 5.4 %all-to-all-start.1 = ((f32[8,32,128]{2,1,0:T(8,128)}), f32[8,32,128]{2,1,0:T(8,128)S(1)}, u32[]{:S(2)}, u32[]{:S(2)}) async-start(f32[8,32,128]{2,1,0:T(8,128)} %shard_map.42), calls=%async_computation.1 | async-start | bytes 262144 | tf_op jit(solution)/shard_map/all_to_all | solution.py:266
  38.2 1.5 %collective-permute-start.3 = (f32[128,128]{1,0:T(8,128)S(1)}, f32[128,128]{1,0:T(8,128)S(1)}, u32[]{:S(2)}, u32[]{:S(2)}) collective-permute-start(f32[128,128]{1,0:T(8,128)S(1)} %get-tuple-element.11.smooth), channel_id=1, source_target_pairs={{0,8},{8,16},{16,24},{24,32},{32,40},{40,48},{48,56},{56,64},{64,7... | collective-permute-start | bytes 196616 | tf_op jit(solution)/shard_map/ppermute | solution.py:265
  39.7 1.3 %collective-permute-done.3.smooth_before = f32[128,128]{1,0:T(8,128)S(1)} collective-permute-done((f32[128,128]{1,0:T(8,128)S(1)}, f32[128,128]{1,0:T(8,128)S(1)}, u32[]{:S(2)}, u32[]{:S(2)}) %collective-permute-start.3) | collective-permute-done | bytes 65568 | tf_op jit(solution)/shard_map/ppermute | solution.py:265
  41.1 5.3 %all-to-all-done.1.received = f32[8,32,128]{2,1,0:T(8,128)S(1)} async-done(((f32[8,32,128]{2,1,0:T(8,128)}), f32[8,32,128]{2,1,0:T(8,128)S(1)}, u32[]{:S(2)}, u32[]{:S(2)}) %all-to-all-start.1) | async-done | bytes 131104 | tf_op jit(solution)/shard_map/all_to_all | solution.py:266
  46.4 0.7 %shard_map.43 = (f32[128,128]{1,0:T(8,128)}, f32[128,128]{1,0:T(8,128)}) custom-call(f32[8,32,128]{2,1,0:T(8,128)S(1)} %all-to-all-done.1.received, f32[128,128]{1,0:T(8,128)S(1)} %get-tuple-element.11.smooth, f32[128,128]{1,0:T(8,128)S(1)} %collective-permute-done.3.smooth_before), custom_call_target="tpu_custom_call" | custom-call | flops 200000 | bytes 262144 | tf_op jit(solution)/shard_map/pallas_call | solution.py:214
  (1 shorter events, 0.0 us)
Async XLA Ops:
  0.6 0.9 %copy-start = (f32[1,4,32,128]{3,2,1,0:T(8,128)S(1)}, f32[1,4,32,128]{3,2,1,0:T(8,128)}, u32[]{:S(2)}) copy-start(f32[1,4,32,128]{3,2,1,0:T(8,128)} %param.2) | copy-start | bytes 196612
  1.6 6.8 %collective-permute-start.1 = (f32[224,128]{1,0:T(8,128)S(1)}, f32[224,128]{1,0:T(8,128)S(1)}, u32[]{:S(2)}, u32[]{:S(2)}) collective-permute-start(f32[224,128]{1,0:T(8,128)S(1)} %get-tuple-element.14.two), channel_id=1, source_target_pairs={{0,7},{1,2},{2,1},{3,4},{4,3},{5,6},{6,5},{7,0},{8,15},{9,10},{10,... | collective-permute-start | bytes 344072 | tf_op jit(solution)/shard_map/ppermute | solution.py:247
  6.2 3.6 %collective-permute-start = (f32[224,128]{1,0:T(8,128)S(1)}, f32[224,128]{1,0:T(8,128)S(1)}, u32[]{:S(2)}, u32[]{:S(2)}) collective-permute-start(f32[224,128]{1,0:T(8,128)S(1)} %get-tuple-element.15.one), channel_id=1, source_target_pairs={{0,1},{1,0},{2,3},{3,2},{4,5},{5,4},{6,7},{7,6},{8,9},{9,8},{10,11... | collective-permute-start | bytes 344072 | tf_op jit(solution)/shard_map/ppermute | solution.py:246
  22.8 3.9 %collective-permute-start.2 = (f32[16,5,4,128]{3,2,1,0:T(4,128)S(1)}, f32[16,5,4,128]{3,2,1,0:T(4,128)S(1)}, u32[]{:S(2)}, u32[]{:S(2)}) collective-permute-start(f32[16,5,4,128]{3,2,1,0:T(4,128)S(1)} %all_to_all.10.received), channel_id=1, source_target_pairs={{0,8},{8,0},{1,9},{9,1},{2,10},{10,2},{3,11},{11,3},{4,12},{12,4},... | collective-permute-start | bytes 491528 | tf_op jit(solution)/shard_map/ppermute | solution.py:256
  32.8 13.5 %all-to-all-start.1 = ((f32[8,32,128]{2,1,0:T(8,128)}), f32[8,32,128]{2,1,0:T(8,128)S(1)}, u32[]{:S(2)}, u32[]{:S(2)}) async-start(f32[8,32,128]{2,1,0:T(8,128)} %shard_map.42), calls=%async_computation.1 | async-start | bytes 262144 | tf_op jit(solution)/shard_map/all_to_all | solution.py:266
  38.2 2.9 %collective-permute-start.3 = (f32[128,128]{1,0:T(8,128)S(1)}, f32[128,128]{1,0:T(8,128)S(1)}, u32[]{:S(2)}, u32[]{:S(2)}) collective-permute-start(f32[128,128]{1,0:T(8,128)S(1)} %get-tuple-element.11.smooth), channel_id=1, source_target_pairs={{0,8},{8,16},{16,24},{24,32},{32,40},{40,48},{48,56},{56,64},{64,7... | collective-permute-start | bytes 196616 | tf_op jit(solution)/shard_map/ppermute | solution.py:265

commit v5 on v4

--- a/solution.py
+++ b/solution.py
@@ -30,6 +30,16 @@
 def line_filter(behind, middle, beyond, kind):
     a, b, c = weights_of(kind)
     return a * behind + b * middle + c * beyond
+
+
+def side_weights(kind):
+    a, b, c = weights_of(kind)
+    return a / b, c / b
+
+
+def scaled_filter(behind, middle, beyond, kind):
+    a, c = side_weights(kind)
+    return middle + (a * behind + c * beyond)
 
 
 def even_lanes():
@@ -68,15 +78,20 @@
     all_rates[pl.ds(pl.multiple_of(jnp.where(is_even, 0, 224), 32), 96)] = from_two[128:224]
     current = wide[...].reshape(12, 32, 128)
     rate = all_rates[...].reshape(10, 32, 128)
+    middle = 1.0
+    for kind in (fine_along_z, fine_along_x, fine_along_y):
+        middle *= weights_of(kind)[1]
+    drop, gain = 1.0 - rate, middle * rate
     for _ in range(FINE):
-        mixed = line_filter(
-            pltpu.roll(current, 1, 2), current, pltpu.roll(current, 127, 2), fine_along_y
+        mixed = scaled_filter(current[:-2], current[1:-1], current[2:], fine_along_z)
+        mixed = scaled_filter(
+            pltpu.roll(mixed, 1, 1), mixed, pltpu.roll(mixed, 31, 1), fine_along_x
         )
-        mixed = line_filter(pltpu.roll(mixed, 1, 1), mixed, pltpu.roll(mixed, 31, 1), fine_along_x)
-        mixed = line_filter(mixed[:-2], mixed[1:-1], mixed[2:], fine_along_z)
-        current = current[1:-1]
-        current = current + rate * (mixed - current)
-        rate = rate[1:-1]
+        mixed = scaled_filter(
+            pltpu.roll(mixed, 1, 2), mixed, pltpu.roll(mixed, 127, 2), fine_along_y
+        )
+        current = drop * current[1:-1] + gain * mixed
+        drop, gain = drop[1:-1], gain[1:-1]
     ends[...] = current.reshape(128, 128)
     coarse = [packed_layer(wide, 64 + 64 * i, even) for i in range(4)]
     flat = [packed_plane_filter(v, even) for v in coarse]
@@ -97,30 +112,18 @@
     send_out[:, 4] = jnp.broadcast_to(layer[None, 0:4], (16, 4, 128))
 
 
-def side_weights(kind):
-    a, b, c = weights_of(kind)
-    return a / b, c / b
-
-
-def scaled_filter(behind, middle, beyond, kind):
-    a, c = side_weights(kind)
-    return middle + (a * behind + c * beyond)
-
-
-def scaled_plane_filter(v, even):
-    near, far = {}, {}
-    for by in (1, 2, 3):
-        near[by], far[by] = pltpu.roll(v, by, 1), pltpu.roll(v, 128 - by, 1)
-    flat = scaled_filter(near[2], v, far[2], coarse_along_y)
-    other = scaled_filter(
-        jnp.where(even, near[1], near[3]),
-        jnp.where(even, far[1], near[1]),
-        jnp.where(even, far[3], far[1]),
-        coarse_along_y,
-    )
-    behind = jnp.where(even, pltpu.roll(other, 1, 0), other)
-    beyond = jnp.where(even, other, pltpu.roll(other, 7, 0))
-    return scaled_filter(behind, flat, beyond, coarse_along_x)
+def spread_pair(v, even):
+    return jnp.where(even, v, pltpu.roll(v, 1, 1)), jnp.where(even, pltpu.roll(v, 127, 1), v)
+
+
+def pair_filter(pair):
+    low, high = (
+        scaled_filter(pltpu.roll(v, 2, 1), v, pltpu.roll(v, 126, 1), coarse_along_y) for v in pair
+    )
+    return (
+        scaled_filter(pltpu.roll(high, 1, 0), low, high, coarse_along_x),
+        scaled_filter(low, high, pltpu.roll(low, 7, 0), coarse_along_x),
+    )
 
 
 def chain_kernel(received, from_core, send_out, history):
@@ -141,8 +144,9 @@
     for kind in (coarse_along_z, coarse_along_x, coarse_along_y):
         middle *= weights_of(kind)[1]
     rates = [joined((z % 2, 0, z // 2), (z % 2, 1, z // 2), 4, 4) for z in depth]
-    drops = [1.0 - rate for rate in rates]
-    rates = [middle * rate for rate in rates]
+    rates = [spread_pair(rate, even) for rate in rates]
+    drops = [[1.0 - rate for rate in pair] for pair in rates]
+    rates = [[middle * rate for rate in pair] for pair in rates]
 
     def term(step):
         at = [((step // 2, step % 2, z // 2), 2 * (z % 2)) for z in depth]
@@ -150,30 +154,32 @@
 
     def keep(step, layers):
         for z in depth:
-            history[step, z] = layers[z]
+            history[step, z] = jnp.where(even, *layers[z])
 
     def advance(layers):
-        flat = [scaled_plane_filter(v, even) for v in layers]
+        flat = [pair_filter(pair) for pair in layers]
         out = []
         for z in depth:
-            mixed = scaled_filter(flat[z - 1], flat[z], flat[(z + 1) % 16], coarse_along_z)
-            out.append(drops[z] * layers[z] + rates[z] * mixed)
+            behind, here, beyond = flat[z - 1], flat[z], flat[(z + 1) % 16]
+            mixed = [scaled_filter(*trio, coarse_along_z) for trio in zip(behind, here, beyond)]
+            out.append([drops[z][i] * layers[z][i] + rates[z][i] * mixed[i] for i in range(2)])
         return out
 
     history[0] = jnp.zeros((16, 8, 128), jnp.float32)
-    layers = term(0)
+    layers = [spread_pair(v, even) for v in term(0)]
     keep(1, layers)
     for step in range(1, GROUP):
-        layers = [a + b for a, b in zip(advance(layers), term(step))]
+        added = [spread_pair(v, even) for v in term(step)]
+        layers = [[a + b for a, b in zip(*both)] for both in zip(advance(layers), added)]
         keep(step + 1, layers)
 
     def body(step, layers):
         layers = advance(layers)
         keep(step + 1, layers)
-        return tuple(layers)
+        return layers
 
     mine = lax.axis_index("z")
-    lax.fori_loop(GROUP, STEPS - GROUP * mine, body, tuple(layers))
+    lax.fori_loop(GROUP, STEPS - GROUP * mine, body, layers)
     place = lax.axis_index("h") * 2 + lax.axis_index("c")
     first = (lax.axis_index("l") * 4 + lax.axis_index("y")) * 2
     for target in range(8):

time: 47.4 us -> 47 us (level)
  Pallas kernels: 7.77 us -> 7.02 us
    pallas_call x3, Pallas kernels: 7.77 us -> 7.02 us  [local(): pl.pallas_call(kernel, out_shape=outputs, in_specs=[pl.BlockSpec(memory_s...]
where the time goes in v5:
time: 47 us; the launch traced here: 46.7 us
  starting transfers between devices  14.8 us (31%)
  blocking collectives  12.1 us (26%)
  waiting for transfers between devices  11.3 us (24%)
  Pallas kernels  7.02 us (15%)
  other arithmetic  0.9 us (2%)
  between operations  0.67 us (1%)
    all_to_all x1, blocking collectives, per_device(): gathered = lax.all_to_all(message, CORES, 0, 0, tiled=True)  12.1 us
    pallas_call x3, Pallas kernels, local(): pl.pallas_call(kernel, out_shape=outputs, in_specs=[pl.BlockSpec(memory_s...  7.02 us
    all_to_all x1, starting transfers between devices, per_device(): shares = lax.all_to_all(pieces, ('z',), 0, 0, tiled=True)  5.75 us
    all_to_all x1, waiting for transfers between devices, per_device(): shares = lax.all_to_all(pieces, ('z',), 0, 0, tiled=True)  5.31 us
    ppermute x1, starting transfers between devices, per_device(): from_two = lax.ppermute(two, GRID, others)  4.58 us
    ppermute x1, starting transfers between devices, per_device(): from_core = lax.ppermute(gathered, ('c',), [(0, 1), (1, 0)])  2.87 us
    ppermute x1, waiting for transfers between devices, per_device(): from_two = lax.ppermute(two, GRID, others)  2.18 us
    ppermute x1, starting transfers between devices, per_device(): lax.ppermute(smooth, SLAB, [(i, (i + 1) % 32) for i in range(32)])  1.54 us
  transfers between devices with their start and end apart: 5, of which 5 were waited for; matrix products, arithmetic and copies ran while one was open for 0% of the time, Pallas kernels for 0%

profile of v5, /device:TPU:1, one launch (start us, length us, event | category | flops | bytes accessed | tf_op | source)
XLA Modules:
  0.0 46.7 jit_solution(1021353994032897859)
XLA Ops:
  0.6 0.0 copy-start
  0.7 0.9 %slice_select_fusion = (f32[3,32,128]{2,1,0:T(8,128)S(1)}, f32[3,32,128]{2,1,0:T(8,128)S(1)}) fusion(f32[4,32,128]{2,1,0:T(8,128)} %param.3, pred[]{:T(512)S(6)} %eq.5), kind=kLoop, calls=%fused_computation.2 | loop fusion | flops 24576 | bytes 196609 | tf_op jit(solution)/shard_map/jit(_where)/select_n | solution.py:245
  1.5 0.0 copy-done
  1.6 4.6 %collective-permute-start.1 = (f32[224,128]{1,0:T(8,128)S(1)}, f32[224,128]{1,0:T(8,128)S(1)}, u32[]{:S(2)}, u32[]{:S(2)}) collective-permute-start(f32[224,128]{1,0:T(8,128)S(1)} %get-tuple-element.14.two), channel_id=1, source_target_pairs={{0,7},{1,2},{2,1},{3,4},{4,3},{5,6},{6,5},{7,0},{8,15},{9,10},{10,... | collective-permute-start | bytes 344072 | tf_op jit(solution)/shard_map/ppermute | solution.py:253
  6.2 0.0 collective-permute-start
  6.2 2.2 %collective-permute-done.1.from_two = f32[224,128]{1,0:T(8,128)S(1)} collective-permute-done((f32[224,128]{1,0:T(8,128)S(1)}, f32[224,128]{1,0:T(8,128)S(1)}, u32[]{:S(2)}, u32[]{:S(2)}) %collective-permute-start.1) | collective-permute-done | bytes 114720 | tf_op jit(solution)/shard_map/ppermute | solution.py:253
  8.3 1.5 %collective-permute-done.from_one = f32[224,128]{1,0:T(8,128)S(1)} collective-permute-done((f32[224,128]{1,0:T(8,128)S(1)}, f32[224,128]{1,0:T(8,128)S(1)}, u32[]{:S(2)}, u32[]{:S(2)}) %collective-permute-start) | collective-permute-done | bytes 114720 | tf_op jit(solution)/shard_map/ppermute | solution.py:252
  9.8 0.8 %shard_map.41 = (f32[128,128]{1,0:T(8,128)S(1)}, f32[16,5,4,128]{3,2,1,0:T(4,128)S(1)}) custom-call(f32[224,128]{1,0:T(8,128)S(1)} %get-tuple-element.15.one, f32[224,128]{1,0:T(8,128)S(1)} %get-tuple-element.14.two, f32[224,128]{1,0:T(8,128)S(1)} %collective-permute-done.from_one, f32[224,128]{1,0:T(8,128)S(1)} %collective-permute-done.1.from_two), custom_call_target="tpu_custom_call" | custom-call | flops 4000000 | bytes 458752 | tf_op jit(solution)/shard_map/pallas_call | solution.py:220
  10.6 12.1 %all_to_all.10.received = f32[16,5,4,128]{3,2,1,0:T(4,128)S(1)} all-to-all(f32[16,5,4,128]{3,2,1,0:T(4,128)S(1)} %get-tuple-element.8), channel_id=1, replica_groups=mesh['z'=8,'h'=2,'c'=2,'l'=2,'y'=4] {'h','l','y'}, dimensions={0} | all-to-all | bytes 327680 | tf_op jit(solution)/shard_map/all_to_all | solution.py:261
  22.6 2.9 %collective-permute-start.2 = (f32[16,5,4,128]{3,2,1,0:T(4,128)S(1)}, f32[16,5,4,128]{3,2,1,0:T(4,128)S(1)}, u32[]{:S(2)}, u32[]{:S(2)}) collective-permute-start(f32[16,5,4,128]{3,2,1,0:T(4,128)S(1)} %all_to_all.10.received), channel_id=1, source_target_pairs={{0,8},{8,0},{1,9},{9,1},{2,10},{10,2},{3,11},{11,3},{4,12},{12,4},... | collective-permute-start | bytes 491528 | tf_op jit(solution)/shard_map/ppermute | solution.py:262
  25.5 1.0 %collective-permute-done.2.from_core = f32[16,5,4,128]{3,2,1,0:T(4,128)S(1)} collective-permute-done((f32[16,5,4,128]{3,2,1,0:T(4,128)S(1)}, f32[16,5,4,128]{3,2,1,0:T(4,128)S(1)}, u32[]{:S(2)}, u32[]{:S(2)}) %collective-permute-start.2) | collective-permute-done | bytes 163872 | tf_op jit(solution)/shard_map/ppermute | solution.py:262
  26.5 5.5 %shard_map.42 = f32[8,32,128]{2,1,0:T(8,128)} custom-call(f32[16,5,4,128]{3,2,1,0:T(4,128)S(1)} %all_to_all.10.received, f32[16,5,4,128]{3,2,1,0:T(4,128)S(1)} %collective-permute-done.2.from_core), custom_call_target="tpu_custom_call" | custom-call | flops 12000000 | bytes 327680 | tf_op jit(solution)/shard_map/pallas_call | solution.py:220
  32.1 5.8 %all-to-all-start.1 = ((f32[8,32,128]{2,1,0:T(8,128)}), f32[8,32,128]{2,1,0:T(8,128)S(1)}, u32[]{:S(2)}, u32[]{:S(2)}) async-start(f32[8,32,128]{2,1,0:T(8,128)} %shard_map.42), calls=%async_computation.1 | async-start | bytes 262144 | tf_op jit(solution)/shard_map/all_to_all | solution.py:272
  37.8 1.5 %collective-permute-start.3 = (f32[128,128]{1,0:T(8,128)S(1)}, f32[128,128]{1,0:T(8,128)S(1)}, u32[]{:S(2)}, u32[]{:S(2)}) collective-permute-start(f32[128,128]{1,0:T(8,128)S(1)} %get-tuple-element.11.smooth), channel_id=1, source_target_pairs={{0,8},{8,16},{16,24},{24,32},{32,40},{40,48},{48,56},{56,64},{64,7... | collective-permute-start | bytes 196616 | tf_op jit(solution)/shard_map/ppermute | solution.py:271
  39.4 1.3 %collective-permute-done.3.smooth_before = f32[128,128]{1,0:T(8,128)S(1)} collective-permute-done((f32[128,128]{1,0:T(8,128)S(1)}, f32[128,128]{1,0:T(8,128)S(1)}, u32[]{:S(2)}, u32[]{:S(2)}) %collective-permute-start.3) | collective-permute-done | bytes 65568 | tf_op jit(solution)/shard_map/ppermute | solution.py:271
  40.7 5.3 %all-to-all-done.1.received = f32[8,32,128]{2,1,0:T(8,128)S(1)} async-done(((f32[8,32,128]{2,1,0:T(8,128)}), f32[8,32,128]{2,1,0:T(8,128)S(1)}, u32[]{:S(2)}, u32[]{:S(2)}) %all-to-all-start.1) | async-done | bytes 131104 | tf_op jit(solution)/shard_map/all_to_all | solution.py:272
  46.0 0.7 %shard_map.43 = (f32[128,128]{1,0:T(8,128)}, f32[128,128]{1,0:T(8,128)}) custom-call(f32[8,32,128]{2,1,0:T(8,128)S(1)} %all-to-all-done.1.received, f32[128,128]{1,0:T(8,128)S(1)} %get-tuple-element.11.smooth, f32[128,128]{1,0:T(8,128)S(1)} %collective-permute-done.3.smooth_before), custom_call_target="tpu_custom_call" | custom-call | flops 200000 | bytes 262144 | tf_op jit(solution)/shard_map/pallas_call | solution.py:220
  (1 shorter events, 0.0 us)
Async XLA Ops:
  0.6 0.9 %copy-start = (f32[1,4,32,128]{3,2,1,0:T(8,128)S(1)}, f32[1,4,32,128]{3,2,1,0:T(8,128)}, u32[]{:S(2)}) copy-start(f32[1,4,32,128]{3,2,1,0:T(8,128)} %param.2) | copy-start | bytes 196612
  1.6 6.8 %collective-permute-start.1 = (f32[224,128]{1,0:T(8,128)S(1)}, f32[224,128]{1,0:T(8,128)S(1)}, u32[]{:S(2)}, u32[]{:S(2)}) collective-permute-start(f32[224,128]{1,0:T(8,128)S(1)} %get-tuple-element.14.two), channel_id=1, source_target_pairs={{0,7},{1,2},{2,1},{3,4},{4,3},{5,6},{6,5},{7,0},{8,15},{9,10},{10,... | collective-permute-start | bytes 344072 | tf_op jit(solution)/shard_map/ppermute | solution.py:253
  6.2 3.6 %collective-permute-start = (f32[224,128]{1,0:T(8,128)S(1)}, f32[224,128]{1,0:T(8,128)S(1)}, u32[]{:S(2)}, u32[]{:S(2)}) collective-permute-start(f32[224,128]{1,0:T(8,128)S(1)} %get-tuple-element.15.one), channel_id=1, source_target_pairs={{0,1},{1,0},{2,3},{3,2},{4,5},{5,4},{6,7},{7,6},{8,9},{9,8},{10,11... | collective-permute-start | bytes 344072 | tf_op jit(solution)/shard_map/ppermute | solution.py:252
  22.6 3.9 %collective-permute-start.2 = (f32[16,5,4,128]{3,2,1,0:T(4,128)S(1)}, f32[16,5,4,128]{3,2,1,0:T(4,128)S(1)}, u32[]{:S(2)}, u32[]{:S(2)}) collective-permute-start(f32[16,5,4,128]{3,2,1,0:T(4,128)S(1)} %all_to_all.10.received), channel_id=1, source_target_pairs={{0,8},{8,0},{1,9},{9,1},{2,10},{10,2},{3,11},{11,3},{4,12},{12,4},... | collective-permute-start | bytes 491528 | tf_op jit(solution)/shard_map/ppermute | solution.py:262
  32.1 13.9 %all-to-all-start.1 = ((f32[8,32,128]{2,1,0:T(8,128)}), f32[8,32,128]{2,1,0:T(8,128)S(1)}, u32[]{:S(2)}, u32[]{:S(2)}) async-start(f32[8,32,128]{2,1,0:T(8,128)} %shard_map.42), calls=%async_computation.1 | async-start | bytes 262144 | tf_op jit(solution)/shard_map/all_to_all | solution.py:272
  37.8 2.9 %collective-permute-start.3 = (f32[128,128]{1,0:T(8,128)S(1)}, f32[128,128]{1,0:T(8,128)S(1)}, u32[]{:S(2)}, u32[]{:S(2)}) collective-permute-start(f32[128,128]{1,0:T(8,128)S(1)} %get-tuple-element.11.smooth), channel_id=1, source_target_pairs={{0,8},{8,16},{16,24},{24,32},{32,40},{40,48},{48,56},{56,64},{64,7... | collective-permute-start | bytes 196616 | tf_op jit(solution)/shard_map/ppermute | solution.py:271

commit v6 on v5

--- a/solution.py
+++ b/solution.py
@@ -130,65 +130,68 @@
     even = even_lanes()
     is_first_core = lax.axis_index("c") == 0
     depth = range(16)
-
-    def piece(source, part):
-        far, core, place = source
+    part = lax.axis_index("l") * 4 + lax.axis_index("y")
+    places = [lax.rem(part + i, 8) for i in range(8)]
+
+    def piece(far, core, layer, row):
         first, second = (received, from_core) if core == 0 else (from_core, received)
-        at = (8 * far + place, part)
+        at = (8 * far + places[layer // 2], row)
         return jnp.where(is_first_core, first[at], second[at])
-
-    def joined(first, second, part, next_part):
-        return jnp.concatenate([piece(first, part), piece(second, next_part)], axis=0)
 
     middle = 1.0
     for kind in (coarse_along_z, coarse_along_x, coarse_along_y):
         middle *= weights_of(kind)[1]
-    rates = [joined((z % 2, 0, z // 2), (z % 2, 1, z // 2), 4, 4) for z in depth]
+    rates = [jnp.concatenate([piece(z % 2, core, z, 4) for core in range(2)], axis=0) for z in depth]
     rates = [spread_pair(rate, even) for rate in rates]
     drops = [[1.0 - rate for rate in pair] for pair in rates]
     rates = [[middle * rate for rate in pair] for pair in rates]
 
     def term(step):
-        at = [((step // 2, step % 2, z // 2), 2 * (z % 2)) for z in depth]
-        return [joined(source, source, part, part + 1) for source, part in at]
+        far, core = step // 2, step % 2
+        rows = [[piece(far, core, z, 2 * (z % 2) + half) for half in range(2)] for z in depth]
+        return [spread_pair(jnp.concatenate(halves, axis=0), even) for halves in rows]
 
     def keep(step, layers):
-        for z in depth:
+        for z in range(2):
             history[step, z] = jnp.where(even, *layers[z])
 
-    def advance(layers):
-        flat = [pair_filter(pair) for pair in layers]
-        out = []
-        for z in depth:
-            behind, here, beyond = flat[z - 1], flat[z], flat[(z + 1) % 16]
+    def advance(layers, wanted):
+        needed = range(wanted[0] - 1, wanted[-1] + 2) if len(wanted) < 16 else wanted
+        flat = {z % 16: pair_filter(layers[z % 16]) for z in needed}
+        out = [None] * 16
+        for z in (z % 16 for z in wanted):
+            behind, here, beyond = flat[(z - 1) % 16], flat[z], flat[(z + 1) % 16]
             mixed = [scaled_filter(*trio, coarse_along_z) for trio in zip(behind, here, beyond)]
-            out.append([drops[z][i] * layers[z][i] + rates[z][i] * mixed[i] for i in range(2)])
+            out[z] = [drops[z][i] * layers[z][i] + rates[z][i] * mixed[i] for i in range(2)]
         return out
 
-    history[0] = jnp.zeros((16, 8, 128), jnp.float32)
-    layers = [spread_pair(v, even) for v in term(0)]
+    history[0] = jnp.zeros((2, 8, 128), jnp.float32)
+    layers = term(0)
     keep(1, layers)
     for step in range(1, GROUP):
-        added = [spread_pair(v, even) for v in term(step)]
-        layers = [[a + b for a, b in zip(*both)] for both in zip(advance(layers), added)]
+        later = advance(layers, depth)
+        layers = [[a + b for a, b in zip(*both)] for both in zip(later, term(step))]
         keep(step + 1, layers)
 
     def body(step, layers):
-        layers = advance(layers)
+        layers = advance(layers, depth)
         keep(step + 1, layers)
         return layers
 
     mine = lax.axis_index("z")
-    lax.fori_loop(GROUP, STEPS - GROUP * mine, body, layers)
+    stop = jnp.maximum(STEPS - GROUP * mine - GROUP, GROUP)
+    layers = lax.fori_loop(GROUP, stop, body, layers)
+    for i in range(GROUP):
+        layers = advance(layers, range(i - GROUP + 1, GROUP + 1 - i))
+        keep(stop + i + 1, layers)
     place = lax.axis_index("h") * 2 + lax.axis_index("c")
-    first = (lax.axis_index("l") * 4 + lax.axis_index("y")) * 2
     for target in range(8):
         begin = jnp.where(mine <= target, GROUP * (target - mine) + place, 0)
         finish = jnp.where(mine <= target, GROUP * (target - mine) + place + 1, 0)
         if target == 0:
             begin = jnp.where(place == 0, STEPS - GROUP * mine, begin)
-        send_out[target, 0:16] = history[begin, pl.ds(first, 2)].reshape(16, 128)
-        send_out[target, 16:32] = history[finish, pl.ds(first, 2)].reshape(16, 128)
+        send_out[target, 0:16] = history[begin].reshape(16, 128)
+        send_out[target, 16:32] = history[finish].reshape(16, 128)
 
 
 def add_spread(out, smooth, first, layer, even):
@@ -264,7 +267,7 @@
         chain_kernel,
         (gathered, from_core),
         array(8, 32, 128),
-        [scratch(STEPS + 1, 16, 8, 128)],
+        [scratch(STEPS + 1, 2, 8, 128)],
         12_000_000,
     )
     pieces, smooth = lax.optimization_barrier((pieces, smooth))

time: 47 us -> 46.7 us (level)
  no operation moved by 1% of the time
where the time goes in v6:
time: 46.7 us; the launch traced here: 46.5 us
  starting transfers between devices  14.7 us (31%)
  blocking collectives  12.1 us (26%)
  waiting for transfers between devices  11.3 us (24%)
  Pallas kernels  6.76 us (14%)
  other arithmetic  0.9 us (2%)
  between operations  0.67 us (1%)
    all_to_all x1, blocking collectives, per_device(): gathered = lax.all_to_all(message, CORES, 0, 0, tiled=True)  12.1 us
    pallas_call x3, Pallas kernels, local(): pl.pallas_call(kernel, out_shape=outputs, in_specs=[pl.BlockSpec(memory_s...  6.76 us
    all_to_all x1, starting transfers between devices, per_device(): shares = lax.all_to_all(pieces, ('z',), 0, 0, tiled=True)  5.74 us
    all_to_all x1, waiting for transfers between devices, per_device(): shares = lax.all_to_all(pieces, ('z',), 0, 0, tiled=True)  5.3 us
    ppermute x1, starting transfers between devices, per_device(): from_two = lax.ppermute(two, GRID, others)  4.58 us
    ppermute x1, starting transfers between devices, per_device(): from_core = lax.ppermute(gathered, ('c',), [(0, 1), (1, 0)])  2.87 us
    ppermute x1, waiting for transfers between devices, per_device(): from_two = lax.ppermute(two, GRID, others)  2.18 us
    ppermute x1, starting transfers between devices, per_device(): lax.ppermute(smooth, SLAB, [(i, (i + 1) % 32) for i in range(32)])  1.54 us
  transfers between devices with their start and end apart: 5, of which 5 were waited for; matrix products, arithmetic and copies ran while one was open for 0% of the time, Pallas kernels for 0%

profile of v6, /device:TPU:1, one launch (start us, length us, event | category | flops | bytes accessed | tf_op | source)
XLA Modules:
  0.0 46.5 jit_solution(15687900434203373843)
XLA Ops:
  0.6 0.0 copy-start
  0.7 0.9 %slice_select_fusion = (f32[3,32,128]{2,1,0:T(8,128)S(1)}, f32[3,32,128]{2,1,0:T(8,128)S(1)}) fusion(f32[4,32,128]{2,1,0:T(8,128)} %param.3, pred[]{:T(512)S(6)} %eq.5), kind=kLoop, calls=%fused_computation.2 | loop fusion | flops 24576 | bytes 196609 | tf_op jit(solution)/shard_map/jit(_where)/select_n | solution.py:248
  1.5 0.0 copy-done
  1.6 4.6 %collective-permute-start.1 = (f32[224,128]{1,0:T(8,128)S(1)}, f32[224,128]{1,0:T(8,128)S(1)}, u32[]{:S(2)}, u32[]{:S(2)}) collective-permute-start(f32[224,128]{1,0:T(8,128)S(1)} %get-tuple-element.14.two), channel_id=1, source_target_pairs={{0,7},{1,2},{2,1},{3,4},{4,3},{5,6},{6,5},{7,0},{8,15},{9,10},{10,... | collective-permute-start | bytes 344072 | tf_op jit(solution)/shard_map/ppermute | solution.py:256
  6.2 0.0 collective-permute-start
  6.2 2.2 %collective-permute-done.1.from_two = f32[224,128]{1,0:T(8,128)S(1)} collective-permute-done((f32[224,128]{1,0:T(8,128)S(1)}, f32[224,128]{1,0:T(8,128)S(1)}, u32[]{:S(2)}, u32[]{:S(2)}) %collective-permute-start.1) | collective-permute-done | bytes 114720 | tf_op jit(solution)/shard_map/ppermute | solution.py:256
  8.3 1.5 %collective-permute-done.from_one = f32[224,128]{1,0:T(8,128)S(1)} collective-permute-done((f32[224,128]{1,0:T(8,128)S(1)}, f32[224,128]{1,0:T(8,128)S(1)}, u32[]{:S(2)}, u32[]{:S(2)}) %collective-permute-start) | collective-permute-done | bytes 114720 | tf_op jit(solution)/shard_map/ppermute | solution.py:255
  9.8 0.8 %shard_map.41 = (f32[128,128]{1,0:T(8,128)S(1)}, f32[16,5,4,128]{3,2,1,0:T(4,128)S(1)}) custom-call(f32[224,128]{1,0:T(8,128)S(1)} %get-tuple-element.15.one, f32[224,128]{1,0:T(8,128)S(1)} %get-tuple-element.14.two, f32[224,128]{1,0:T(8,128)S(1)} %collective-permute-done.from_one, f32[224,128]{1,0:T(8,128)S(1)} %collective-permute-done.1.from_two), custom_call_target="tpu_custom_call" | custom-call | flops 4000000 | bytes 458752 | tf_op jit(solution)/shard_map/pallas_call | solution.py:223
  10.6 12.1 %all_to_all.10.received = f32[16,5,4,128]{3,2,1,0:T(4,128)S(1)} all-to-all(f32[16,5,4,128]{3,2,1,0:T(4,128)S(1)} %get-tuple-element.8), channel_id=1, replica_groups=mesh['z'=8,'h'=2,'c'=2,'l'=2,'y'=4] {'h','l','y'}, dimensions={0} | all-to-all | bytes 327680 | tf_op jit(solution)/shard_map/all_to_all | solution.py:264
  22.6 2.9 %collective-permute-start.2 = (f32[16,5,4,128]{3,2,1,0:T(4,128)S(1)}, f32[16,5,4,128]{3,2,1,0:T(4,128)S(1)}, u32[]{:S(2)}, u32[]{:S(2)}) collective-permute-start(f32[16,5,4,128]{3,2,1,0:T(4,128)S(1)} %all_to_all.10.received), channel_id=1, source_target_pairs={{0,8},{8,0},{1,9},{9,1},{2,10},{10,2},{3,11},{11,3},{4,12},{12,4},... | collective-permute-start | bytes 491528 | tf_op jit(solution)/shard_map/ppermute | solution.py:265
  25.5 1.0 %collective-permute-done.2.from_core = f32[16,5,4,128]{3,2,1,0:T(4,128)S(1)} collective-permute-done((f32[16,5,4,128]{3,2,1,0:T(4,128)S(1)}, f32[16,5,4,128]{3,2,1,0:T(4,128)S(1)}, u32[]{:S(2)}, u32[]{:S(2)}) %collective-permute-start.2) | collective-permute-done | bytes 163872 | tf_op jit(solution)/shard_map/ppermute | solution.py:265
  26.5 5.3 %shard_map.42 = f32[8,32,128]{2,1,0:T(8,128)} custom-call(f32[16,5,4,128]{3,2,1,0:T(4,128)S(1)} %all_to_all.10.received, f32[16,5,4,128]{3,2,1,0:T(4,128)S(1)} %collective-permute-done.2.from_core), custom_call_target="tpu_custom_call" | custom-call | flops 12000000 | bytes 327680 | tf_op jit(solution)/shard_map/pallas_call | solution.py:223
  31.8 5.7 %all-to-all-start.1 = ((f32[8,32,128]{2,1,0:T(8,128)}), f32[8,32,128]{2,1,0:T(8,128)S(1)}, u32[]{:S(2)}, u32[]{:S(2)}) async-start(f32[8,32,128]{2,1,0:T(8,128)} %shard_map.42), calls=%async_computation.1 | async-start | bytes 262144 | tf_op jit(solution)/shard_map/all_to_all | solution.py:275
  37.6 1.5 %collective-permute-start.3 = (f32[128,128]{1,0:T(8,128)S(1)}, f32[128,128]{1,0:T(8,128)S(1)}, u32[]{:S(2)}, u32[]{:S(2)}) collective-permute-start(f32[128,128]{1,0:T(8,128)S(1)} %get-tuple-element.11.smooth), channel_id=1, source_target_pairs={{0,8},{8,16},{16,24},{24,32},{32,40},{40,48},{48,56},{56,64},{64,7... | collective-permute-start | bytes 196616 | tf_op jit(solution)/shard_map/ppermute | solution.py:274
  39.1 1.3 %collective-permute-done.3.smooth_before = f32[128,128]{1,0:T(8,128)S(1)} collective-permute-done((f32[128,128]{1,0:T(8,128)S(1)}, f32[128,128]{1,0:T(8,128)S(1)}, u32[]{:S(2)}, u32[]{:S(2)}) %collective-permute-start.3) | collective-permute-done | bytes 65568 | tf_op jit(solution)/shard_map/ppermute | solution.py:274
  40.4 5.3 %all-to-all-done.1.received = f32[8,32,128]{2,1,0:T(8,128)S(1)} async-done(((f32[8,32,128]{2,1,0:T(8,128)}), f32[8,32,128]{2,1,0:T(8,128)S(1)}, u32[]{:S(2)}, u32[]{:S(2)}) %all-to-all-start.1) | async-done | bytes 131104 | tf_op jit(solution)/shard_map/all_to_all | solution.py:275
  45.7 0.7 %shard_map.43 = (f32[128,128]{1,0:T(8,128)}, f32[128,128]{1,0:T(8,128)}) custom-call(f32[8,32,128]{2,1,0:T(8,128)S(1)} %all-to-all-done.1.received, f32[128,128]{1,0:T(8,128)S(1)} %get-tuple-element.11.smooth, f32[128,128]{1,0:T(8,128)S(1)} %collective-permute-done.3.smooth_before), custom_call_target="tpu_custom_call" | custom-call | flops 200000 | bytes 262144 | tf_op jit(solution)/shard_map/pallas_call | solution.py:223
  (1 shorter events, 0.0 us)
Async XLA Ops:
  0.6 0.9 %copy-start = (f32[1,4,32,128]{3,2,1,0:T(8,128)S(1)}, f32[1,4,32,128]{3,2,1,0:T(8,128)}, u32[]{:S(2)}) copy-start(f32[1,4,32,128]{3,2,1,0:T(8,128)} %param.2) | copy-start | bytes 196612
  1.6 6.8 %collective-permute-start.1 = (f32[224,128]{1,0:T(8,128)S(1)}, f32[224,128]{1,0:T(8,128)S(1)}, u32[]{:S(2)}, u32[]{:S(2)}) collective-permute-start(f32[224,128]{1,0:T(8,128)S(1)} %get-tuple-element.14.two), channel_id=1, source_target_pairs={{0,7},{1,2},{2,1},{3,4},{4,3},{5,6},{6,5},{7,0},{8,15},{9,10},{10,... | collective-permute-start | bytes 344072 | tf_op jit(solution)/shard_map/ppermute | solution.py:256
  6.2 3.6 %collective-permute-start = (f32[224,128]{1,0:T(8,128)S(1)}, f32[224,128]{1,0:T(8,128)S(1)}, u32[]{:S(2)}, u32[]{:S(2)}) collective-permute-start(f32[224,128]{1,0:T(8,128)S(1)} %get-tuple-element.15.one), channel_id=1, source_target_pairs={{0,1},{1,0},{2,3},{3,2},{4,5},{5,4},{6,7},{7,6},{8,9},{9,8},{10,11... | collective-permute-start | bytes 344072 | tf_op jit(solution)/shard_map/ppermute | solution.py:255
  22.6 3.9 %collective-permute-start.2 = (f32[16,5,4,128]{3,2,1,0:T(4,128)S(1)}, f32[16,5,4,128]{3,2,1,0:T(4,128)S(1)}, u32[]{:S(2)}, u32[]{:S(2)}) collective-permute-start(f32[16,5,4,128]{3,2,1,0:T(4,128)S(1)} %all_to_all.10.received), channel_id=1, source_target_pairs={{0,8},{8,0},{1,9},{9,1},{2,10},{10,2},{3,11},{11,3},{4,12},{12,4},... | collective-permute-start | bytes 491528 | tf_op jit(solution)/shard_map/ppermute | solution.py:265
  31.8 13.9 %all-to-all-start.1 = ((f32[8,32,128]{2,1,0:T(8,128)}), f32[8,32,128]{2,1,0:T(8,128)S(1)}, u32[]{:S(2)}, u32[]{:S(2)}) async-start(f32[8,32,128]{2,1,0:T(8,128)} %shard_map.42), calls=%async_computation.1 | async-start | bytes 262144 | tf_op jit(solution)/shard_map/all_to_all | solution.py:275
  37.6 2.9 %collective-permute-start.3 = (f32[128,128]{1,0:T(8,128)S(1)}, f32[128,128]{1,0:T(8,128)S(1)}, u32[]{:S(2)}, u32[]{:S(2)}) collective-permute-start(f32[128,128]{1,0:T(8,128)S(1)} %get-tuple-element.11.smooth), channel_id=1, source_target_pairs={{0,8},{8,16},{16,24},{24,32},{32,40},{40,48},{48,56},{56,64},{64,7... | collective-permute-start | bytes 196616 | tf_op jit(solution)/shard_map/ppermute | solution.py:274

commit v7 on v6

--- a/solution.py
+++ b/solution.py
@@ -64,7 +64,7 @@
     return 0.125 * jnp.where(even, low + pltpu.roll(low, 127, 1), high + pltpu.roll(high, 1, 1))
 
 
-def fine_kernel(one, two, from_one, from_two, smooth_out, send_out, wide, ends, all_rates, rates):
+def fine_kernel(one, two, from_one, from_two, ends, send_out, wide, all_rates, rates):
     even = even_lanes()
     is_first = (lax.axis_index("z") == 0) & (lax.axis_index("h") == 0) & (lax.axis_index("c") == 0)
     is_even = lax.axis_index("y") % 2 == 0
@@ -102,7 +102,6 @@
         guess = coarse[i + 1] + coarse_rates[i] * (mixed - coarse[i + 1])
         end = packed_layer(ends, 64 * i, even)
         terms.append(end - jnp.where(is_first, jnp.zeros_like(guess), guess))
-        add_spread(smooth_out, ends, 64 * i, -end, even)
     layer = jnp.where(lax.axis_index("h") == 0, coarse_rates[0], coarse_rates[1])
     layer = jnp.where(lax.axis_index("c") == 0, layer, pltpu.roll(layer, 4, 0))
     for i in range(2):
@@ -209,8 +208,10 @@
     for source in range(1, 8):
         total = total + received[source]
     for i in range(2):
-        add_spread(starts_out, smooth_before, 64 * i, total[8 * i : 8 * i + 8], even)
-        add_spread(ends_out, smooth, 64 * i, total[16 + 8 * i : 24 + 8 * i], even)
+        before = total[8 * i : 8 * i + 8] - packed_layer(smooth_before, 64 * i, even)
+        own = total[16 + 8 * i : 24 + 8 * i] - packed_layer(smooth, 64 * i, even)
+        add_spread(starts_out, smooth_before, 64 * i, before, even)
+        add_spread(ends_out, smooth, 64 * i, own, even)
 
 
 def array(*shape):
@@ -258,7 +259,7 @@
         fine_kernel,
         (one, two, from_one, from_two),
         (array(128, 128), array(16, 5, 4, 128)),
-        [scratch(384, 128), scratch(128, 128), scratch(320, 128), scratch(128, 128)],
+        [scratch(384, 128), scratch(320, 128), scratch(128, 128)],
         4_000_000,
     )
     gathered = lax.all_to_all(message, CORES, 0, 0, tiled=True)

time: 46.7 us -> 46.8 us (level)
  no operation moved by 1% of the time
where the time goes in v7:
time: 46.8 us; the launch traced here: 46.5 us
  starting transfers between devices  14.7 us (31%)
  blocking collectives  12.1 us (26%)
  waiting for transfers between devices  11.3 us (24%)
  Pallas kernels  6.77 us (14%)
  other arithmetic  0.9 us (2%)
  between operations  0.68 us (1%)
    all_to_all x1, blocking collectives, per_device(): gathered = lax.all_to_all(message, CORES, 0, 0, tiled=True)  12.1 us
    pallas_call x3, Pallas kernels, local(): pl.pallas_call(kernel, out_shape=outputs, in_specs=[pl.BlockSpec(memory_s...  6.77 us
    all_to_all x1, starting transfers between devices, per_device(): shares = lax.all_to_all(pieces, ('z',), 0, 0, tiled=True)  5.74 us
    all_to_all x1, waiting for transfers between devices, per_device(): shares = lax.all_to_all(pieces, ('z',), 0, 0, tiled=True)  5.3 us
    ppermute x1, starting transfers between devices, per_device(): from_two = lax.ppermute(two, GRID, others)  4.58 us
    ppermute x1, starting transfers between devices, per_device(): from_core = lax.ppermute(gathered, ('c',), [(0, 1), (1, 0)])  2.87 us
    ppermute x1, waiting for transfers between devices, per_device(): from_two = lax.ppermute(two, GRID, others)  2.18 us
    ppermute x1, starting transfers between devices, per_device(): lax.ppermute(smooth, SLAB, [(i, (i + 1) % 32) for i in range(32)])  1.54 us
  transfers between devices with their start and end apart: 5, of which 5 were waited for; matrix products, arithmetic and copies ran while one was open for 0% of the time, Pallas kernels for 0%

profile of v7, /device:TPU:1, one launch (start us, length us, event | category | flops | bytes accessed | tf_op | source)
XLA Modules:
  0.0 46.5 jit_solution(511868861098324909)
XLA Ops:
  0.6 0.0 copy-start
  0.7 0.9 %slice_select_fusion = (f32[3,32,128]{2,1,0:T(8,128)S(1)}, f32[3,32,128]{2,1,0:T(8,128)S(1)}) fusion(f32[4,32,128]{2,1,0:T(8,128)} %param.3, pred[]{:T(512)S(6)} %eq.5), kind=kLoop, calls=%fused_computation.2 | loop fusion | flops 24576 | bytes 196609 | tf_op jit(solution)/shard_map/jit(_where)/select_n | solution.py:249
  1.5 0.0 copy-done
  1.6 4.6 %collective-permute-start.1 = (f32[224,128]{1,0:T(8,128)S(1)}, f32[224,128]{1,0:T(8,128)S(1)}, u32[]{:S(2)}, u32[]{:S(2)}) collective-permute-start(f32[224,128]{1,0:T(8,128)S(1)} %get-tuple-element.14.two), channel_id=1, source_target_pairs={{0,7},{1,2},{2,1},{3,4},{4,3},{5,6},{6,5},{7,0},{8,15},{9,10},{10,... | collective-permute-start | bytes 344072 | tf_op jit(solution)/shard_map/ppermute | solution.py:257
  6.2 0.0 collective-permute-start
  6.2 2.2 %collective-permute-done.1.from_two = f32[224,128]{1,0:T(8,128)S(1)} collective-permute-done((f32[224,128]{1,0:T(8,128)S(1)}, f32[224,128]{1,0:T(8,128)S(1)}, u32[]{:S(2)}, u32[]{:S(2)}) %collective-permute-start.1) | collective-permute-done | bytes 114720 | tf_op jit(solution)/shard_map/ppermute | solution.py:257
  8.3 1.5 %collective-permute-done.from_one = f32[224,128]{1,0:T(8,128)S(1)} collective-permute-done((f32[224,128]{1,0:T(8,128)S(1)}, f32[224,128]{1,0:T(8,128)S(1)}, u32[]{:S(2)}, u32[]{:S(2)}) %collective-permute-start) | collective-permute-done | bytes 114720 | tf_op jit(solution)/shard_map/ppermute | solution.py:256
  9.8 0.7 %shard_map.41 = (f32[128,128]{1,0:T(8,128)S(1)}, f32[16,5,4,128]{3,2,1,0:T(4,128)S(1)}) custom-call(f32[224,128]{1,0:T(8,128)S(1)} %get-tuple-element.15.one, f32[224,128]{1,0:T(8,128)S(1)} %get-tuple-element.14.two, f32[224,128]{1,0:T(8,128)S(1)} %collective-permute-done.from_one, f32[224,128]{1,0:T(8,128)S(1)} %collective-permute-done.1.from_two), custom_call_target="tpu_custom_call" | custom-call | flops 4000000 | bytes 458752 | tf_op jit(solution)/shard_map/pallas_call | solution.py:224
  10.5 12.1 %all_to_all.10.received = f32[16,5,4,128]{3,2,1,0:T(4,128)S(1)} all-to-all(f32[16,5,4,128]{3,2,1,0:T(4,128)S(1)} %get-tuple-element.8), channel_id=1, replica_groups=mesh['z'=8,'h'=2,'c'=2,'l'=2,'y'=4] {'h','l','y'}, dimensions={0} | all-to-all | bytes 327680 | tf_op jit(solution)/shard_map/all_to_all | solution.py:265
  22.6 2.9 %collective-permute-start.2 = (f32[16,5,4,128]{3,2,1,0:T(4,128)S(1)}, f32[16,5,4,128]{3,2,1,0:T(4,128)S(1)}, u32[]{:S(2)}, u32[]{:S(2)}) collective-permute-start(f32[16,5,4,128]{3,2,1,0:T(4,128)S(1)} %all_to_all.10.received), channel_id=1, source_target_pairs={{0,8},{8,0},{1,9},{9,1},{2,10},{10,2},{3,11},{11,3},{4,12},{12,4},... | collective-permute-start | bytes 491528 | tf_op jit(solution)/shard_map/ppermute | solution.py:266
  25.5 1.0 %collective-permute-done.2.from_core = f32[16,5,4,128]{3,2,1,0:T(4,128)S(1)} collective-permute-done((f32[16,5,4,128]{3,2,1,0:T(4,128)S(1)}, f32[16,5,4,128]{3,2,1,0:T(4,128)S(1)}, u32[]{:S(2)}, u32[]{:S(2)}) %collective-permute-start.2) | collective-permute-done | bytes 163872 | tf_op jit(solution)/shard_map/ppermute | solution.py:266
  26.5 5.3 %shard_map.42 = f32[8,32,128]{2,1,0:T(8,128)} custom-call(f32[16,5,4,128]{3,2,1,0:T(4,128)S(1)} %all_to_all.10.received, f32[16,5,4,128]{3,2,1,0:T(4,128)S(1)} %collective-permute-done.2.from_core), custom_call_target="tpu_custom_call" | custom-call | flops 12000000 | bytes 327680 | tf_op jit(solution)/shard_map/pallas_call | solution.py:224
  31.8 5.7 %all-to-all-start.1 = ((f32[8,32,128]{2,1,0:T(8,128)}), f32[8,32,128]{2,1,0:T(8,128)S(1)}, u32[]{:S(2)}, u32[]{:S(2)}) async-start(f32[8,32,128]{2,1,0:T(8,128)} %shard_map.42), calls=%async_computation.1 | async-start | bytes 262144 | tf_op jit(solution)/shard_map/all_to_all | solution.py:276
  37.5 1.5 %collective-permute-start.3 = (f32[128,128]{1,0:T(8,128)S(1)}, f32[128,128]{1,0:T(8,128)S(1)}, u32[]{:S(2)}, u32[]{:S(2)}) collective-permute-start(f32[128,128]{1,0:T(8,128)S(1)} %get-tuple-element.11.smooth), channel_id=1, source_target_pairs={{0,8},{8,16},{16,24},{24,32},{32,40},{40,48},{48,56},{56,64},{64,7... | collective-permute-start | bytes 196616 | tf_op jit(solution)/shard_map/ppermute | solution.py:275
  39.1 1.3 %collective-permute-done.3.smooth_before = f32[128,128]{1,0:T(8,128)S(1)} collective-permute-done((f32[128,128]{1,0:T(8,128)S(1)}, f32[128,128]{1,0:T(8,128)S(1)}, u32[]{:S(2)}, u32[]{:S(2)}) %collective-permute-start.3) | collective-permute-done | bytes 65568 | tf_op jit(solution)/shard_map/ppermute | solution.py:275
  40.4 5.3 %all-to-all-done.1.received = f32[8,32,128]{2,1,0:T(8,128)S(1)} async-done(((f32[8,32,128]{2,1,0:T(8,128)}), f32[8,32,128]{2,1,0:T(8,128)S(1)}, u32[]{:S(2)}, u32[]{:S(2)}) %all-to-all-start.1) | async-done | bytes 131104 | tf_op jit(solution)/shard_map/all_to_all | solution.py:276
  45.7 0.8 %shard_map.43 = (f32[128,128]{1,0:T(8,128)}, f32[128,128]{1,0:T(8,128)}) custom-call(f32[8,32,128]{2,1,0:T(8,128)S(1)} %all-to-all-done.1.received, f32[128,128]{1,0:T(8,128)S(1)} %get-tuple-element.11.smooth, f32[128,128]{1,0:T(8,128)S(1)} %collective-permute-done.3.smooth_before), custom_call_target="tpu_custom_call" | custom-call | flops 200000 | bytes 262144 | tf_op jit(solution)/shard_map/pallas_call | solution.py:224
  (1 shorter events, 0.0 us)
Async XLA Ops:
  0.6 0.9 %copy-start = (f32[1,4,32,128]{3,2,1,0:T(8,128)S(1)}, f32[1,4,32,128]{3,2,1,0:T(8,128)}, u32[]{:S(2)}) copy-start(f32[1,4,32,128]{3,2,1,0:T(8,128)} %param.2) | copy-start | bytes 196612
  1.6 6.8 %collective-permute-start.1 = (f32[224,128]{1,0:T(8,128)S(1)}, f32[224,128]{1,0:T(8,128)S(1)}, u32[]{:S(2)}, u32[]{:S(2)}) collective-permute-start(f32[224,128]{1,0:T(8,128)S(1)} %get-tuple-element.14.two), channel_id=1, source_target_pairs={{0,7},{1,2},{2,1},{3,4},{4,3},{5,6},{6,5},{7,0},{8,15},{9,10},{10,... | collective-permute-start | bytes 344072 | tf_op jit(solution)/shard_map/ppermute | solution.py:257
  6.2 3.6 %collective-permute-start = (f32[224,128]{1,0:T(8,128)S(1)}, f32[224,128]{1,0:T(8,128)S(1)}, u32[]{:S(2)}, u32[]{:S(2)}) collective-permute-start(f32[224,128]{1,0:T(8,128)S(1)} %get-tuple-element.15.one), channel_id=1, source_target_pairs={{0,1},{1,0},{2,3},{3,2},{4,5},{5,4},{6,7},{7,6},{8,9},{9,8},{10,11... | collective-permute-start | bytes 344072 | tf_op jit(solution)/shard_map/ppermute | solution.py:256
  22.6 3.9 %collective-permute-start.2 = (f32[16,5,4,128]{3,2,1,0:T(4,128)S(1)}, f32[16,5,4,128]{3,2,1,0:T(4,128)S(1)}, u32[]{:S(2)}, u32[]{:S(2)}) collective-permute-start(f32[16,5,4,128]{3,2,1,0:T(4,128)S(1)} %all_to_all.10.received), channel_id=1, source_target_pairs={{0,8},{8,0},{1,9},{9,1},{2,10},{10,2},{3,11},{11,3},{4,12},{12,4},... | collective-permute-start | bytes 491528 | tf_op jit(solution)/shard_map/ppermute | solution.py:266
  31.8 13.9 %all-to-all-start.1 = ((f32[8,32,128]{2,1,0:T(8,128)}), f32[8,32,128]{2,1,0:T(8,128)S(1)}, u32[]{:S(2)}, u32[]{:S(2)}) async-start(f32[8,32,128]{2,1,0:T(8,128)} %shard_map.42), calls=%async_computation.1 | async-start | bytes 262144 | tf_op jit(solution)/shard_map/all_to_all | solution.py:276
  37.5 2.9 %collective-permute-start.3 = (f32[128,128]{1,0:T(8,128)S(1)}, f32[128,128]{1,0:T(8,128)S(1)}, u32[]{:S(2)}, u32[]{:S(2)}) collective-permute-start(f32[128,128]{1,0:T(8,128)S(1)} %get-tuple-element.11.smooth), channel_id=1, source_target_pairs={{0,8},{8,16},{16,24},{24,32},{32,40},{40,48},{48,56},{56,64},{64,7... | collective-permute-start | bytes 196616 | tf_op jit(solution)/shard_map/ppermute | solution.py:275

commit v8 on v6

--- a/solution.py
+++ b/solution.py
@@ -143,8 +143,6 @@
         middle *= weights_of(kind)[1]
     rates = [jnp.concatenate([piece(z % 2, core, z, 4) for core in range(2)], axis=0) for z in depth]
     rates = [spread_pair(rate, even) for rate in rates]
-    drops = [[1.0 - rate for rate in pair] for pair in rates]
-    rates = [[middle * rate for rate in pair] for pair in rates]
 
     def term(step):
         far, core = step // 2, step % 2
@@ -162,7 +160,9 @@
         for z in (z % 16 for z in wanted):
             behind, here, beyond = flat[(z - 1) % 16], flat[z], flat[(z + 1) % 16]
             mixed = [scaled_filter(*trio, coarse_along_z) for trio in zip(behind, here, beyond)]
-            out[z] = [drops[z][i] * layers[z][i] + rates[z][i] * mixed[i] for i in range(2)]
+            out[z] = [
+                layers[z][i] + rates[z][i] * (middle * mixed[i] - layers[z][i]) for i in range(2)
+            ]
         return out
 
     history[0] = jnp.zeros((2, 8, 128), jnp.float32)
@@ -173,14 +173,15 @@
         layers = [[a + b for a, b in zip(*both)] for both in zip(later, term(step))]
         keep(step + 1, layers)
 
-    def body(step, layers):
-        layers = advance(layers, depth)
-        keep(step + 1, layers)
+    def body(turn, layers):
+        for step in (GROUP + 2 * turn, GROUP + 2 * turn + 1):
+            layers = advance(layers, depth)
+            keep(step + 1, layers)
         return layers
 
     mine = lax.axis_index("z")
     stop = jnp.maximum(STEPS - GROUP * mine - GROUP, GROUP)
-    layers = lax.fori_loop(GROUP, stop, body, layers)
+    layers = lax.fori_loop(0, (stop - GROUP) // 2, body, layers)
     for i in range(GROUP):
         layers = advance(layers, range(i - GROUP + 1, GROUP + 1 - i))
         keep(stop + i + 1, layers)

time: 46.7 us -> 46.7 us (level)
  no operation moved by 1% of the time
where the time goes in v8:
time: 46.7 us; the launch traced here: 46.4 us
  starting transfers between devices  14.9 us (32%)
  blocking collectives  12.1 us (26%)
  waiting for transfers between devices  11.3 us (24%)
  Pallas kernels  6.5 us (14%)
  other arithmetic  0.9 us (2%)
  between operations  0.67 us (1%)
    all_to_all x1, blocking collectives, per_device(): gathered = lax.all_to_all(message, CORES, 0, 0, tiled=True)  12.1 us
    pallas_call x3, Pallas kernels, local(): pl.pallas_call(kernel, out_shape=outputs, in_specs=[pl.BlockSpec(memory_s...  6.5 us
    all_to_all x1, starting transfers between devices, per_device(): shares = lax.all_to_all(pieces, ('z',), 0, 0, tiled=True)  5.93 us
    all_to_all x1, waiting for transfers between devices, per_device(): shares = lax.all_to_all(pieces, ('z',), 0, 0, tiled=True)  5.3 us
    ppermute x1, starting transfers between devices, per_device(): from_two = lax.ppermute(two, GRID, others)  4.58 us
    ppermute x1, starting transfers between devices, per_device(): from_core = lax.ppermute(gathered, ('c',), [(0, 1), (1, 0)])  2.87 us
    ppermute x1, waiting for transfers between devices, per_device(): from_two = lax.ppermute(two, GRID, others)  2.18 us
    ppermute x1, starting transfers between devices, per_device(): lax.ppermute(smooth, SLAB, [(i, (i + 1) % 32) for i in range(32)])  1.54 us
  transfers between devices with their start and end apart: 5, of which 5 were waited for; matrix products, arithmetic and copies ran while one was open for 0% of the time, Pallas kernels for 0%

profile of v8, /device:TPU:1, one launch (start us, length us, event | category | flops | bytes accessed | tf_op | source)
XLA Modules:
  0.0 46.4 jit_solution(5760114526302761047)
XLA Ops:
  0.6 0.0 copy-start
  0.7 0.9 %slice_select_fusion = (f32[3,32,128]{2,1,0:T(8,128)S(1)}, f32[3,32,128]{2,1,0:T(8,128)S(1)}) fusion(f32[4,32,128]{2,1,0:T(8,128)} %param.3, pred[]{:T(512)S(6)} %eq.5), kind=kLoop, calls=%fused_computation.2 | loop fusion | flops 24576 | bytes 196609 | tf_op jit(solution)/shard_map/jit(_where)/select_n | solution.py:249
  1.5 0.0 copy-done
  1.6 4.6 %collective-permute-start.1 = (f32[224,128]{1,0:T(8,128)S(1)}, f32[224,128]{1,0:T(8,128)S(1)}, u32[]{:S(2)}, u32[]{:S(2)}) collective-permute-start(f32[224,128]{1,0:T(8,128)S(1)} %get-tuple-element.14.two), channel_id=1, source_target_pairs={{0,7},{1,2},{2,1},{3,4},{4,3},{5,6},{6,5},{7,0},{8,15},{9,10},{10,... | collective-permute-start | bytes 344072 | tf_op jit(solution)/shard_map/ppermute | solution.py:257
  6.2 0.0 collective-permute-start
  6.2 2.2 %collective-permute-done.1.from_two = f32[224,128]{1,0:T(8,128)S(1)} collective-permute-done((f32[224,128]{1,0:T(8,128)S(1)}, f32[224,128]{1,0:T(8,128)S(1)}, u32[]{:S(2)}, u32[]{:S(2)}) %collective-permute-start.1) | collective-permute-done | bytes 114720 | tf_op jit(solution)/shard_map/ppermute | solution.py:257
  8.3 1.5 %collective-permute-done.from_one = f32[224,128]{1,0:T(8,128)S(1)} collective-permute-done((f32[224,128]{1,0:T(8,128)S(1)}, f32[224,128]{1,0:T(8,128)S(1)}, u32[]{:S(2)}, u32[]{:S(2)}) %collective-permute-start) | collective-permute-done | bytes 114720 | tf_op jit(solution)/shard_map/ppermute | solution.py:256
  9.8 0.8 %shard_map.41 = (f32[128,128]{1,0:T(8,128)S(1)}, f32[16,5,4,128]{3,2,1,0:T(4,128)S(1)}) custom-call(f32[224,128]{1,0:T(8,128)S(1)} %get-tuple-element.15.one, f32[224,128]{1,0:T(8,128)S(1)} %get-tuple-element.14.two, f32[224,128]{1,0:T(8,128)S(1)} %collective-permute-done.from_one, f32[224,128]{1,0:T(8,128)S(1)} %collective-permute-done.1.from_two), custom_call_target="tpu_custom_call" | custom-call | flops 4000000 | bytes 458752 | tf_op jit(solution)/shard_map/pallas_call | solution.py:224
  10.6 12.1 %all_to_all.10.received = f32[16,5,4,128]{3,2,1,0:T(4,128)S(1)} all-to-all(f32[16,5,4,128]{3,2,1,0:T(4,128)S(1)} %get-tuple-element.8), channel_id=1, replica_groups=mesh['z'=8,'h'=2,'c'=2,'l'=2,'y'=4] {'h','l','y'}, dimensions={0} | all-to-all | bytes 327680 | tf_op jit(solution)/shard_map/all_to_all | solution.py:265
  22.6 2.9 %collective-permute-start.2 = (f32[16,5,4,128]{3,2,1,0:T(4,128)S(1)}, f32[16,5,4,128]{3,2,1,0:T(4,128)S(1)}, u32[]{:S(2)}, u32[]{:S(2)}) collective-permute-start(f32[16,5,4,128]{3,2,1,0:T(4,128)S(1)} %all_to_all.10.received), channel_id=1, source_target_pairs={{0,8},{8,0},{1,9},{9,1},{2,10},{10,2},{3,11},{11,3},{4,12},{12,4},... | collective-permute-start | bytes 491528 | tf_op jit(solution)/shard_map/ppermute | solution.py:266
  25.5 1.0 %collective-permute-done.2.from_core = f32[16,5,4,128]{3,2,1,0:T(4,128)S(1)} collective-permute-done((f32[16,5,4,128]{3,2,1,0:T(4,128)S(1)}, f32[16,5,4,128]{3,2,1,0:T(4,128)S(1)}, u32[]{:S(2)}, u32[]{:S(2)}) %collective-permute-start.2) | collective-permute-done | bytes 163872 | tf_op jit(solution)/shard_map/ppermute | solution.py:266
  26.5 5.0 %shard_map.42 = f32[8,32,128]{2,1,0:T(8,128)} custom-call(f32[16,5,4,128]{3,2,1,0:T(4,128)S(1)} %all_to_all.10.received, f32[16,5,4,128]{3,2,1,0:T(4,128)S(1)} %collective-permute-done.2.from_core), custom_call_target="tpu_custom_call" | custom-call | flops 12000000 | bytes 327680 | tf_op jit(solution)/shard_map/pallas_call | solution.py:224
  31.6 5.9 %all-to-all-start.1 = ((f32[8,32,128]{2,1,0:T(8,128)}), f32[8,32,128]{2,1,0:T(8,128)S(1)}, u32[]{:S(2)}, u32[]{:S(2)}) async-start(f32[8,32,128]{2,1,0:T(8,128)} %shard_map.42), calls=%async_computation.1 | async-start | bytes 262144 | tf_op jit(solution)/shard_map/all_to_all | solution.py:276
  37.5 1.5 %collective-permute-start.3 = (f32[128,128]{1,0:T(8,128)S(1)}, f32[128,128]{1,0:T(8,128)S(1)}, u32[]{:S(2)}, u32[]{:S(2)}) collective-permute-start(f32[128,128]{1,0:T(8,128)S(1)} %get-tuple-element.11.smooth), channel_id=1, source_target_pairs={{0,8},{8,16},{16,24},{24,32},{32,40},{40,48},{48,56},{56,64},{64,7... | collective-permute-start | bytes 196616 | tf_op jit(solution)/shard_map/ppermute | solution.py:275
  39.0 1.3 %collective-permute-done.3.smooth_before = f32[128,128]{1,0:T(8,128)S(1)} collective-permute-done((f32[128,128]{1,0:T(8,128)S(1)}, f32[128,128]{1,0:T(8,128)S(1)}, u32[]{:S(2)}, u32[]{:S(2)}) %collective-permute-start.3) | collective-permute-done | bytes 65568 | tf_op jit(solution)/shard_map/ppermute | solution.py:275
  40.4 5.3 %all-to-all-done.1.received = f32[8,32,128]{2,1,0:T(8,128)S(1)} async-done(((f32[8,32,128]{2,1,0:T(8,128)}), f32[8,32,128]{2,1,0:T(8,128)S(1)}, u32[]{:S(2)}, u32[]{:S(2)}) %all-to-all-start.1) | async-done | bytes 131104 | tf_op jit(solution)/shard_map/all_to_all | solution.py:276
  45.7 0.7 %shard_map.43 = (f32[128,128]{1,0:T(8,128)}, f32[128,128]{1,0:T(8,128)}) custom-call(f32[8,32,128]{2,1,0:T(8,128)S(1)} %all-to-all-done.1.received, f32[128,128]{1,0:T(8,128)S(1)} %get-tuple-element.11.smooth, f32[128,128]{1,0:T(8,128)S(1)} %collective-permute-done.3.smooth_before), custom_call_target="tpu_custom_call" | custom-call | flops 200000 | bytes 262144 | tf_op jit(solution)/shard_map/pallas_call | solution.py:224
  (1 shorter events, 0.0 us)
Async XLA Ops:
  0.6 0.9 %copy-start = (f32[1,4,32,128]{3,2,1,0:T(8,128)S(1)}, f32[1,4,32,128]{3,2,1,0:T(8,128)}, u32[]{:S(2)}) copy-start(f32[1,4,32,128]{3,2,1,0:T(8,128)} %param.2) | copy-start | bytes 196612
  1.6 6.8 %collective-permute-start.1 = (f32[224,128]{1,0:T(8,128)S(1)}, f32[224,128]{1,0:T(8,128)S(1)}, u32[]{:S(2)}, u32[]{:S(2)}) collective-permute-start(f32[224,128]{1,0:T(8,128)S(1)} %get-tuple-element.14.two), channel_id=1, source_target_pairs={{0,7},{1,2},{2,1},{3,4},{4,3},{5,6},{6,5},{7,0},{8,15},{9,10},{10,... | collective-permute-start | bytes 344072 | tf_op jit(solution)/shard_map/ppermute | solution.py:257
  6.2 3.6 %collective-permute-start = (f32[224,128]{1,0:T(8,128)S(1)}, f32[224,128]{1,0:T(8,128)S(1)}, u32[]{:S(2)}, u32[]{:S(2)}) collective-permute-start(f32[224,128]{1,0:T(8,128)S(1)} %get-tuple-element.15.one), channel_id=1, source_target_pairs={{0,1},{1,0},{2,3},{3,2},{4,5},{5,4},{6,7},{7,6},{8,9},{9,8},{10,11... | collective-permute-start | bytes 344072 | tf_op jit(solution)/shard_map/ppermute | solution.py:256
  22.6 3.9 %collective-permute-start.2 = (f32[16,5,4,128]{3,2,1,0:T(4,128)S(1)}, f32[16,5,4,128]{3,2,1,0:T(4,128)S(1)}, u32[]{:S(2)}, u32[]{:S(2)}) collective-permute-start(f32[16,5,4,128]{3,2,1,0:T(4,128)S(1)} %all_to_all.10.received), channel_id=1, source_target_pairs={{0,8},{8,0},{1,9},{9,1},{2,10},{10,2},{3,11},{11,3},{4,12},{12,4},... | collective-permute-start | bytes 491528 | tf_op jit(solution)/shard_map/ppermute | solution.py:266
  31.6 14.1 %all-to-all-start.1 = ((f32[8,32,128]{2,1,0:T(8,128)}), f32[8,32,128]{2,1,0:T(8,128)S(1)}, u32[]{:S(2)}, u32[]{:S(2)}) async-start(f32[8,32,128]{2,1,0:T(8,128)} %shard_map.42), calls=%async_computation.1 | async-start | bytes 262144 | tf_op jit(solution)/shard_map/all_to_all | solution.py:276
  37.5 2.9 %collective-permute-start.3 = (f32[128,128]{1,0:T(8,128)S(1)}, f32[128,128]{1,0:T(8,128)S(1)}, u32[]{:S(2)}, u32[]{:S(2)}) collective-permute-start(f32[128,128]{1,0:T(8,128)S(1)} %get-tuple-element.11.smooth), channel_id=1, source_target_pairs={{0,8},{8,16},{16,24},{24,32},{32,40},{40,48},{48,56},{56,64},{64,7... | collective-permute-start | bytes 196616 | tf_op jit(solution)/shard_map/ppermute | solution.py:275
